TPU v7x, 32 devices: a whole 2x2x4 slice. The times are simulated.
32 devices in a mesh: rep: 2 (over x), feat: 16 (over z, y, core).
Axes of the slice: x: 2, y: 2, z: 4, core: 2. Of those that a mesh axis runs over, the one named last changes fastest.
Arguments:
- tokens: bfloat16 [3, 32, 16384], P(None, ('rep', 'feat')), parts along dimension 1, may hold values from -6 to 6
- query_weight: bfloat16 [16384, 16384], P(None, 'feat'), may hold values from -0.046875 to 0.046875
- adapter_down_weight: bfloat16 [64, 16384, 128], P(None, 'feat'), may hold values from -0.046875 to 0.046875
- adapter_up_weight: bfloat16 [64, 128, 16384], P(None, None, 'feat'), may hold values from -0.5 to 0.5
- adapter_index_table: int32 [3, 32], P(None, 'rep'), parts along dimension 1, may hold values from 0 to 63
- adapter_rank_sizes: int32 [64], replicated, may hold values from 16 to 128, as said below
Outputs:
- queries: bfloat16 [3, 32, 16384], P(None, ('rep', 'feat')), parts along dimension 1
There are 2 independent parts, one for each index of `rep`. A program takes and returns all parts, laid end to end along the dimension named above; an argument that names none is the same for every part. Nothing has to cross between parts.
Inputs may be any that keep to these rules, and one draw needn't show every extreme that they name: `adapter_rank_sizes`: a multiple of 16.
All inputs are finite; a program needn't handle non-finite values.
Results may differ from a plain program's by a relative error of at most 0.0027.
Values may be sent and summed in bfloat16 or wider, within the bound.
No kernel may reach another device: no remote copies, remote signals or barrier semaphores. Data moves between devices by JAX's collectives and lax.ppermute only.
A program may use at most 192 MiB of HBM per device.

v0:
```python
import jax
import jax.numpy as jnp
from jax import lax
from jax.sharding import PartitionSpec as P


def scaled_rows(hidden, rank_rows, width):
    keep = jnp.arange(width)[None, None, :] < rank_rows[:, :, None]
    factor = 0.25 * width / rank_rows.astype(jnp.float32)
    return jnp.where(keep, hidden * factor[:, :, None], jnp.float32(0.0)).astype(jnp.bfloat16)


def apply_query_weight(
    token_block,
    adapter_indices,
    query_weight,
    adapter_down_weight,
    adapter_up_weight,
    adapter_rank_sizes,
):
    whole = lax.all_gather(token_block, "feat", axis=1, tiled=True)
    width = query_weight.shape[1]
    rank_column_width = adapter_down_weight.shape[2]
    offset = lax.axis_index("feat") * width
    column_slice = lax.dynamic_slice_in_dim(whole, offset, width, 2)
    down_matrices = adapter_down_weight[adapter_indices]
    partial_output = jnp.einsum(
        "xun,xune->xue", column_slice, down_matrices, preferred_element_type=jnp.float32
    )
    matches = adapter_indices[:, :, None] == jnp.arange(adapter_rank_sizes.shape[0])[None, None, :]
    rank_rows = jnp.sum(jnp.where(matches, adapter_rank_sizes[None, None, :], 0), axis=2)
    summed = lax.psum(partial_output, "feat")
    reduced_state = scaled_rows(summed, rank_rows, rank_column_width)
    up_matrices = adapter_up_weight[adapter_indices]
    adapter_update = jnp.einsum(
        "jma,jmap->jmp", reduced_state, up_matrices, preferred_element_type=jnp.float32
    )
    base = jnp.einsum("sbd,dc->sbc", whole, query_weight, preferred_element_type=jnp.float32)
    out_cols = (base + adapter_update).astype(jnp.bfloat16)
    return lax.all_to_all(out_cols, "feat", split_axis=1, concat_axis=2, tiled=True)


def on_device(
    tokens,
    query_weight,
    adapter_down_weight,
    adapter_up_weight,
    adapter_index_table,
    adapter_rank_sizes,
):
    pieces = []
    for step in range(tokens.shape[0]):
        pieces.append(
            apply_query_weight(
                tokens[step : step + 1],
                adapter_index_table[step : step + 1],
                query_weight,
                adapter_down_weight,
                adapter_up_weight,
                adapter_rank_sizes,
            )
        )
    return jnp.concatenate(pieces, axis=0)


def solution(mesh):
    in_specs = (
        P(None, ("rep", "feat"), None),
        P(None, "feat"),
        P(None, "feat", None),
        P(None, None, "feat"),
        P(None, "rep"),
        P(),
    )
    out_specs = P(None, ("rep", "feat"), None)
    return jax.shard_map(
        on_device, mesh=mesh, in_specs=in_specs, out_specs=out_specs, check_vma=False
    )
```

profile of v0, /device:TPU:0, one launch (start us, length us, event | category | flops | bytes accessed | tf_op | source)
XLA Modules:
  0.0 262.0 jit_solution(13404439309594310081)
XLA Ops:
  0.0 1.3 fusion.30
  1.3 26.2 %all_gather.10 = bf16[1,16,16384]{2,0,1:T(2,128)(2,1)S(1)} all-gather(bf16[1,1,16384]{2,0,1:T(2,128)(2,1)S(1)} %get-tuple-element.13), channel_id=1, replica_groups=mesh['rep'=2,'feat'=16] {'feat'}, dimensions={1}, use_global_device_ids=true | all-gather | bytes 557056 | tf_op jit(solution)/shard_map/all_gather | solution.py:21
  27.5 20.5 %all_gather.9 = bf16[1,16,16384]{2,0,1:T(2,128)(2,1)S(1)} all-gather(bf16[1,1,16384]{2,0,1:T(2,128)(2,1)S(1)} %get-tuple-element.11), channel_id=1, replica_groups=mesh['rep'=2,'feat'=16] {'feat'}, dimensions={1}, use_global_device_ids=true | all-gather | bytes 557056 | tf_op jit(solution)/shard_map/all_gather | solution.py:21
  48.0 0.1 constant_dynamic-slice_fusion
  48.1 0.8 slice_bitcast_fusion
  49.0 8.8 %gather_fusion.2 = bf16[16,1024,128]{2,1,0:T(8,128)(2,1)} fusion(bf16[64,1024,128]{2,1,0:T(8,128)(2,1)} %param.8, s32[1024]{0:T(1024)S(1)} %pad_clamp_fusion.1), kind=kCustom, calls=%fused_computation.2 | custom fusion | bytes 8388672 | tf_op jit(solution)/shard_map/gather | solution.py:26
  57.8 8.8 %gather_fusion = bf16[16,1024,128]{2,1,0:T(8,128)(2,1)} fusion(bf16[64,1024,128]{2,1,0:T(8,128)(2,1)} %param.8, s32[1024]{0:T(1024)S(1)} %pad_clamp_fusion.2), kind=kCustom, calls=%fused_computation | custom fusion | bytes 8388672 | tf_op jit(solution)/shard_map/gather | solution.py:26
  66.6 24.3 %all_gather.11 = bf16[1,16,16384]{2,0,1:T(2,128)(2,1)S(1)} all-gather(bf16[1,1,16384]{2,0,1:T(2,128)(2,1)S(1)} %get-tuple-element.12), channel_id=1, replica_groups=mesh['rep'=2,'feat'=16] {'feat'}, dimensions={1}, use_global_device_ids=true | all-gather | bytes 557056 | tf_op jit(solution)/shard_map/all_gather | solution.py:21
  91.0 0.1 constant_dynamic-slice_fusion.2
  91.1 8.8 %gather_fusion.4 = bf16[16,1024,128]{2,1,0:T(8,128)(2,1)} fusion(bf16[64,1024,128]{2,1,0:T(8,128)(2,1)} %param.8, s32[1024]{0:T(1024)S(1)} %pad_clamp_fusion), kind=kCustom, calls=%fused_computation.4 | custom fusion | bytes 8388672 | tf_op jit(solution)/shard_map/gather | solution.py:26
  99.9 8.5 %gather_fusion.3 = bf16[16,128,1024]{2,1,0:T(8,128)(2,1)} fusion(bf16[64,128,1024]{2,1,0:T(8,128)(2,1)} %param.9, s32[1024]{0:T(1024)S(1)} %pad_clamp_fusion.1), kind=kCustom, calls=%fused_computation.3 | custom fusion | bytes 8388672 | tf_op jit(solution)/shard_map/gather | solution.py:34
  108.4 0.0 copy-start.1
  108.4 0.0 copy-start.2
  108.4 3.0 %fusion.14 = f32[16,1,128]{2,1,0:T(1,128)S(1)} fusion(bf16[16,1024,128]{2,1,0:T(8,128)(2,1)} %gather_fusion.2, bf16[16,1024,1]{1,0,2:T(8,128)(2,1)S(1)} %bitcast.93), kind=kOutput, calls=%fused_computation.24 | convolution fusion | flops 4194304 | bytes 4235264 | tf_op jit(solution)/shard_map/xun,xune->xue/dot_general | solution.py:27
  111.4 0.5 copy-done.1
  111.8 0.0 copy-start.3
  111.8 0.6 fusion.16
  112.5 0.6 copy-done.2
  113.1 0.6 fusion.12
  113.8 0.0 copy-done.3
  113.8 0.2 select_reduce_fusion.2
  114.0 57.8 %all-reduce = (f32[1,16,128]{2,1,0:T(8,128)S(1)}, f32[1,16,128]{2,1,0:T(8,128)S(1)}, f32[1,16,128]{2,1,0:T(8,128)S(1)}) all-reduce(f32[1,16,128]{2,1,0:T(8,128)S(1)} %bitcast.104, f32[1,16,128]{2,1,0:T(8,128)S(1)} %bitcast.102, f32[1,16,128]{2,1,0:T(8,128)S(1)} %bitcast.103), channel_id=1, replica_groups=mesh['rep'=2,'feat'=16] {'feat'}, use_global_device_ids=true, to_apply=%region_5.6 | all-reduce | flops 6144 | bytes 49152 | tf_op jit(solution)/shard_map/psum | solution.py:32
  171.8 0.1 fusion.25
  171.9 2.8 %fusion.20 = f32[16,1,1024]{2,1,0:T(1,128)S(1)} fusion(bf16[16,128,1024]{2,1,0:T(8,128)(2,1)} %gather_fusion.3, bf16[16,128,1]{1,0,2:T(8,128)(2,1)S(1)} %fusion.25), kind=kOutput, calls=%fused_computation.33 | convolution fusion | flops 4194304 | bytes 4263936 | tf_op jit(solution)/shard_map/jma,jmap->jmp/dot_general | solution.py:35
  174.8 12.8 %fusion.4 = bf16[1,16,1024]{2,1,0:T(8,128)(2,1)S(1)} fusion(bf16[16384,1024]{1,0:T(8,128)(2,1)} %param.7, bf16[1,16,16384]{2,0,1:T(2,128)(2,1)S(1)} %all_gather.10, f32[16,1,1024]{2,1,0:T(1,128)S(1)} %fusion.20), kind=kOutput, calls=%fused_computation.13 | convolution fusion | flops 536903680 | bytes 34177024 | tf_op jit(solution)/shard_map/sbd,dc->sbc/dot_general | solution.py:38
  187.6 0.1 copy.89
  187.7 0.5 broadcast.297
  188.2 0.7 reduce.4
  188.9 0.6 reshape.481
  189.5 3.7 %all-to-all-start.1 = ((bf16[16,2,512]{2,1,0:T(2,128)(2,1)}), bf16[16,2,512]{2,1,0:T(2,128)(2,1)S(1)}, u32[]{:S(2)}, u32[]{:S(2)}) async-start(bf16[16,2,512]{2,1,0:T(2,128)(2,1)} %reshape.481), calls=%async_computation.1 | async-start | bytes 65536 | tf_op jit(solution)/shard_map/all_to_all | solution.py:40
  193.2 8.5 %gather_fusion.5 = bf16[16,128,1024]{2,1,0:T(8,128)(2,1)} fusion(bf16[64,128,1024]{2,1,0:T(8,128)(2,1)} %param.9, s32[1024]{0:T(1024)S(1)} %pad_clamp_fusion), kind=kCustom, calls=%fused_computation.5 | custom fusion | bytes 8388672 | tf_op jit(solution)/shard_map/gather | solution.py:34
  201.7 8.6 %gather_fusion.1 = bf16[16,128,1024]{2,1,0:T(8,128)(2,1)} fusion(bf16[64,128,1024]{2,1,0:T(8,128)(2,1)} %param.9, s32[1024]{0:T(1024)S(1)} %pad_clamp_fusion.2), kind=kCustom, calls=%fused_computation.1 | custom fusion | bytes 8388672 | tf_op jit(solution)/shard_map/gather | solution.py:34
  210.3 0.1 fusion.26
  210.3 2.8 %fusion.18 = f32[16,1,1024]{2,1,0:T(1,128)S(1)} fusion(bf16[16,128,1024]{2,1,0:T(8,128)(2,1)} %gather_fusion.5, bf16[16,128,1]{1,0,2:T(8,128)(2,1)S(1)} %fusion.26), kind=kOutput, calls=%fused_computation.31 | convolution fusion | flops 4194304 | bytes 4263936 | tf_op jit(solution)/shard_map/jma,jmap->jmp/dot_general | solution.py:35
  213.2 0.0 copy-start
  213.2 13.0 %fusion.3 = bf16[1,16,1024]{2,1,0:T(8,128)(2,1)S(1)} fusion(bf16[16384,1024]{1,0:T(8,128)(2,1)} %param.7, bf16[1,16,16384]{2,0,1:T(2,128)(2,1)S(1)} %all_gather.11, f32[16,1,1024]{2,1,0:T(1,128)S(1)} %fusion.18), kind=kOutput, calls=%fused_computation.12 | convolution fusion | flops 536903680 | bytes 34177024 | tf_op jit(solution)/shard_map/sbd,dc->sbc/dot_general | solution.py:38
  226.2 0.1 fusion.24
  226.3 0.0 copy-done
  226.3 0.7 fusion.22
  226.9 0.1 copy.88
  227.0 0.7 reduce.3
  227.7 0.6 reshape.479
  228.4 0.0 all-to-all-done.1
  228.4 5.8 %all-to-all-start.2 = ((bf16[16,2,512]{2,1,0:T(2,128)(2,1)}), bf16[16,2,512]{2,1,0:T(2,128)(2,1)S(1)}, u32[]{:S(2)}, u32[]{:S(2)}) async-start(bf16[16,2,512]{2,1,0:T(2,128)(2,1)} %reshape.479), calls=%async_computation.2 | async-start | bytes 65536 | tf_op jit(solution)/shard_map/all_to_all | solution.py:40
  234.2 12.8 %fusion.5 = bf16[1,16,1024]{2,1,0:T(8,128)(2,1)S(1)} fusion(bf16[16384,1024]{1,0:T(8,128)(2,1)} %param.7, bf16[1,16,16384]{2,0,1:T(2,128)(2,1)S(1)} %all_gather.9, f32[16,1,1024]{2,1,0:T(1,128)S(1)} %fusion.22), kind=kOutput, calls=%fused_computation.14 | convolution fusion | flops 536903680 | bytes 34177024 | tf_op jit(solution)/shard_map/sbd,dc->sbc/dot_general | solution.py:38
  247.0 0.1 copy.90
  247.1 0.7 reduce.5
  247.8 0.6 reshape.483
  248.4 0.0 all-to-all-done.2
  248.4 6.0 %all-to-all-start = ((bf16[16,2,512]{2,1,0:T(2,128)(2,1)}), bf16[16,2,512]{2,1,0:T(2,128)(2,1)S(1)}, u32[]{:S(2)}, u32[]{:S(2)}) async-start(bf16[16,2,512]{2,1,0:T(2,128)(2,1)} %reshape.483), calls=%async_computation | async-start | bytes 65536 | tf_op jit(solution)/shard_map/all_to_all | solution.py:40
  254.5 6.6 %all-to-all-done = bf16[16,2,512]{2,1,0:T(2,128)(2,1)S(1)} async-done(((bf16[16,2,512]{2,1,0:T(2,128)(2,1)}), bf16[16,2,512]{2,1,0:T(2,128)(2,1)S(1)}, u32[]{:S(2)}, u32[]{:S(2)}) %all-to-all-start) | async-done | bytes 32800 | tf_op jit(solution)/shard_map/all_to_all | solution.py:40
  261.1 0.9 pad_maximum_fusion
  (11 shorter events, 0.2 us)
Async XLA Ops:
  108.4 3.4 %copy-start.1 = (bf16[16,1024,128]{2,1,0:T(8,128)(2,1)S(1)}, bf16[16,1024,128]{2,1,0:T(8,128)(2,1)}, u32[]{:S(2)}) copy-start(bf16[16,1024,128]{2,1,0:T(8,128)(2,1)} %gather_fusion) | copy-start | bytes 12582916
  108.4 4.7 %copy-start.2 = (bf16[16,1024,128]{2,1,0:T(8,128)(2,1)S(1)}, bf16[16,1024,128]{2,1,0:T(8,128)(2,1)}, u32[]{:S(2)}) copy-start(bf16[16,1024,128]{2,1,0:T(8,128)(2,1)} %gather_fusion.4) | copy-start | bytes 12582916
  111.8 1.9 copy-start.3
  189.5 38.8 %all-to-all-start.1 = ((bf16[16,2,512]{2,1,0:T(2,128)(2,1)}), bf16[16,2,512]{2,1,0:T(2,128)(2,1)S(1)}, u32[]{:S(2)}, u32[]{:S(2)}) async-start(bf16[16,2,512]{2,1,0:T(2,128)(2,1)} %reshape.481), calls=%async_computation.1 | async-start | bytes 65536 | tf_op jit(solution)/shard_map/all_to_all | solution.py:40
  213.2 13.1 %copy-start = (bf16[16,128,1024]{2,1,0:T(8,128)(2,1)S(1)}, bf16[16,128,1024]{2,1,0:T(8,128)(2,1)}, u32[]{:S(2)}) copy-start(bf16[16,128,1024]{2,1,0:T(8,128)(2,1)} %gather_fusion.1) | copy-start | bytes 12582916
  228.4 20.1 %all-to-all-start.2 = ((bf16[16,2,512]{2,1,0:T(2,128)(2,1)}), bf16[16,2,512]{2,1,0:T(2,128)(2,1)S(1)}, u32[]{:S(2)}, u32[]{:S(2)}) async-start(bf16[16,2,512]{2,1,0:T(2,128)(2,1)} %reshape.479), calls=%async_computation.2 | async-start | bytes 65536 | tf_op jit(solution)/shard_map/all_to_all | solution.py:40
  248.4 12.6 %all-to-all-start = ((bf16[16,2,512]{2,1,0:T(2,128)(2,1)}), bf16[16,2,512]{2,1,0:T(2,128)(2,1)S(1)}, u32[]{:S(2)}, u32[]{:S(2)}) async-start(bf16[16,2,512]{2,1,0:T(2,128)(2,1)} %reshape.483), calls=%async_computation | async-start | bytes 65536 | tf_op jit(solution)/shard_map/all_to_all | solution.py:40
where the time goes:
time: 263 us; the launch traced here: 262 us
  blocking collectives  129 us (49%)
  local copies, waits for them, and re-layouts  57.3 us (22%)
  matrix products  49.3 us (19%)
  starting transfers between devices  15.5 us (6%)
  waiting for transfers between devices  6.57 us (2%)
  other arithmetic  4.41 us (2%)
    all_gather x3, blocking collectives, apply_query_weight(): whole = lax.all_gather(token_block, 'feat', axis=1, tiled=True)  71 us
    psum x1, blocking collectives, apply_query_weight(): summed = lax.psum(partial_output, 'feat')  57.8 us
    dot_general x3, matrix products, apply_query_weight(): jnp.einsum('sbd,dc->sbc', whole, query_weight, preferred_element_type=jnp...  38.7 us
    gather x3, local copies, waits for them, and re-layouts, apply_query_weight(): down_matrices = adapter_down_weight[adapter_indices]  26.4 us
    gather x3, local copies, waits for them, and re-layouts, apply_query_weight(): up_matrices = adapter_up_weight[adapter_indices]  25.6 us
    all_to_all x3, starting transfers between devices, apply_query_weight(): lax.all_to_all(out_cols, 'feat', split_axis=1, concat_axis=2, tiled=True)  15.5 us
    all_to_all x3, waiting for transfers between devices, apply_query_weight(): lax.all_to_all(out_cols, 'feat', split_axis=1, concat_axis=2, tiled=True)  6.57 us
    dot_general x3, matrix products, apply_query_weight(): jnp.einsum('jma,jmap->jmp', reduced_state, up_matrices, preferred_element...  6.33 us
  transfers between devices with their start and end apart: 3, of which 1 were waited for; matrix products, arithmetic and copies ran while one was open for 19% of the time, Pallas kernels for 0%

commit v1 on v0

v1 whole, which is shorter than its diff:
```python
import functools

import jax
import jax.numpy as jnp
from jax import lax
from jax.experimental import pallas as pl
from jax.experimental.pallas import tpu as pltpu
from jax.sharding import PartitionSpec as P

VMEM, SMEM, ANY = pltpu.VMEM, pltpu.SMEM, pl.ANY
GROUP = 4
LANES = 128


def start_slices(table_ref, weight_ref, held, sems, seen, listed):
    steps, owners = table_ref.shape
    width = 128

    def clear(i, carry):
        seen[i] = jnp.int32(0)
        return carry

    def unlist(i, carry):
        listed[i] = jnp.int32(-1)
        return carry

    lax.fori_loop(0, weight_ref.shape[0], clear, 0)
    lax.fori_loop(0, held.shape[0], unlist, 0)

    def one(b, count):
        adapter = table_ref[b % steps, b // steps]
        new = seen[adapter] == 0

        @pl.when(new)
        def _():
            seen[adapter] = jnp.int32(1)
            listed[count] = adapter
            pltpu.make_async_copy(weight_ref.at[adapter], held.at[count], sems.at[count]).start()

        return count + new.astype(jnp.int32)

    return lax.fori_loop(0, steps * owners, one, jnp.int32(0))


def wait_group(group, count, listed, weight_ref, held, sems):
    for i in range(GROUP):
        slot = group * GROUP + i

        @pl.when(slot < count)
        def _():
            pltpu.make_async_copy(weight_ref.at[0], held.at[slot], sems.at[slot]).wait()


def down_kernel(order, me_ref, table_ref, adapter_rows_ref, *refs):
    parts = refs[: len(order)]
    weight_ref, lhs_ref, partial_ref, wide, held, seen, listed, sems = refs[len(order) :]
    count = start_slices(table_ref, weight_ref, held, sems, seen, listed)
    chunks, rows, depth = lhs_ref.shape
    block = rows // chunks * chunks
    me = me_ref[0]
    for part, owners in zip(parts, order, strict=True):
        for place, distance in enumerate(owners):
            owner = jnp.bitwise_xor(me, distance)
            at = pl.ds(pl.multiple_of(owner * block, block), block)
            for tile in range(depth // LANES):
                piece = part[place * block : (place + 1) * block, tile * LANES : (tile + 1) * LANES]
                wide[tile, at, :] = piece.astype(jnp.float32)
    for chunk in range(chunks):
        for tile in range(depth // LANES):
            piece = wide[tile, pl.ds(chunk, rows, stride=chunks), :]
            lhs_ref[chunk, :, tile * LANES : (tile + 1) * LANES] = piece.astype(jnp.bfloat16)
    mine = lhs_ref[me]
    adapter_rows = adapter_rows_ref[...]

    def one(group, total):
        wait_group(group, count, listed, weight_ref, held, sems)
        for pair in range(0, GROUP, 2):
            slot = group * GROUP + pair
            both = jnp.concatenate([held[slot], held[slot + 1]], axis=1)
            product = jnp.dot(mine, both, preferred_element_type=jnp.float32)
            half = product.shape[1] // 2
            total = jnp.where(adapter_rows == listed[slot], product[:, :half], total)
            total = jnp.where(adapter_rows == listed[slot + 1], product[:, half:], total)
        return total

    zeros = jnp.zeros(partial_ref.shape, jnp.float32)
    partial_ref[...] = lax.fori_loop(0, (count + GROUP - 1) // GROUP, one, zeros)


def base_kernel(lhs_ref, weight_ref, out_ref, held, sems):
    chunks, rows, depth = lhs_ref.shape
    copies = []
    for chunk in range(chunks):
        copy = pltpu.make_async_copy(weight_ref.at[pl.ds(chunk * depth, depth)], held.at[chunk], sems.at[chunk])
        copy.start()
        copies.append(copy)
    total = jnp.zeros(out_ref.shape, jnp.float32)
    for chunk in range(chunks):
        copies[chunk].wait()
        total += jnp.dot(lhs_ref[chunk], held[chunk], preferred_element_type=jnp.float32)
    out_ref[...] = total


def up_kernel(table_ref, adapter_rows_ref, rank_rows_ref, hidden_ref, base_ref, weight_ref, out_ref, held, seen, listed, sems):
    count = start_slices(table_ref, weight_ref, held, sems, seen, listed)
    width = hidden_ref.shape[1]
    rank_rows = rank_rows_ref[...]
    keep = lax.broadcasted_iota(jnp.int32, rank_rows.shape, 1) < rank_rows
    factor = 0.25 * width / rank_rows.astype(jnp.float32)
    lowrank = jnp.where(keep, hidden_ref[...] * factor, jnp.float32(0.0))
    adapter_rows = adapter_rows_ref[...]

    def one(group, total):
        wait_group(group, count, listed, weight_ref, held, sems)
        for i in range(GROUP):
            slot = group * GROUP + i
            own = jnp.where(adapter_rows == listed[slot], lowrank, jnp.float32(0.0)).astype(jnp.bfloat16)
            matrix = held[slot]
            product = jnp.dot(own, matrix, preferred_element_type=jnp.float32)
            hit = adapter_rows[:, :1] == listed[slot]
            total = total + jnp.where(hit, product, jnp.float32(0.0))
        return total

    total = lax.fori_loop(0, (count + GROUP - 1) // GROUP, one, base_ref[...])
    total = total.astype(jnp.bfloat16)
    steps = out_ref.shape[1]
    for owner in range(out_ref.shape[0]):
        out_ref[owner] = total[owner * steps : (owner + 1) * steps, :]


def exchange(value, distance, ranks):
    return lax.ppermute(value, "feat", [(i, i ^ distance) for i in range(ranks)])


def fast(tokens, query_weight, adapter_down_weight, adapter_up_weight, adapter_index_table, adapter_rank_sizes):
    steps, _, features = tokens.shape
    ranks = adapter_index_table.shape[1]
    columns = query_weight.shape[1]
    adapters, depth, width = adapter_down_weight.shape
    rows = steps * ranks
    swap = functools.partial(exchange, ranks=ranks)
    spec = lambda space: pl.BlockSpec(memory_space=space)

    adapter_rows = jnp.broadcast_to(adapter_index_table.T.reshape(rows, 1), (rows, width))
    matches = adapter_rows[:, :1] == jnp.arange(adapters)[None, :]
    rank_rows = jnp.sum(jnp.where(matches, adapter_rank_sizes[None, :], 0), axis=1, keepdims=True)
    rank_rows = jnp.broadcast_to(rank_rows, (rows, width))
    me = lax.axis_index("feat").astype(jnp.int32).reshape(1)

    own = tokens.reshape(steps * ranks, features // ranks)
    near = jnp.concatenate([own, swap(own, 4), swap(own, 8), swap(own, 12)], axis=0)
    far = swap(near, 2)
    parts = (near, far, swap(near, 1), swap(far, 1))
    order = tuple(tuple(first ^ z for z in (0, 4, 8, 12)) for first in (0, 2, 1, 3))

    lhs, partial = pl.pallas_call(
        functools.partial(down_kernel, order),
        out_shape=(
            jax.ShapeDtypeStruct((ranks, rows, features // ranks), jnp.bfloat16),
            jax.ShapeDtypeStruct((rows, width), jnp.float32),
        ),
        in_specs=[spec(SMEM), spec(SMEM), spec(VMEM)] + [spec(VMEM)] * len(parts) + [spec(ANY)],
        out_specs=(spec(VMEM), spec(VMEM)),
        scratch_shapes=[
            VMEM((depth // LANES, rows * ranks, LANES), jnp.float32),
            VMEM((rows, depth, width), jnp.bfloat16),
            SMEM((adapters,), jnp.int32),
            SMEM((rows,), jnp.int32),
            pltpu.SemaphoreType.DMA((rows,)),
        ],
        compiler_params=pltpu.CompilerParams(vmem_limit_bytes=48 << 20),
        cost_estimate=pl.CostEstimate(flops=2 * rows * depth * width, bytes_accessed=12 << 20, transcendentals=0),
    )(me, adapter_index_table, adapter_rows, *parts, adapter_down_weight)

    base = pl.pallas_call(
        base_kernel,
        out_shape=jax.ShapeDtypeStruct((rows, columns), jnp.float32),
        in_specs=[spec(VMEM), spec(ANY)],
        out_specs=spec(VMEM),
        scratch_shapes=[
            VMEM((ranks, features // ranks, columns), jnp.bfloat16),
            pltpu.SemaphoreType.DMA((ranks,)),
        ],
        compiler_params=pltpu.CompilerParams(vmem_limit_bytes=48 << 20),
        cost_estimate=pl.CostEstimate(flops=2 * rows * features * columns, bytes_accessed=34 << 20, transcendentals=0),
    )(lhs, query_weight)

    hidden = partial + swap(partial, 1)
    hidden = hidden + swap(hidden, 2) + swap(hidden, 4) + swap(hidden, 6)
    hidden = hidden + swap(hidden, 8)

    out = pl.pallas_call(
        up_kernel,
        out_shape=jax.ShapeDtypeStruct((ranks, steps, columns), jnp.bfloat16),
        in_specs=[spec(SMEM)] + [spec(VMEM)] * 4 + [spec(ANY)],
        out_specs=spec(VMEM),
        scratch_shapes=[
            VMEM((rows, width, columns), jnp.bfloat16),
            SMEM((adapters,), jnp.int32),
            SMEM((rows,), jnp.int32),
            pltpu.SemaphoreType.DMA((rows,)),
        ],
        compiler_params=pltpu.CompilerParams(vmem_limit_bytes=48 << 20),
        cost_estimate=pl.CostEstimate(flops=2 * rows * width * columns, bytes_accessed=12 << 20, transcendentals=0),
    )(adapter_index_table, adapter_rows, rank_rows, hidden, base, adapter_up_weight)

    gathered = lax.all_to_all(out, "feat", split_axis=0, concat_axis=0, tiled=True)
    return gathered.transpose(1, 0, 2).reshape(steps, 1, features)


def plain(tokens, query_weight, adapter_down_weight, adapter_up_weight, adapter_index_table, adapter_rank_sizes):
    width = query_weight.shape[1]
    rank_width = adapter_down_weight.shape[2]
    depth = adapter_down_weight.shape[1]
    whole = lax.all_gather(tokens, "feat", axis=1, tiled=True)
    piece = lax.dynamic_slice_in_dim(whole, lax.axis_index("feat") * depth, depth, 2)
    matrices = adapter_down_weight[adapter_index_table]
    partial = jnp.einsum("xun,xune->xue", piece, matrices, preferred_element_type=jnp.float32)
    hidden = lax.psum(partial, "feat")
    rank_rows = adapter_rank_sizes[adapter_index_table]
    keep = jnp.arange(rank_width)[None, None, :] < rank_rows[:, :, None]
    factor = 0.25 * rank_width / rank_rows.astype(jnp.float32)
    lowrank = jnp.where(keep, hidden * factor[:, :, None], jnp.float32(0.0)).astype(jnp.bfloat16)
    matrices = adapter_up_weight[adapter_index_table]
    update = jnp.einsum("jma,jmap->jmp", lowrank, matrices, preferred_element_type=jnp.float32)
    base = jnp.einsum("sbd,dc->sbc", whole, query_weight, preferred_element_type=jnp.float32)
    out = (base + update).astype(jnp.bfloat16)
    return lax.all_to_all(out, "feat", split_axis=1, concat_axis=2, tiled=True)


def on_device(tokens, query_weight, *rest):
    ranks = rest[2].shape[1]
    fits = ranks == 16 and query_weight.shape[1] % 256 == 0
    return (fast if fits else plain)(tokens, query_weight, *rest)


def solution(mesh):
    in_specs = (
        P(None, ("rep", "feat"), None),
        P(None, "feat"),
        P(None, "feat", None),
        P(None, None, "feat"),
        P(None, "rep"),
        P(),
    )
    out_specs = P(None, ("rep", "feat"), None)
    return jax.shard_map(
        on_device, mesh=mesh, in_specs=in_specs, out_specs=out_specs, check_vma=False
    )
```

time: 263 us -> 73.6 us (0.28)
  blocking collectives: 129 us -> 11.1 us
  local copies, waits for them, and re-layouts: 57.3 us -> 3.42 us
  matrix products: 49.3 us -> 0 us
  Pallas kernels: 0 us -> 24.4 us
  waiting for transfers between devices: 6.57 us -> 21.7 us
  other arithmetic: 4.41 us -> 0.19 us
  starting transfers between devices: 15.5 us -> 12.4 us
    all_gather x3 -> x0, blocking collectives: 71 us -> none  [apply_query_weight(): whole = lax.all_gather(token_block, 'feat', axis=1, tiled=True)]
    psum x1 -> x0, blocking collectives: 57.8 us -> none  [apply_query_weight(): summed = lax.psum(partial_output, 'feat')]
    gather x6 -> x0, local copies, waits for them, and re-layouts: 52 us -> none  [the longest x3 26.4 us: apply_query_weight(): down_matrices = adapter_down_weight[adapter_indices]]
    dot_general x9 -> x0, matrix products: 49.3 us -> none  [the longest x3 38.7 us: apply_query_weight(): jnp.einsum('sbd,dc->sbc', whole, query_weight, preferred_element_type=jnp...]
    pallas_call x0 -> x3, Pallas kernels: none -> 24.4 us  [the longest x1 11.2 us: fast(): pl.pallas_call(base_kernel, out_shape=jax.ShapeDtypeStruct((rows, columns...]
    ppermute x0 -> x11, waiting for transfers between devices: none -> 21.7 us  [exchange(): lax.ppermute(value, 'feat', [(i, i ^ distance) for i in range(ranks)])]
    all_to_all x3 -> x0, starting transfers between devices: 15.5 us -> none  [apply_query_weight(): lax.all_to_all(out_cols, 'feat', split_axis=1, concat_axis=2, tiled=True)]
    ppermute x0 -> x11, starting transfers between devices: none -> 12.4 us  [exchange(): lax.ppermute(value, 'feat', [(i, i ^ distance) for i in range(ranks)])]
  transfers between devices with their start and end apart: 3 -> 11, of which waited for: 1 -> 7; matrix products, arithmetic and copies ran while one was open for 19% -> 1% of each run, Pallas kernels for 0% -> 15%
where the time goes in v1:
time: 73.6 us; the launch traced here: 73.4 us
  Pallas kernels  24.4 us (33%)
  waiting for transfers between devices  21.7 us (29%)
  starting transfers between devices  12.4 us (17%)
  blocking collectives  11.1 us (15%)
  local copies, waits for them, and re-layouts  3.42 us (5%)
    ppermute x11, waiting for transfers between devices, exchange(): lax.ppermute(value, 'feat', [(i, i ^ distance) for i in range(ranks)])  21.7 us
    ppermute x11, starting transfers between devices, exchange(): lax.ppermute(value, 'feat', [(i, i ^ distance) for i in range(ranks)])  12.4 us
    pallas_call x1, Pallas kernels, fast(): pl.pallas_call(base_kernel, out_shape=jax.ShapeDtypeStruct((rows, columns...  11.2 us
    all_to_all x1, blocking collectives, fast(): lax.all_to_all(out, 'feat', split_axis=0, concat_axis=0, tiled=True)  11.1 us
    pallas_call x1, Pallas kernels, fast(): pl.pallas_call(functools.partial(down_kernel, order), out_shape=(jax.Shap...  7.27 us
    pallas_call x1, Pallas kernels, fast(): pl.pallas_call(up_kernel, out_shape=jax.ShapeDtypeStruct((ranks, steps, c...  5.91 us
  transfers between devices with their start and end apart: 11, of which 7 were waited for; matrix products, arithmetic and copies ran while one was open for 1% of the time, Pallas kernels for 15%

profile of v1, /device:TPU:0, one launch (start us, length us, event | category | flops | bytes accessed | tf_op | source)
XLA Modules:
  0.0 73.4 jit_solution(5092372901515842236)
XLA Ops:
  0.0 0.0 copy-start.2
  0.0 1.1 %reshape.16 = bf16[48,1024]{1,0:T(8,128)(2,1)S(1)} reshape(bf16[3,1,16384]{2,0,1:T(4,128)(2,1)} %param.6) | data formatting | bytes 196608 | tf_op jit(solution)/shard_map/reshape | solution.py:150
  1.1 3.1 %collective-permute-start = (bf16[48,1024]{1,0:T(8,128)(2,1)S(1)}, bf16[48,1024]{1,0:T(8,128)(2,1)S(1)}, u32[]{:S(2)}, u32[]{:S(2)}) collective-permute-start(bf16[48,1024]{1,0:T(8,128)(2,1)S(1)} %reshape.16), channel_id=1, source_target_pairs={{0,4},{1,5},{2,6},{3,7},{4,0},{5,1},{6,2},{7,3},{8,12},{9,13},{10,... | collective-permute-start | bytes 294920 | tf_op jit(solution)/shard_map/ppermute | solution.py:132
  4.2 2.6 %collective-permute-start.1 = (bf16[48,1024]{1,0:T(8,128)(2,1)S(1)}, bf16[48,1024]{1,0:T(8,128)(2,1)S(1)}, u32[]{:S(2)}, u32[]{:S(2)}) collective-permute-start(bf16[48,1024]{1,0:T(8,128)(2,1)S(1)} %reshape.16), channel_id=1, source_target_pairs={{0,8},{1,9},{2,10},{3,11},{4,12},{5,13},{6,14},{7,15},{8,0},{9,1},... | collective-permute-start | bytes 294920 | tf_op jit(solution)/shard_map/ppermute | solution.py:132
  6.7 0.0 collective-permute-start.2
  6.8 0.2 collective-permute-done
  7.0 7.6 %collective-permute-done.1 = bf16[48,1024]{1,0:T(8,128)(2,1)S(1)} collective-permute-done((bf16[48,1024]{1,0:T(8,128)(2,1)S(1)}, bf16[48,1024]{1,0:T(8,128)(2,1)S(1)}, u32[]{:S(2)}, u32[]{:S(2)}) %collective-permute-start.1) | collective-permute-done | bytes 98336 | tf_op jit(solution)/shard_map/ppermute | solution.py:132
  14.6 0.0 collective-permute-done.2
  14.6 1.6 %collective-permute-start.3 = (bf16[192,1024]{1,0:T(8,128)(2,1)S(1)}, bf16[192,1024]{1,0:T(8,128)(2,1)S(1)}, u32[]{:S(2)}, u32[]{:S(2)}) collective-permute-start(bf16[192,1024]{1,0:T(8,128)(2,1)S(1)} %constant_dynamic-update-slice_fusion.refs_0_), channel_id=1, source_target_pairs={{0,2},{1,3},{2,0},{3,1},{4,6},{5,7},{6,4},{7,5},{8,10},{9,11},{10,... | collective-permute-start | bytes 1179656 | tf_op jit(solution)/shard_map/ppermute | solution.py:132
  16.2 0.0 collective-permute-start.4
  16.2 7.4 %collective-permute-done.3.refs_1_ = bf16[192,1024]{1,0:T(8,128)(2,1)S(1)} collective-permute-done((bf16[192,1024]{1,0:T(8,128)(2,1)S(1)}, bf16[192,1024]{1,0:T(8,128)(2,1)S(1)}, u32[]{:S(2)}, u32[]{:S(2)}) %collective-permute-start.3) | collective-permute-done | bytes 393248 | tf_op jit(solution)/shard_map/ppermute | solution.py:132
  23.6 0.0 collective-permute-start.5
  23.6 0.8 %copy.9 = s32[16,3]{1,0:T(8,128)S(1)} copy(s32[16,3]{0,1:T(4,128)} %bitcast.7) | data formatting | bytes 384 | tf_op jit(solution)/shard_map/transpose | solution.py:144
  24.4 0.1 broadcast_in_dim.27
  24.5 0.0 collective-permute-done.4.refs_2_
  24.5 0.9 %collective-permute-done.5.refs_3_ = bf16[192,1024]{1,0:T(8,128)(2,1)S(1)} collective-permute-done((bf16[192,1024]{1,0:T(8,128)(2,1)S(1)}, bf16[192,1024]{1,0:T(8,128)(2,1)S(1)}, u32[]{:S(2)}, u32[]{:S(2)}) %collective-permute-start.5) | collective-permute-done | bytes 393248 | tf_op jit(solution)/shard_map/ppermute | solution.py:132
  25.4 0.1 broadcast_in_dim.28.adapter_rows_ref
  25.4 0.0 copy-start
  25.4 0.7 copy-done
  26.1 7.3 %shard_map.64 = (bf16[16,48,1024]{2,1,0:T(8,128)(2,1)S(1)}, f32[48,128]{1,0:T(8,128)S(1)}) custom-call(s32[1]{0:T(128)} %bitcast.1.me_ref, s32[3,16]{1,0:T(4,128)S(1)} %copy-done, s32[48,128]{1,0:T(8,128)S(1)} %broadcast_in_dim.28.adapter_rows_ref, bf16[192,1024]{1,0:T(8,128)(2,1)S(1)} %constant_dynamic-update-slice_fusion.refs_0_, ...), custom_call_target="tpu_custom_call" | custom-call | flops 12582912 | bytes 12582912 | tf_op jit(solution)/shard_map/pallas_call | solution.py:156
  33.4 0.2 collective-permute-start.6
  33.6 1.1 %collective-permute-done.6 = f32[48,128]{1,0:T(8,128)S(1)} collective-permute-done((f32[48,128]{1,0:T(8,128)S(1)}, f32[48,128]{1,0:T(8,128)S(1)}, u32[]{:S(2)}, u32[]{:S(2)}) %collective-permute-start.6) | collective-permute-done | bytes 24608 | tf_op jit(solution)/shard_map/ppermute | solution.py:132
  34.7 1.5 %collective-permute-start.7 = (f32[48,128]{1,0:T(8,128)S(1)}, f32[48,128]{1,0:T(8,128)S(1)}, u32[]{:S(2)}, u32[]{:S(2)}) collective-permute-start(f32[48,128]{1,0:T(8,128)S(1)} %add.15), channel_id=1, source_target_pairs={{0,2},{1,3},{2,0},{3,1},{4,6},{5,7},{6,4},{7,5},{8,10},{9,11},{10,... | collective-permute-start | bytes 73736 | tf_op jit(solution)/shard_map/ppermute | solution.py:132
  36.2 2.3 %collective-permute-start.8 = (f32[48,128]{1,0:T(8,128)S(1)}, f32[48,128]{1,0:T(8,128)S(1)}, u32[]{:S(2)}, u32[]{:S(2)}) collective-permute-start(f32[48,128]{1,0:T(8,128)S(1)} %add.15), channel_id=1, source_target_pairs={{0,4},{1,5},{2,6},{3,7},{4,0},{5,1},{6,2},{7,3},{8,12},{9,13},{10,... | collective-permute-start | bytes 73736 | tf_op jit(solution)/shard_map/ppermute | solution.py:132
  38.5 0.0 collective-permute-start.9
  38.5 0.0 copy-done.2
  38.5 0.2 select_reduce_fusion
  38.7 0.0 collective-permute-done.7
  38.7 1.6 %collective-permute-done.8 = f32[48,128]{1,0:T(8,128)S(1)} collective-permute-done((f32[48,128]{1,0:T(8,128)S(1)}, f32[48,128]{1,0:T(8,128)S(1)}, u32[]{:S(2)}, u32[]{:S(2)}) %collective-permute-start.8) | collective-permute-done | bytes 24608 | tf_op jit(solution)/shard_map/ppermute | solution.py:132
  40.3 2.9 %collective-permute-done.9 = f32[48,128]{1,0:T(8,128)S(1)} collective-permute-done((f32[48,128]{1,0:T(8,128)S(1)}, f32[48,128]{1,0:T(8,128)S(1)}, u32[]{:S(2)}, u32[]{:S(2)}) %collective-permute-start.9) | collective-permute-done | bytes 24608 | tf_op jit(solution)/shard_map/ppermute | solution.py:132
  43.2 1.1 %collective-permute-start.10 = (f32[48,128]{1,0:T(8,128)S(1)}, f32[48,128]{1,0:T(8,128)S(1)}, u32[]{:S(2)}, u32[]{:S(2)}) collective-permute-start(f32[48,128]{1,0:T(8,128)S(1)} %add_add_fusion), channel_id=1, source_target_pairs={{0,8},{1,9},{2,10},{3,11},{4,12},{5,13},{6,14},{7,15},{8,0},{9,1},... | collective-permute-start | bytes 73736 | tf_op jit(solution)/shard_map/ppermute | solution.py:132
  44.3 0.0 copy-start.1
  44.3 11.2 %shard_map.65.base_ref = f32[48,1024]{1,0:T(8,128)S(1)} custom-call(bf16[16,48,1024]{2,1,0:T(8,128)(2,1)S(1)} %get-tuple-element.8.lhs_ref, bf16[16384,1024]{1,0:T(8,128)(2,1)} %weight_ref.2), custom_call_target="tpu_custom_call" | custom-call | flops 1610612736 | bytes 35651584 | tf_op jit(solution)/shard_map/pallas_call | solution.py:175
  55.6 0.0 collective-permute-done.10
  55.6 0.1 broadcast_in_dim.31.rank_rows_ref
  55.7 0.0 copy-done.1
  55.7 5.9 %shard_map.66 = bf16[16,3,1024]{2,1,0:T(4,128)(2,1)S(1)} custom-call(s32[3,16]{1,0:T(4,128)S(1)} %copy-done.1, s32[48,128]{1,0:T(8,128)S(1)} %broadcast_in_dim.28.adapter_rows_ref, s32[48,128]{1,0:T(8,128)S(1)} %broadcast_in_dim.31.rank_rows_ref, f32[48,128]{1,0:T(8,128)S(1)} %add.19.hidden_ref, f32[48,1024]{1,0:T(8,128)S(1)} %shard_map.65.base_ref, ...), custom_call_target="tpu_custom_call" | custom-call | flops 12582912 | bytes 12582912 | tf_op jit(solution)/shard_map/pallas_call | solution.py:192
  61.6 11.1 %all_to_all.5 = bf16[16,3,1024]{2,1,0:T(4,128)(2,1)S(1)} all-to-all(bf16[16,3,1024]{2,1,0:T(4,128)(2,1)S(1)} %shard_map.66), channel_id=1, replica_groups=mesh['rep'=2,'feat'=16] {'feat'}, dimensions={0} | all-to-all | bytes 196608 | tf_op jit(solution)/shard_map/all_to_all | solution.py:207
  72.7 0.7 copy.14
  (7 shorter events, 0.1 us)
Async XLA Ops:
  0.0 38.5 %copy-start.2 = (s32[64]{0:T(128)S(1)}, s32[64]{0:T(128)}, u32[]{:S(2)}) copy-start(s32[64]{0:T(128)} %param.11) | copy-start | bytes 772
  1.1 5.9 %collective-permute-start = (bf16[48,1024]{1,0:T(8,128)(2,1)S(1)}, bf16[48,1024]{1,0:T(8,128)(2,1)S(1)}, u32[]{:S(2)}, u32[]{:S(2)}) collective-permute-start(bf16[48,1024]{1,0:T(8,128)(2,1)S(1)} %reshape.16), channel_id=1, source_target_pairs={{0,4},{1,5},{2,6},{3,7},{4,0},{5,1},{6,2},{7,3},{8,12},{9,13},{10,... | collective-permute-start | bytes 294920 | tf_op jit(solution)/shard_map/ppermute | solution.py:132
  4.2 10.4 %collective-permute-start.1 = (bf16[48,1024]{1,0:T(8,128)(2,1)S(1)}, bf16[48,1024]{1,0:T(8,128)(2,1)S(1)}, u32[]{:S(2)}, u32[]{:S(2)}) collective-permute-start(bf16[48,1024]{1,0:T(8,128)(2,1)S(1)} %reshape.16), channel_id=1, source_target_pairs={{0,8},{1,9},{2,10},{3,11},{4,12},{5,13},{6,14},{7,15},{8,0},{9,1},... | collective-permute-start | bytes 294920 | tf_op jit(solution)/shard_map/ppermute | solution.py:132
  6.7 7.8 %collective-permute-start.2 = (bf16[48,1024]{1,0:T(8,128)(2,1)S(1)}, bf16[48,1024]{1,0:T(8,128)(2,1)S(1)}, u32[]{:S(2)}, u32[]{:S(2)}) collective-permute-start(bf16[48,1024]{1,0:T(8,128)(2,1)S(1)} %reshape.16), channel_id=1, source_target_pairs={{0,12},{1,13},{2,14},{3,15},{4,8},{5,9},{6,10},{7,11},{8,4},{9,5},... | collective-permute-start | bytes 294920 | tf_op jit(solution)/shard_map/ppermute | solution.py:132
  14.6 9.0 %collective-permute-start.3 = (bf16[192,1024]{1,0:T(8,128)(2,1)S(1)}, bf16[192,1024]{1,0:T(8,128)(2,1)S(1)}, u32[]{:S(2)}, u32[]{:S(2)}) collective-permute-start(bf16[192,1024]{1,0:T(8,128)(2,1)S(1)} %constant_dynamic-update-slice_fusion.refs_0_), channel_id=1, source_target_pairs={{0,2},{1,3},{2,0},{3,1},{4,6},{5,7},{6,4},{7,5},{8,10},{9,11},{10,... | collective-permute-start | bytes 1179656 | tf_op jit(solution)/shard_map/ppermute | solution.py:132
  16.2 8.3 %collective-permute-start.4 = (bf16[192,1024]{1,0:T(8,128)(2,1)S(1)}, bf16[192,1024]{1,0:T(8,128)(2,1)S(1)}, u32[]{:S(2)}, u32[]{:S(2)}) collective-permute-start(bf16[192,1024]{1,0:T(8,128)(2,1)S(1)} %constant_dynamic-update-slice_fusion.refs_0_), channel_id=1, source_target_pairs={{0,1},{1,0},{2,3},{3,2},{4,5},{5,4},{6,7},{7,6},{8,9},{9,8},{10,11... | collective-permute-start | bytes 1179656 | tf_op jit(solution)/shard_map/ppermute | solution.py:132
  23.6 1.7 %collective-permute-start.5 = (bf16[192,1024]{1,0:T(8,128)(2,1)S(1)}, bf16[192,1024]{1,0:T(8,128)(2,1)S(1)}, u32[]{:S(2)}, u32[]{:S(2)}) collective-permute-start(bf16[192,1024]{1,0:T(8,128)(2,1)S(1)} %collective-permute-done.3.refs_1_), channel_id=1, source_target_pairs={{0,1},{1,0},{2,3},{3,2},{4,5},{5,4},{6,7},{7,6},{8,9},{9,8},{10,11... | collective-permute-start | bytes 1179656 | tf_op jit(solution)/shard_map/ppermute | solution.py:132
  25.4 0.7 copy-start
  33.4 1.3 %collective-permute-start.6 = (f32[48,128]{1,0:T(8,128)S(1)}, f32[48,128]{1,0:T(8,128)S(1)}, u32[]{:S(2)}, u32[]{:S(2)}) collective-permute-start(f32[48,128]{1,0:T(8,128)S(1)} %get-tuple-element.7), channel_id=1, source_target_pairs={{0,1},{1,0},{2,3},{3,2},{4,5},{5,4},{6,7},{7,6},{8,9},{9,8},{10,11... | collective-permute-start | bytes 73736 | tf_op jit(solution)/shard_map/ppermute | solution.py:132
  34.7 4.0 %collective-permute-start.7 = (f32[48,128]{1,0:T(8,128)S(1)}, f32[48,128]{1,0:T(8,128)S(1)}, u32[]{:S(2)}, u32[]{:S(2)}) collective-permute-start(f32[48,128]{1,0:T(8,128)S(1)} %add.15), channel_id=1, source_target_pairs={{0,2},{1,3},{2,0},{3,1},{4,6},{5,7},{6,4},{7,5},{8,10},{9,11},{10,... | collective-permute-start | bytes 73736 | tf_op jit(solution)/shard_map/ppermute | solution.py:132
  36.2 4.1 %collective-permute-start.8 = (f32[48,128]{1,0:T(8,128)S(1)}, f32[48,128]{1,0:T(8,128)S(1)}, u32[]{:S(2)}, u32[]{:S(2)}) collective-permute-start(f32[48,128]{1,0:T(8,128)S(1)} %add.15), channel_id=1, source_target_pairs={{0,4},{1,5},{2,6},{3,7},{4,0},{5,1},{6,2},{7,3},{8,12},{9,13},{10,... | collective-permute-start | bytes 73736 | tf_op jit(solution)/shard_map/ppermute | solution.py:132
  38.5 4.7 %collective-permute-start.9 = (f32[48,128]{1,0:T(8,128)S(1)}, f32[48,128]{1,0:T(8,128)S(1)}, u32[]{:S(2)}, u32[]{:S(2)}) collective-permute-start(f32[48,128]{1,0:T(8,128)S(1)} %add.15), channel_id=1, source_target_pairs={{0,6},{1,7},{2,4},{3,5},{4,2},{5,3},{6,0},{7,1},{8,14},{9,15},{10,... | collective-permute-start | bytes 73736 | tf_op jit(solution)/shard_map/ppermute | solution.py:132
  43.2 12.3 %collective-permute-start.10 = (f32[48,128]{1,0:T(8,128)S(1)}, f32[48,128]{1,0:T(8,128)S(1)}, u32[]{:S(2)}, u32[]{:S(2)}) collective-permute-start(f32[48,128]{1,0:T(8,128)S(1)} %add_add_fusion), channel_id=1, source_target_pairs={{0,8},{1,9},{2,10},{3,11},{4,12},{5,13},{6,14},{7,15},{8,0},{9,1},... | collective-permute-start | bytes 73736 | tf_op jit(solution)/shard_map/ppermute | solution.py:132
  44.3 11.4 %copy-start.1 = (s32[3,16]{1,0:T(4,128)S(1)}, s32[3,16]{1,0:T(4,128)}, u32[]{:S(2)}) copy-start(s32[3,16]{1,0:T(4,128)} %table_ref.3) | copy-start | bytes 580

commit v2 on v1

v2 whole, which is shorter than its diff:
```python
import functools

import jax
import jax.numpy as jnp
from jax import lax
from jax.experimental import pallas as pl
from jax.experimental.pallas import tpu as pltpu
from jax.sharding import PartitionSpec as P

VMEM, SMEM, ANY = pltpu.VMEM, pltpu.SMEM, pl.ANY
GROUP = 4
LANES = 128


def list_adapters(table_ref, seen, listed):
    steps, owners = table_ref.shape
    rows = steps * owners

    def clear(i, carry):
        seen[i] = jnp.int32(0)
        return carry

    def unlist(i, carry):
        listed[i] = jnp.int32(-1)
        return carry

    lax.fori_loop(0, seen.shape[0], clear, 0)
    lax.fori_loop(0, rows, unlist, 0)
    count = jnp.int32(0)
    for b in range(rows):
        adapter = table_ref[b % steps, b // steps]
        new = seen[adapter] == 0

        @pl.when(new)
        def _():
            seen[adapter] = jnp.int32(1)
            listed[count] = adapter

        count = count + new.astype(jnp.int32)
    listed[rows] = count


def padded(count):
    return (count + GROUP - 1) // GROUP * GROUP


def start_slices(listed, weight_ref, held, sem):
    def one(slot, carry):
        adapter = jnp.maximum(listed[slot], 0)
        pltpu.make_async_copy(weight_ref.at[adapter], held.at[slot], sem).start()
        return carry

    lax.fori_loop(0, padded(listed[held.shape[0]]), one, 0)


def wait_slices(listed, weight_ref, held, sem):
    def one(slot, carry):
        pltpu.make_async_copy(weight_ref.at[0], held.at[slot], sem).wait()
        return carry

    lax.fori_loop(0, padded(listed[held.shape[0]]), one, 0)


def fetch_kernel(first, weight_ref, *refs):
    held, sem = refs[-2:]
    copy = pltpu.make_async_copy(weight_ref.at[pl.ds(first, held.shape[0])], held, sem)
    copy.start()
    copy.wait()


def fetch_both_kernel(first, table_ref, weight_ref, slices_ref, held, slices, listed, seen, sem, slice_sem):
    copy = pltpu.make_async_copy(weight_ref.at[pl.ds(first, held.shape[0])], held, sem)
    copy.start()
    list_adapters(table_ref, seen, listed)
    start_slices(listed, slices_ref, slices, slice_sem)
    wait_slices(listed, slices_ref, slices, slice_sem)
    copy.wait()


def down_kernel(listed, place_ref, adapter_rows_ref, *refs):
    *parts, slices, out_ref = refs
    rows, width = out_ref.shape
    place = place_ref[...][:, :1]
    mine = jnp.zeros((rows, slices.shape[1]), jnp.float32)
    first = 0
    for part in parts:
        chosen = lax.broadcasted_iota(jnp.int32, (rows, part.shape[0]), 1) + first == place
        chosen = jnp.where(chosen, jnp.float32(1.0), jnp.float32(0.0)).astype(jnp.bfloat16)
        mine += jnp.dot(chosen, part[...], preferred_element_type=jnp.float32)
        first += part.shape[0]
    mine = mine.astype(jnp.bfloat16)
    adapter_rows = adapter_rows_ref[...]

    def one(group, total):
        for pair in range(0, GROUP, 2):
            slot = group * GROUP + pair
            both = jnp.concatenate([slices[slot], slices[slot + 1]], axis=1)
            product = jnp.dot(mine, both, preferred_element_type=jnp.float32)
            total = jnp.where(adapter_rows == listed[slot], product[:, :width], total)
            total = jnp.where(adapter_rows == listed[slot + 1], product[:, width:], total)
        return total

    zeros = jnp.zeros((rows, width), jnp.float32)
    out_ref[...] = lax.fori_loop(0, padded(listed[rows]) // GROUP, one, zeros)


def first_base_kernel(order, me_ref, listed, *refs):
    parts = refs[: len(order)]
    weight, slices_ref, lhs_ref, out_ref, slices, wide, slice_sem = refs[len(order) :]
    start_slices(listed, slices_ref, slices, slice_sem)
    chunks, rows, depth = lhs_ref.shape
    block = rows // chunks * chunks
    me = me_ref[0]
    for part, owners in zip(parts, order, strict=True):
        for place, distance in enumerate(owners):
            owner = jnp.bitwise_xor(me, distance)
            at = pl.ds(pl.multiple_of(owner * block, block), block)
            for tile in range(depth // LANES):
                piece = part[place * block : (place + 1) * block, tile * LANES : (tile + 1) * LANES]
                wide[tile, at, :] = piece.astype(jnp.float32)
    for chunk in range(chunks):
        for tile in range(depth // LANES):
            piece = wide[tile, pl.ds(chunk, rows, stride=chunks), :]
            lhs_ref[chunk, :, tile * LANES : (tile + 1) * LANES] = piece.astype(jnp.bfloat16)
    total = jnp.zeros(out_ref.shape, jnp.float32)
    for chunk in range(weight.shape[0] // depth):
        matrix = weight[chunk * depth : (chunk + 1) * depth, :]
        total += jnp.dot(lhs_ref[chunk], matrix, preferred_element_type=jnp.float32)
    out_ref[...] = total
    wait_slices(listed, slices_ref, slices, slice_sem)


def rest_base_kernel(lhs_ref, base_ref, weight, rest_ref, out_ref, rest, sems):
    chunks, rows, depth = lhs_ref.shape
    start = rest_ref.shape[0] - rest.shape[0] * depth
    copies = []
    for chunk in range(rest.shape[0]):
        there = rest_ref.at[pl.ds(start + chunk * depth, depth)]
        copies.append(pltpu.make_async_copy(there, rest.at[chunk], sems.at[chunk]))
        copies[chunk].start()
    total = base_ref[...]
    here = weight.shape[0] // depth
    first = chunks - here - len(copies)
    for chunk in range(here):
        matrix = weight[chunk * depth : (chunk + 1) * depth, :]
        total += jnp.dot(lhs_ref[first + chunk], matrix, preferred_element_type=jnp.float32)
    for chunk in range(len(copies)):
        copies[chunk].wait()
        total += jnp.dot(lhs_ref[first + here + chunk], rest[chunk], preferred_element_type=jnp.float32)
    out_ref[...] = total


def up_kernel(listed, adapter_rows_ref, rank_rows_ref, hidden_ref, base_ref, slices, out_ref):
    rows, width = hidden_ref.shape
    rank_rows = rank_rows_ref[...]
    keep = lax.broadcasted_iota(jnp.int32, rank_rows.shape, 1) < rank_rows
    factor = 0.25 * width / rank_rows.astype(jnp.float32)
    lowrank = jnp.where(keep, hidden_ref[...] * factor, jnp.float32(0.0))
    adapter_rows = adapter_rows_ref[...]

    def one(group, total):
        slot = group * GROUP
        own = [jnp.where(adapter_rows == listed[slot + i], lowrank, jnp.float32(0.0)) for i in range(GROUP)]
        own = jnp.concatenate(own, axis=1).astype(jnp.bfloat16)
        matrix = jnp.concatenate([slices[slot + i] for i in range(GROUP)], axis=0)
        return total + jnp.dot(own, matrix, preferred_element_type=jnp.float32)

    total = lax.fori_loop(0, padded(listed[rows]) // GROUP, one, base_ref[...])
    total = total.astype(jnp.bfloat16)
    steps = out_ref.shape[1]
    for owner in range(out_ref.shape[0]):
        out_ref[owner] = total[owner * steps : (owner + 1) * steps, :]


def exchange(value, distance, ranks):
    return lax.ppermute(value, "feat", [(i, i ^ distance) for i in range(ranks)])


def spec(space, count=1):
    return [pl.BlockSpec(memory_space=space)] * count


def cost(flops, size):
    return pl.CostEstimate(flops=flops, bytes_accessed=size, transcendentals=0)


def held_here(value):
    return pltpu.with_memory_space_constraint(value, VMEM)


def left_there(value):
    return pltpu.with_memory_space_constraint(value, pltpu.HBM)


def fast(tokens, query_weight, adapter_down_weight, adapter_up_weight, adapter_index_table, adapter_rank_sizes):
    steps, _, features = tokens.shape
    ranks = adapter_index_table.shape[1]
    columns = query_weight.shape[1]
    adapters, depth, width = adapter_down_weight.shape
    rows = steps * ranks
    bf16, f32 = jnp.bfloat16, jnp.float32
    swap = functools.partial(exchange, ranks=ranks)
    shape = jax.ShapeDtypeStruct
    params = pltpu.CompilerParams(vmem_limit_bytes=5 << 20)
    flops = 2 * rows * features * columns

    adapter_rows = jnp.broadcast_to(adapter_index_table.T.reshape(rows, 1), (rows, width))
    matches = adapter_rows[:, :1] == jnp.arange(adapters)[None, :]
    rank_rows = jnp.sum(jnp.where(matches, adapter_rank_sizes[None, :], 0), axis=1, keepdims=True)
    rank_rows = jnp.broadcast_to(rank_rows, (rows, width))
    me = lax.axis_index("feat").astype(jnp.int32)
    row = jnp.arange(rows, dtype=jnp.int32)
    distance = (row // steps) ^ me
    number = (distance & 1) * 2 + ((distance >> 1) & 1)
    place = (number * (ranks // 4) + (distance >> 2)) * rows + (row % steps) * ranks + me
    place = jnp.broadcast_to(place[:, None], (rows, width))
    me = me.reshape(1)
    order = tuple(tuple(first ^ z for z in (0, 4, 8, 12)) for first in (0, 2, 1, 3))

    early, late = features // 16 * 7, features // 16 * 4
    weight_early = pl.pallas_call(
        functools.partial(fetch_kernel, 0),
        out_shape=VMEM((early, columns), bf16),
        in_specs=spec(ANY, 5),
        out_specs=spec(VMEM)[0],
        scratch_shapes=[pltpu.SemaphoreType.DMA],
        compiler_params=params,
        cost_estimate=cost(0, early * columns * 2),
    )(left_there(query_weight), me, place, adapter_rows, rank_rows)
    own = tokens.reshape(steps * ranks, features // ranks)
    across = (swap(own, 4), swap(own, 8), swap(own, 12))
    across, weight_early = lax.optimization_barrier((across, weight_early))
    near = jnp.concatenate([own, *across], axis=0)
    weight_late, down_slices, listed = pl.pallas_call(
        functools.partial(fetch_both_kernel, early),
        out_shape=(
            VMEM((late, columns), bf16),
            VMEM((rows, depth, width), bf16),
            shape((rows + 1,), jnp.int32),
        ),
        in_specs=spec(SMEM) + spec(ANY, 2),
        out_specs=spec(VMEM, 2) + spec(SMEM),
        scratch_shapes=[
            SMEM((adapters,), jnp.int32),
            pltpu.SemaphoreType.DMA,
            pltpu.SemaphoreType.DMA,
        ],
        compiler_params=params,
        cost_estimate=cost(0, late * columns * 2 + rows * depth * width * 2),
    )(adapter_index_table, left_there(query_weight), left_there(adapter_down_weight))
    far = swap(near, 2)
    far, weight_late, down_slices, listed = lax.optimization_barrier((far, weight_late, down_slices, listed))
    parts = (near, far, swap(near, 1), swap(far, 1))

    hidden = pl.pallas_call(
        down_kernel,
        out_shape=shape((rows, width), f32),
        in_specs=spec(SMEM) + spec(VMEM, 2 + len(parts) + 1),
        out_specs=spec(VMEM)[0],
        compiler_params=params,
        cost_estimate=cost(2 * rows * depth * width * rows, 1 << 20),
    )(listed, place, adapter_rows, *parts, held_here(down_slices))

    lhs, base, up_slices = pl.pallas_call(
        functools.partial(first_base_kernel, order),
        out_shape=(
            shape((ranks, rows, features // ranks), bf16),
            shape((rows, columns), f32),
            VMEM((rows, width, columns), bf16),
        ),
        in_specs=spec(SMEM, 2) + spec(VMEM, len(parts) + 1) + spec(ANY),
        out_specs=spec(VMEM, 3),
        scratch_shapes=[
            VMEM((depth // LANES, rows * ranks, LANES), f32),
            pltpu.SemaphoreType.DMA,
        ],
        compiler_params=params,
        cost_estimate=cost(flops // 2, 16 << 20),
    )(me, listed, *parts, held_here(weight_early), left_there(adapter_up_weight))

    hidden = hidden + swap(hidden, 1)
    three = (swap(hidden, 2), swap(hidden, 4), swap(hidden, 6))
    three, lhs, base, up_slices = lax.optimization_barrier((three, lhs, base, up_slices))
    hidden = hidden + three[0] + three[1] + three[2]

    base = pl.pallas_call(
        rest_base_kernel,
        out_shape=shape((rows, columns), f32),
        in_specs=spec(VMEM, 3) + spec(ANY),
        out_specs=spec(VMEM)[0],
        scratch_shapes=[
            VMEM((5, features // ranks, columns), bf16),
            pltpu.SemaphoreType.DMA((5,)),
        ],
        compiler_params=pltpu.CompilerParams(vmem_limit_bytes=15 << 20),
        cost_estimate=cost(flops // 2, 10 << 20),
    )(lhs, base, held_here(weight_late), left_there(query_weight))
    last, base = lax.optimization_barrier((swap(hidden, 8), base))
    hidden = hidden + last

    out = pl.pallas_call(
        up_kernel,
        out_shape=shape((ranks, steps, columns), bf16),
        in_specs=spec(SMEM) + spec(VMEM, 5),
        out_specs=spec(VMEM)[0],
        compiler_params=params,
        cost_estimate=cost(2 * rows * width * columns * rows, 1 << 20),
    )(listed, adapter_rows, rank_rows, hidden, base, held_here(up_slices))

    gathered = lax.all_to_all(out, "feat", split_axis=0, concat_axis=0, tiled=True)
    return gathered.transpose(1, 0, 2).reshape(steps, 1, features)


def plain(tokens, query_weight, adapter_down_weight, adapter_up_weight, adapter_index_table, adapter_rank_sizes):
    width = query_weight.shape[1]
    rank_width = adapter_down_weight.shape[2]
    depth = adapter_down_weight.shape[1]
    whole = lax.all_gather(tokens, "feat", axis=1, tiled=True)
    piece = lax.dynamic_slice_in_dim(whole, lax.axis_index("feat") * depth, depth, 2)
    matrices = adapter_down_weight[adapter_index_table]
    partial = jnp.einsum("xun,xune->xue", piece, matrices, preferred_element_type=jnp.float32)
    hidden = lax.psum(partial, "feat")
    rank_rows = adapter_rank_sizes[adapter_index_table]
    keep = jnp.arange(rank_width)[None, None, :] < rank_rows[:, :, None]
    factor = 0.25 * rank_width / rank_rows.astype(jnp.float32)
    lowrank = jnp.where(keep, hidden * factor[:, :, None], jnp.float32(0.0)).astype(jnp.bfloat16)
    matrices = adapter_up_weight[adapter_index_table]
    update = jnp.einsum("jma,jmap->jmp", lowrank, matrices, preferred_element_type=jnp.float32)
    base = jnp.einsum("sbd,dc->sbc", whole, query_weight, preferred_element_type=jnp.float32)
    out = (base + update).astype(jnp.bfloat16)
    return lax.all_to_all(out, "feat", split_axis=1, concat_axis=2, tiled=True)


def on_device(tokens, query_weight, *rest):
    ranks = rest[2].shape[1]
    fits = ranks == 16 and query_weight.shape[1] % 256 == 0
    return (fast if fits else plain)(tokens, query_weight, *rest)


def solution(mesh):
    in_specs = (
        P(None, ("rep", "feat"), None),
        P(None, "feat"),
        P(None, "feat", None),
        P(None, None, "feat"),
        P(None, "rep"),
        P(),
    )
    out_specs = P(None, ("rep", "feat"), None)
    return jax.shard_map(
        on_device, mesh=mesh, in_specs=in_specs, out_specs=out_specs, check_vma=False
    )
```

time: 73.6 us -> 62.1 us (0.84)
  waiting for transfers between devices: 21.7 us -> 4.64 us
  Pallas kernels: 24.4 us -> 28.2 us
    ppermute x11, waiting for transfers between devices: 21.7 us -> 4.64 us  [exchange(): lax.ppermute(value, 'feat', [(i, i ^ distance) for i in range(ranks)])]
    pallas_call x3 -> x6, Pallas kernels: 24.4 us -> 28.2 us  [the longest x1 7.18 us: fast(): pl.pallas_call(functools.partial(fetch_both_kernel, early), out_shape=(VM...]
    ppermute x11, starting transfers between devices: 12.4 us -> 13.1 us  [exchange(): lax.ppermute(value, 'feat', [(i, i ^ distance) for i in range(ranks)])]
  transfers between devices with their start and end apart: 11 -> 11, of which waited for: 7 -> 5; matrix products, arithmetic and copies ran while one was open for 1% -> 3% of each run, Pallas kernels for 15% -> 35%
where the time goes in v2:
time: 62.1 us; the launch traced here: 61.6 us
  Pallas kernels  28.2 us (45%)
  starting transfers between devices  13.1 us (21%)
  blocking collectives  11.8 us (19%)
  waiting for transfers between devices  4.64 us (7%)
  local copies, waits for them, and re-layouts  2.79 us (4%)
  other arithmetic  0.88 us (1%)
    ppermute x11, starting transfers between devices, exchange(): lax.ppermute(value, 'feat', [(i, i ^ distance) for i in range(ranks)])  13.1 us
    all_to_all x1, blocking collectives, fast(): lax.all_to_all(out, 'feat', split_axis=0, concat_axis=0, tiled=True)  11.8 us
    pallas_call x1, Pallas kernels, fast(): pl.pallas_call(functools.partial(fetch_both_kernel, early), out_shape=(VM...  7.18 us
    pallas_call x1, Pallas kernels, fast(): pl.pallas_call(functools.partial(fetch_kernel, 0), out_shape=VMEM((early,...  5.21 us
    pallas_call x1, Pallas kernels, fast(): pl.pallas_call(functools.partial(first_base_kernel, order), out_shape=(sh...  4.78 us
    ppermute x11, waiting for transfers between devices, exchange(): lax.ppermute(value, 'feat', [(i, i ^ distance) for i in range(ranks)])  4.64 us
    pallas_call x1, Pallas kernels, fast(): pl.pallas_call(rest_base_kernel, out_shape=shape((rows, columns), f32), i...  4.58 us
    pallas_call x1, Pallas kernels, fast(): pl.pallas_call(down_kernel, out_shape=shape((rows, width), f32), in_specs...  3.35 us
  transfers between devices with their start and end apart: 11, of which 5 were waited for; matrix products, arithmetic and copies ran while one was open for 3% of the time, Pallas kernels for 35%

profile of v2, /device:TPU:0, one launch (start us, length us, event | category | flops | bytes accessed | tf_op | source)
XLA Modules:
  0.0 61.6 jit_solution(13597802575683883693)
XLA Ops:
  0.0 1.0 %reshape.45 = bf16[48,1024]{1,0:T(8,128)(2,1)S(1)} reshape(bf16[3,1,16384]{2,0,1:T(4,128)(2,1)} %param.6) | data formatting | bytes 196608 | tf_op jit(solution)/shard_map/reshape | solution.py:230
  1.0 5.1 %collective-permute-start.2 = (bf16[48,1024]{1,0:T(8,128)(2,1)S(1)}, bf16[48,1024]{1,0:T(8,128)(2,1)S(1)}, u32[]{:S(2)}, u32[]{:S(2)}) collective-permute-start(bf16[48,1024]{1,0:T(8,128)(2,1)S(1)} %reshape.45), channel_id=1, source_target_pairs={{0,12},{1,13},{2,14},{3,15},{4,8},{5,9},{6,10},{7,11},{8,4},{9,5},... | collective-permute-start | bytes 294920 | tf_op jit(solution)/shard_map/ppermute | solution.py:176
  6.2 0.0 collective-permute-start.1
  6.2 0.6 %collective-permute-start = (bf16[48,1024]{1,0:T(8,128)(2,1)S(1)}, bf16[48,1024]{1,0:T(8,128)(2,1)S(1)}, u32[]{:S(2)}, u32[]{:S(2)}) collective-permute-start(bf16[48,1024]{1,0:T(8,128)(2,1)S(1)} %reshape.45), channel_id=1, source_target_pairs={{0,4},{1,5},{2,6},{3,7},{4,0},{5,1},{6,2},{7,3},{8,12},{9,13},{10,... | collective-permute-start | bytes 294920 | tf_op jit(solution)/shard_map/ppermute | solution.py:176
  6.8 0.8 %copy.9 = s32[16,3]{1,0:T(8,128)S(1)} copy(s32[16,3]{0,1:T(4,128)} %bitcast.7) | data formatting | bytes 384 | tf_op jit(solution)/shard_map/transpose | solution.py:207
  7.6 0.1 broadcast_in_dim.34
  7.7 0.8 %select_reduce_fusion = s32[48]{0:T(128)S(1)} fusion(s32[64]{0:T(128)} %param.11, s32[48]{0:T(128)S(1)} %broadcast_in_dim.34), kind=kLoop, calls=%fused_computation.1 | loop fusion | flops 9168 | bytes 640 | tf_op jit(solution)/shard_map/reduce_sum | solution.py:209
  8.5 0.1 broadcast_in_dim.35.refs_2_.adapter_rows_ref
  8.6 0.1 broadcast_in_dim.38.refs_3_.rank_rows_ref
  8.6 0.1 broadcast_in_dim.20.refs_1_.place_ref
  8.7 0.0 copy-start
  8.7 5.2 %shard_map.64.refs_4_ = bf16[7168,1024]{1,0:T(8,128)(2,1)S(1)} custom-call(bf16[16384,1024]{1,0:T(8,128)(2,1)} %rest_ref.1, s32[1]{0:T(128)} %bitcast.refs_0_.me_ref, s32[48,128]{1,0:T(8,128)S(1)} %broadcast_in_dim.20.refs_1_.place_ref, s32[48,128]{1,0:T(8,128)S(1)} %broadcast_in_dim.35.refs_2_.adapter_rows_ref, ...), custom_call_target="tpu_custom_call" | custom-call | bytes 14680064 | tf_op jit(solution)/shard_map/pallas_call | solution.py:221
  14.0 0.0 collective-permute-done.2
  14.0 0.5 collective-permute-done.1
  14.4 0.0 collective-permute-done
  14.5 1.6 %collective-permute-start.3 = (bf16[192,1024]{1,0:T(8,128)(2,1)S(1)}, bf16[192,1024]{1,0:T(8,128)(2,1)S(1)}, u32[]{:S(2)}, u32[]{:S(2)}) collective-permute-start(bf16[192,1024]{1,0:T(8,128)(2,1)S(1)} %constant_dynamic-update-slice_fusion.refs_0_), channel_id=1, source_target_pairs={{0,2},{1,3},{2,0},{3,1},{4,6},{5,7},{6,4},{7,5},{8,10},{9,11},{10,... | collective-permute-start | bytes 1179656 | tf_op jit(solution)/shard_map/ppermute | solution.py:176
  16.1 0.0 copy-done
  16.1 7.2 %shard_map.65 = (bf16[4096,1024]{1,0:T(8,128)(2,1)S(1)}, bf16[48,1024,128]{2,1,0:T(8,128)(2,1)S(1)}, s32[49]{0:T(128)S(1)}) custom-call(s32[3,16]{1,0:T(4,128)S(1)} %copy-done, bf16[16384,1024]{1,0:T(8,128)(2,1)} %rest_ref.1, bf16[64,1024,128]{2,1,0:T(8,128)(2,1)} %slices_ref.1), custom_call_target="tpu_custom_call" | custom-call | bytes 20971520 | tf_op jit(solution)/shard_map/pallas_call | solution.py:234
  23.2 0.1 collective-permute-start.4
  23.3 1.4 %collective-permute-done.3.refs_1_ = bf16[192,1024]{1,0:T(8,128)(2,1)S(1)} collective-permute-done((bf16[192,1024]{1,0:T(8,128)(2,1)S(1)}, bf16[192,1024]{1,0:T(8,128)(2,1)S(1)}, u32[]{:S(2)}, u32[]{:S(2)}) %collective-permute-start.3) | collective-permute-done | bytes 393248 | tf_op jit(solution)/shard_map/ppermute | solution.py:176
  24.7 0.0 collective-permute-start.5
  24.7 0.3 collective-permute-done.4.refs_2_
  25.0 1.4 %collective-permute-done.5.refs_3_ = bf16[192,1024]{1,0:T(8,128)(2,1)S(1)} collective-permute-done((bf16[192,1024]{1,0:T(8,128)(2,1)S(1)}, bf16[192,1024]{1,0:T(8,128)(2,1)S(1)}, u32[]{:S(2)}, u32[]{:S(2)}) %collective-permute-start.5) | collective-permute-done | bytes 393248 | tf_op jit(solution)/shard_map/ppermute | solution.py:176
  26.4 3.4 %shard_map.66 = f32[48,128]{1,0:T(8,128)S(1)} custom-call(s32[49]{0:T(128)S(1)} %get-tuple-element.33.listed, s32[48,128]{1,0:T(8,128)S(1)} %broadcast_in_dim.20.refs_1_.place_ref, s32[48,128]{1,0:T(8,128)S(1)} %broadcast_in_dim.35.refs_2_.adapter_rows_ref, bf16[192,1024]{1,0:T(8,128)(2,1)S(1)} %constant_dynamic-update-slice_fusion.refs_0_, ...), custom_call_target="tpu_custom_call" | custom-call | flops 603979776 | bytes 1048576 | tf_op jit(solution)/shard_map/pallas_call | solution.py:255
  29.8 0.2 collective-permute-start.6
  30.0 1.1 %collective-permute-done.6 = f32[48,128]{1,0:T(8,128)S(1)} collective-permute-done((f32[48,128]{1,0:T(8,128)S(1)}, f32[48,128]{1,0:T(8,128)S(1)}, u32[]{:S(2)}, u32[]{:S(2)}) %collective-permute-start.6) | collective-permute-done | bytes 24608 | tf_op jit(solution)/shard_map/ppermute | solution.py:176
  31.1 2.0 %collective-permute-start.9 = (f32[48,128]{1,0:T(8,128)S(1)}, f32[48,128]{1,0:T(8,128)S(1)}, u32[]{:S(2)}, u32[]{:S(2)}) collective-permute-start(f32[48,128]{1,0:T(8,128)S(1)} %add.64), channel_id=1, source_target_pairs={{0,6},{1,7},{2,4},{3,5},{4,2},{5,3},{6,0},{7,1},{8,14},{9,15},{10,... | collective-permute-start | bytes 73736 | tf_op jit(solution)/shard_map/ppermute | solution.py:176
  33.1 1.0 %collective-permute-start.8 = (f32[48,128]{1,0:T(8,128)S(1)}, f32[48,128]{1,0:T(8,128)S(1)}, u32[]{:S(2)}, u32[]{:S(2)}) collective-permute-start(f32[48,128]{1,0:T(8,128)S(1)} %add.64), channel_id=1, source_target_pairs={{0,4},{1,5},{2,6},{3,7},{4,0},{5,1},{6,2},{7,3},{8,12},{9,13},{10,... | collective-permute-start | bytes 73736 | tf_op jit(solution)/shard_map/ppermute | solution.py:176
  34.0 0.5 collective-permute-start.7
  34.6 4.8 %shard_map.67 = (bf16[16,48,1024]{2,1,0:T(8,128)(2,1)S(1)}, f32[48,1024]{1,0:T(8,128)S(1)}, bf16[48,128,1024]{2,1,0:T(8,128)(2,1)S(1)}) custom-call(s32[1]{0:T(128)} %bitcast.refs_0_.me_ref, s32[49]{0:T(128)S(1)} %get-tuple-element.33.listed, bf16[192,1024]{1,0:T(8,128)(2,1)S(1)} %constant_dynamic-update-slice_fusion.refs_0_, ...), custom_call_target="tpu_custom_call" | custom-call | flops 805306368 | bytes 16777216 | tf_op jit(solution)/shard_map/pallas_call | solution.py:264
  39.3 0.0 collective-permute-done.9
  39.4 0.0 collective-permute-done.8
  39.4 0.0 collective-permute-done.7
  39.4 2.0 %collective-permute-start.10 = (f32[48,128]{1,0:T(8,128)S(1)}, f32[48,128]{1,0:T(8,128)S(1)}, u32[]{:S(2)}, u32[]{:S(2)}) collective-permute-start(f32[48,128]{1,0:T(8,128)S(1)} %add_add_fusion), channel_id=1, source_target_pairs={{0,8},{1,9},{2,10},{3,11},{4,12},{5,13},{6,14},{7,15},{8,0},{9,1},... | collective-permute-start | bytes 73736 | tf_op jit(solution)/shard_map/ppermute | solution.py:176
  41.4 4.6 %shard_map.68.base_ref = f32[48,1024]{1,0:T(8,128)S(1)} custom-call(bf16[16,48,1024]{2,1,0:T(8,128)(2,1)S(1)} %get-tuple-element.43.lhs_ref, f32[48,1024]{1,0:T(8,128)S(1)} %get-tuple-element.44.base_ref, bf16[4096,1024]{1,0:T(8,128)(2,1)S(1)} %get-tuple-element.45.weight, bf16[16384,1024]{1,0:T(8,128)(2,1)} %rest_ref.1), custom_call_target="tpu_custom_call" | custom-call | flops 805306368 | bytes 10485760 | tf_op jit(solution)/shard_map/pallas_call | solution.py:286
  46.0 0.0 collective-permute-done.10
  46.0 3.1 %shard_map.69 = bf16[16,3,1024]{2,1,0:T(4,128)(2,1)S(1)} custom-call(s32[49]{0:T(128)S(1)} %get-tuple-element.33.listed, s32[48,128]{1,0:T(8,128)S(1)} %broadcast_in_dim.35.refs_2_.adapter_rows_ref, s32[48,128]{1,0:T(8,128)S(1)} %broadcast_in_dim.38.refs_3_.rank_rows_ref, f32[48,128]{1,0:T(8,128)S(1)} %add.68.hidden_ref, f32[48,1024]{1,0:T(8,128)S(1)} %shard_map.68.base_ref, ...), custom_call_target="tpu_custom_call" | custom-call | flops 603979776 | bytes 1048576 | tf_op jit(solution)/shard_map/pallas_call | solution.py:301
  49.1 11.8 %all_to_all.5 = bf16[16,3,1024]{2,1,0:T(4,128)(2,1)S(1)} all-to-all(bf16[16,3,1024]{2,1,0:T(4,128)(2,1)S(1)} %shard_map.69), channel_id=1, replica_groups=mesh['rep'=2,'feat'=16] {'feat'}, dimensions={0} | all-to-all | bytes 196608 | tf_op jit(solution)/shard_map/all_to_all | solution.py:310
  60.9 0.7 %copy.14 = bf16[3,1,16384]{2,0,1:T(4,128)(2,1)} copy(bf16[3,1,16384]{2,0,1:T(4,128)(2,1)S(1)} %bitcast.8) | data formatting | bytes 196608
  (8 shorter events, 0.1 us)
Async XLA Ops:
  1.0 12.9 %collective-permute-start.2 = (bf16[48,1024]{1,0:T(8,128)(2,1)S(1)}, bf16[48,1024]{1,0:T(8,128)(2,1)S(1)}, u32[]{:S(2)}, u32[]{:S(2)}) collective-permute-start(bf16[48,1024]{1,0:T(8,128)(2,1)S(1)} %reshape.45), channel_id=1, source_target_pairs={{0,12},{1,13},{2,14},{3,15},{4,8},{5,9},{6,10},{7,11},{8,4},{9,5},... | collective-permute-start | bytes 294920 | tf_op jit(solution)/shard_map/ppermute | solution.py:176
  6.2 8.3 %collective-permute-start.1 = (bf16[48,1024]{1,0:T(8,128)(2,1)S(1)}, bf16[48,1024]{1,0:T(8,128)(2,1)S(1)}, u32[]{:S(2)}, u32[]{:S(2)}) collective-permute-start(bf16[48,1024]{1,0:T(8,128)(2,1)S(1)} %reshape.45), channel_id=1, source_target_pairs={{0,8},{1,9},{2,10},{3,11},{4,12},{5,13},{6,14},{7,15},{8,0},{9,1},... | collective-permute-start | bytes 294920 | tf_op jit(solution)/shard_map/ppermute | solution.py:176
  6.2 8.3 %collective-permute-start = (bf16[48,1024]{1,0:T(8,128)(2,1)S(1)}, bf16[48,1024]{1,0:T(8,128)(2,1)S(1)}, u32[]{:S(2)}, u32[]{:S(2)}) collective-permute-start(bf16[48,1024]{1,0:T(8,128)(2,1)S(1)} %reshape.45), channel_id=1, source_target_pairs={{0,4},{1,5},{2,6},{3,7},{4,0},{5,1},{6,2},{7,3},{8,12},{9,13},{10,... | collective-permute-start | bytes 294920 | tf_op jit(solution)/shard_map/ppermute | solution.py:176
  8.7 7.3 %copy-start = (s32[3,16]{1,0:T(4,128)S(1)}, s32[3,16]{1,0:T(4,128)}, u32[]{:S(2)}) copy-start(s32[3,16]{1,0:T(4,128)} %table_ref.1) | copy-start | bytes 580
  14.5 10.2 %collective-permute-start.3 = (bf16[192,1024]{1,0:T(8,128)(2,1)S(1)}, bf16[192,1024]{1,0:T(8,128)(2,1)S(1)}, u32[]{:S(2)}, u32[]{:S(2)}) collective-permute-start(bf16[192,1024]{1,0:T(8,128)(2,1)S(1)} %constant_dynamic-update-slice_fusion.refs_0_), channel_id=1, source_target_pairs={{0,2},{1,3},{2,0},{3,1},{4,6},{5,7},{6,4},{7,5},{8,10},{9,11},{10,... | collective-permute-start | bytes 1179656 | tf_op jit(solution)/shard_map/ppermute | solution.py:176
  23.2 1.8 %collective-permute-start.4 = (bf16[192,1024]{1,0:T(8,128)(2,1)S(1)}, bf16[192,1024]{1,0:T(8,128)(2,1)S(1)}, u32[]{:S(2)}, u32[]{:S(2)}) collective-permute-start(bf16[192,1024]{1,0:T(8,128)(2,1)S(1)} %constant_dynamic-update-slice_fusion.refs_0_), channel_id=1, source_target_pairs={{0,1},{1,0},{2,3},{3,2},{4,5},{5,4},{6,7},{7,6},{8,9},{9,8},{10,11... | collective-permute-start | bytes 1179656 | tf_op jit(solution)/shard_map/ppermute | solution.py:176
  24.7 1.7 %collective-permute-start.5 = (bf16[192,1024]{1,0:T(8,128)(2,1)S(1)}, bf16[192,1024]{1,0:T(8,128)(2,1)S(1)}, u32[]{:S(2)}, u32[]{:S(2)}) collective-permute-start(bf16[192,1024]{1,0:T(8,128)(2,1)S(1)} %collective-permute-done.3.refs_1_), channel_id=1, source_target_pairs={{0,1},{1,0},{2,3},{3,2},{4,5},{5,4},{6,7},{7,6},{8,9},{9,8},{10,11... | collective-permute-start | bytes 1179656 | tf_op jit(solution)/shard_map/ppermute | solution.py:176
  29.8 1.3 %collective-permute-start.6 = (f32[48,128]{1,0:T(8,128)S(1)}, f32[48,128]{1,0:T(8,128)S(1)}, u32[]{:S(2)}, u32[]{:S(2)}) collective-permute-start(f32[48,128]{1,0:T(8,128)S(1)} %shard_map.66), channel_id=1, source_target_pairs={{0,1},{1,0},{2,3},{3,2},{4,5},{5,4},{6,7},{7,6},{8,9},{9,8},{10,11... | collective-permute-start | bytes 73736 | tf_op jit(solution)/shard_map/ppermute | solution.py:176
  31.1 8.3 %collective-permute-start.9 = (f32[48,128]{1,0:T(8,128)S(1)}, f32[48,128]{1,0:T(8,128)S(1)}, u32[]{:S(2)}, u32[]{:S(2)}) collective-permute-start(f32[48,128]{1,0:T(8,128)S(1)} %add.64), channel_id=1, source_target_pairs={{0,6},{1,7},{2,4},{3,5},{4,2},{5,3},{6,0},{7,1},{8,14},{9,15},{10,... | collective-permute-start | bytes 73736 | tf_op jit(solution)/shard_map/ppermute | solution.py:176
  33.1 6.3 %collective-permute-start.8 = (f32[48,128]{1,0:T(8,128)S(1)}, f32[48,128]{1,0:T(8,128)S(1)}, u32[]{:S(2)}, u32[]{:S(2)}) collective-permute-start(f32[48,128]{1,0:T(8,128)S(1)} %add.64), channel_id=1, source_target_pairs={{0,4},{1,5},{2,6},{3,7},{4,0},{5,1},{6,2},{7,3},{8,12},{9,13},{10,... | collective-permute-start | bytes 73736 | tf_op jit(solution)/shard_map/ppermute | solution.py:176
  34.0 5.3 %collective-permute-start.7 = (f32[48,128]{1,0:T(8,128)S(1)}, f32[48,128]{1,0:T(8,128)S(1)}, u32[]{:S(2)}, u32[]{:S(2)}) collective-permute-start(f32[48,128]{1,0:T(8,128)S(1)} %add.64), channel_id=1, source_target_pairs={{0,2},{1,3},{2,0},{3,1},{4,6},{5,7},{6,4},{7,5},{8,10},{9,11},{10,... | collective-permute-start | bytes 73736 | tf_op jit(solution)/shard_map/ppermute | solution.py:176
  39.4 6.6 %collective-permute-start.10 = (f32[48,128]{1,0:T(8,128)S(1)}, f32[48,128]{1,0:T(8,128)S(1)}, u32[]{:S(2)}, u32[]{:S(2)}) collective-permute-start(f32[48,128]{1,0:T(8,128)S(1)} %add_add_fusion), channel_id=1, source_target_pairs={{0,8},{1,9},{2,10},{3,11},{4,12},{5,13},{6,14},{7,15},{8,0},{9,1},... | collective-permute-start | bytes 73736 | tf_op jit(solution)/shard_map/ppermute | solution.py:176

commit v3 on v2

v3 whole, which is shorter than its diff:
```python
import functools

import jax
import jax.numpy as jnp
from jax import lax
from jax.experimental import pallas as pl
from jax.experimental.pallas import tpu as pltpu
from jax.sharding import PartitionSpec as P

VMEM, SMEM, ANY = pltpu.VMEM, pltpu.SMEM, pl.ANY
GROUP = 8
FETCHED = (0, 5, 10, 13)
LANES = 128


def list_adapters(me, table_ref, sizes_ref, seen, listed, adapter_rows, rank_rows, place):
    steps, owners = table_ref.shape
    rows, lanes = adapter_rows.shape
    for i in range(seen.shape[0]):
        seen[i] = jnp.int32(0)
    for i in range(listed.shape[0]):
        listed[i] = jnp.int32(-1)
    count = jnp.int32(0)
    for b in range(rows):
        adapter = table_ref[b % steps, b // steps]
        new = jnp.int32(1) - seen[adapter]
        seen[adapter] = jnp.int32(1)
        listed[count] = adapter
        count = count + new
        distance = jnp.bitwise_xor(me, jnp.int32(b // steps))
        part = (distance & 1) * 2 + ((distance >> 1) & 1)
        across = (distance >> 2) + jnp.where(distance < 4, 0, jnp.where(distance < 8, 2, -1))
        spot = (part * (owners // 4) + across) * rows + (b % steps) * owners + me
        adapter_rows[b : b + 1, :] = jnp.full((1, lanes), adapter, jnp.int32)
        rank_rows[b : b + 1, :] = jnp.full((1, lanes), sizes_ref[adapter], jnp.int32)
        place[b : b + 1, :] = jnp.full((1, lanes), spot, jnp.int32)
    listed[count] = jnp.int32(-1)
    listed[rows + 1] = count


def padded(count):
    return (count + GROUP - 1) // GROUP * GROUP


def start_slices(listed, weight_ref, held, sem):
    def one(slot, carry):
        adapter = jnp.maximum(listed[slot], 0)
        pltpu.make_async_copy(weight_ref.at[adapter], held.at[slot], sem).start()
        return carry

    lax.fori_loop(0, padded(listed[held.shape[0] + 1]), one, 0)


def wait_slices(listed, weight_ref, held, sem):
    def one(slot, carry):
        pltpu.make_async_copy(weight_ref.at[0], held.at[slot], sem).wait()
        return carry

    lax.fori_loop(0, padded(listed[held.shape[0] + 1]), one, 0)


def fetch_rows(first, weight_ref, held, sem):
    return pltpu.make_async_copy(weight_ref.at[pl.ds(first, held.shape[0])], held, sem)


def fetch_and_list_kernel(
    first, me_ref, table_ref, sizes_ref, weight_ref, held, listed, adapter_rows, rank_rows, place, seen, sem
):
    copy = fetch_rows(first, weight_ref, held, sem)
    copy.start()
    list_adapters(me_ref[0], table_ref, sizes_ref, seen, listed, adapter_rows, rank_rows, place)
    copy.wait()


def fetch_both_kernel(first, listed, weight_ref, slices_ref, held, slices, sem, slice_sem):
    start_slices(listed, slices_ref, slices, slice_sem)
    copy = fetch_rows(first, weight_ref, held, sem)
    copy.start()
    wait_slices(listed, slices_ref, slices, slice_sem)
    copy.wait()


def down_kernel(first_row, listed, place_ref, adapter_rows_ref, *refs):
    *parts, slices, weight_ref, out_ref, held, sem = refs
    copy = fetch_rows(first_row, weight_ref, held, sem)
    copy.start()
    rows, width = out_ref.shape
    place = place_ref[...][:, :1]
    mine = jnp.zeros((rows, slices.shape[1]), jnp.float32)
    first = 0
    for part in parts:
        chosen = lax.broadcasted_iota(jnp.int32, (rows, part.shape[0]), 1) + first == place
        chosen = jnp.where(chosen, jnp.float32(1.0), jnp.float32(0.0)).astype(jnp.bfloat16)
        mine += jnp.dot(chosen, part[...], preferred_element_type=jnp.float32)
        first += part.shape[0]
    mine = mine.astype(jnp.bfloat16)
    adapter_rows = adapter_rows_ref[...]

    def one(group, total):
        for pair in range(0, GROUP, 2):
            slot = group * GROUP + pair
            both = jnp.concatenate([slices[slot], slices[slot + 1]], axis=1)
            product = jnp.dot(mine, both, preferred_element_type=jnp.float32)
            total = jnp.where(adapter_rows == listed[slot], product[:, :width], total)
            total = jnp.where(adapter_rows == listed[slot + 1], product[:, width:], total)
        return total

    zeros = jnp.zeros((rows, width), jnp.float32)
    out_ref[...] = lax.fori_loop(0, padded(listed[rows + 1]) // GROUP, one, zeros)
    copy.wait()


def first_base_kernel(order, me_ref, listed, *refs):
    parts = refs[: len(order)]
    weight, slices_ref, lhs_ref, out_ref, slices, wide, slice_sem = refs[len(order) :]
    start_slices(listed, slices_ref, slices, slice_sem)
    rest, rows, depth = lhs_ref.shape
    chunks = rest + weight.shape[0] // depth
    block = rows // chunks * chunks
    me = me_ref[0]
    for part, owners in zip(parts, order, strict=True):
        for place, distance in enumerate(owners):
            owner = jnp.bitwise_xor(me, distance)
            at = pl.ds(pl.multiple_of(owner * block, block), block)
            for tile in range(depth // LANES):
                piece = part[place * block : (place + 1) * block, tile * LANES : (tile + 1) * LANES]
                wide[tile, at, :] = piece.astype(jnp.float32)

    def whole(chunk):
        pieces = [wide[tile, pl.ds(chunk, rows, stride=chunks), :] for tile in range(depth // LANES)]
        return jnp.concatenate(pieces, axis=1).astype(jnp.bfloat16)

    total = jnp.zeros(out_ref.shape, jnp.float32)
    here = weight.shape[0] // depth
    for chunk in range(here):
        matrix = weight[chunk * depth : (chunk + 1) * depth, :]
        total += jnp.dot(whole(chunk), matrix, preferred_element_type=jnp.float32)
        for other in range(here + chunk, chunks, here):
            lhs_ref[other - here] = whole(other)
    out_ref[...] = total
    wait_slices(listed, slices_ref, slices, slice_sem)


def rest_base_kernel(lhs_ref, base_ref, *refs):
    *weights, rest_ref, out_ref, rest, sems = refs
    chunks, rows, depth = lhs_ref.shape
    streamed = rest.shape[0]
    start = rest_ref.shape[0] - streamed * depth
    copies = []
    for i in range(streamed):
        there = rest_ref.at[pl.ds(start + i * depth, depth)]
        copies.append(pltpu.make_async_copy(there, rest.at[i], sems.at[i]))
        copies[i].start()
    total = base_ref[...]
    chunk = 0
    for weight in weights:
        for first in range(0, weight.shape[0], depth):
            matrix = weight[first : first + depth, :]
            total += jnp.dot(lhs_ref[chunk], matrix, preferred_element_type=jnp.float32)
            chunk += 1
    for i in range(streamed):
        copies[i].wait()
        total += jnp.dot(lhs_ref[chunk + i], rest[i], preferred_element_type=jnp.float32)
    out_ref[...] = total


def up_kernel(listed, adapter_rows_ref, rank_rows_ref, hidden_ref, base_ref, slices, out_ref):
    rows, width = hidden_ref.shape
    rank_rows = rank_rows_ref[...]
    keep = lax.broadcasted_iota(jnp.int32, rank_rows.shape, 1) < rank_rows
    factor = 0.25 * width / rank_rows.astype(jnp.float32)
    lowrank = jnp.where(keep, hidden_ref[...] * factor, jnp.float32(0.0))
    adapter_rows = adapter_rows_ref[...]

    def one(group, total):
        slot = group * GROUP
        own = [jnp.where(adapter_rows == listed[slot + i], lowrank, jnp.float32(0.0)) for i in range(GROUP)]
        own = jnp.concatenate(own, axis=1).astype(jnp.bfloat16)
        matrix = jnp.concatenate([slices[slot + i] for i in range(GROUP)], axis=0)
        return total + jnp.dot(own, matrix, preferred_element_type=jnp.float32)

    total = lax.fori_loop(0, padded(listed[rows + 1]) // GROUP, one, base_ref[...])
    total = total.astype(jnp.bfloat16)
    steps = out_ref.shape[1]
    for owner in range(out_ref.shape[0]):
        out_ref[owner] = total[owner * steps : (owner + 1) * steps, :]


def exchange(value, distance, ranks):
    return lax.ppermute(value, "feat", [(i, i ^ distance) for i in range(ranks)])


def spec(space, count=1):
    return [pl.BlockSpec(memory_space=space)] * count


def cost(flops, size):
    return pl.CostEstimate(flops=flops, bytes_accessed=size, transcendentals=0)


def held_here(value):
    return pltpu.with_memory_space_constraint(value, VMEM)


def left_there(value):
    return pltpu.with_memory_space_constraint(value, pltpu.HBM)


def fast(tokens, query_weight, adapter_down_weight, adapter_up_weight, adapter_index_table, adapter_rank_sizes):
    steps, _, features = tokens.shape
    ranks = adapter_index_table.shape[1]
    columns = query_weight.shape[1]
    adapters, depth, width = adapter_down_weight.shape
    rows = steps * ranks
    bf16, f32 = jnp.bfloat16, jnp.float32
    swap = functools.partial(exchange, ranks=ranks)
    shape = jax.ShapeDtypeStruct
    params = pltpu.CompilerParams(vmem_limit_bytes=5 << 20)
    flops = 2 * rows * features * columns

    me = lax.axis_index("feat").astype(jnp.int32).reshape(1)
    chunk = features // ranks
    at = [chunk * count for count in FETCHED]

    def piece(i):
        return VMEM((at[i + 1] - at[i], columns), bf16)

    held_0, listed, adapter_rows, rank_rows, place = pl.pallas_call(
        functools.partial(fetch_and_list_kernel, at[0]),
        out_shape=(piece(0), shape((rows + 2,), jnp.int32)) + (shape((rows, width), jnp.int32),) * 3,
        in_specs=spec(SMEM, 3) + spec(ANY),
        out_specs=spec(VMEM) + spec(SMEM) + spec(VMEM, 3),
        scratch_shapes=[SMEM((adapters,), jnp.int32), pltpu.SemaphoreType.DMA],
        compiler_params=params,
        cost_estimate=cost(0, (at[1] - at[0]) * columns * 2),
    )(me, left_there(adapter_index_table), left_there(adapter_rank_sizes), left_there(query_weight))
    own = tokens.reshape(steps * ranks, chunk)
    across = (swap(own, 2), swap(own, 4), swap(own, 12), swap(own, 8))
    across, held_0, listed = lax.optimization_barrier((across, held_0, listed))
    own_y = across[0]
    near = jnp.concatenate(across[:0:-1], axis=0)
    held_1, down_slices = pl.pallas_call(
        functools.partial(fetch_both_kernel, at[1]),
        out_shape=(piece(1), VMEM((rows, depth, width), bf16)),
        in_specs=spec(SMEM) + spec(ANY, 2),
        out_specs=spec(VMEM, 2),
        scratch_shapes=[pltpu.SemaphoreType.DMA, pltpu.SemaphoreType.DMA],
        compiler_params=params,
        cost_estimate=cost(0, (at[2] - at[1]) * columns * 2 + rows * depth * width * 2),
    )(listed, left_there(query_weight), left_there(adapter_down_weight))
    far = swap(near, 2)
    far, held_1, down_slices = lax.optimization_barrier((far, held_1, down_slices))
    parts = (own, near, own_y, far)
    parts = parts + tuple(swap(part, 1) for part in parts)
    order = ((0,), (8, 12, 4), (2,), (10, 14, 6))
    order = order + tuple(tuple(i ^ 1 for i in owners) for owners in order)

    hidden, held_2 = pl.pallas_call(
        functools.partial(down_kernel, at[2]),
        out_shape=(shape((rows, width), f32), piece(2)),
        in_specs=spec(SMEM) + spec(VMEM, 2 + len(parts) + 1) + spec(ANY),
        out_specs=spec(VMEM, 2),
        scratch_shapes=[pltpu.SemaphoreType.DMA],
        compiler_params=params,
        cost_estimate=cost(2 * rows * depth * width * rows, 1 << 20),
    )(listed, place, adapter_rows, *parts, held_here(down_slices), left_there(query_weight))

    lhs, base, up_slices = pl.pallas_call(
        functools.partial(first_base_kernel, order),
        out_shape=(
            shape((ranks - FETCHED[1], rows, chunk), bf16),
            shape((rows, columns), f32),
            VMEM((rows, width, columns), bf16),
        ),
        in_specs=spec(SMEM, 2) + spec(VMEM, len(parts) + 1) + spec(ANY),
        out_specs=spec(VMEM, 3),
        scratch_shapes=[
            VMEM((depth // LANES, rows * ranks, LANES), f32),
            pltpu.SemaphoreType.DMA,
        ],
        compiler_params=params,
        cost_estimate=cost(flops // 2, 16 << 20),
    )(me, listed, *parts, held_here(held_0), left_there(adapter_up_weight))

    hidden = hidden + swap(hidden, 1)
    three = (swap(hidden, 2), swap(hidden, 4), swap(hidden, 6))
    three, lhs, base, up_slices = lax.optimization_barrier((three, lhs, base, up_slices))
    hidden = hidden + three[0] + three[1] + three[2]

    base = pl.pallas_call(
        rest_base_kernel,
        out_shape=shape((rows, columns), f32),
        in_specs=spec(VMEM, 4) + spec(ANY),
        out_specs=spec(VMEM)[0],
        scratch_shapes=[
            VMEM((ranks - FETCHED[-1], chunk, columns), bf16),
            pltpu.SemaphoreType.DMA((ranks - FETCHED[-1],)),
        ],
        compiler_params=pltpu.CompilerParams(vmem_limit_bytes=(2 * (ranks - FETCHED[-1]) + 3) << 20),
        cost_estimate=cost(flops // 2, 10 << 20),
    )(lhs, base, held_here(held_1), held_here(held_2), left_there(query_weight))
    last, base = lax.optimization_barrier((swap(hidden, 8), base))
    hidden = hidden + last

    out = pl.pallas_call(
        up_kernel,
        out_shape=shape((ranks, steps, columns), bf16),
        in_specs=spec(SMEM) + spec(VMEM, 5),
        out_specs=spec(VMEM)[0],
        compiler_params=params,
        cost_estimate=cost(2 * rows * width * columns * rows, 1 << 20),
    )(listed, adapter_rows, rank_rows, hidden, base, held_here(up_slices))

    gathered = lax.all_to_all(out, "feat", split_axis=0, concat_axis=0, tiled=True)
    return gathered.transpose(1, 0, 2).reshape(steps, 1, features)


def plain(tokens, query_weight, adapter_down_weight, adapter_up_weight, adapter_index_table, adapter_rank_sizes):
    width = query_weight.shape[1]
    rank_width = adapter_down_weight.shape[2]
    depth = adapter_down_weight.shape[1]
    whole = lax.all_gather(tokens, "feat", axis=1, tiled=True)
    piece = lax.dynamic_slice_in_dim(whole, lax.axis_index("feat") * depth, depth, 2)
    matrices = adapter_down_weight[adapter_index_table]
    partial = jnp.einsum("xun,xune->xue", piece, matrices, preferred_element_type=jnp.float32)
    hidden = lax.psum(partial, "feat")
    rank_rows = adapter_rank_sizes[adapter_index_table]
    keep = jnp.arange(rank_width)[None, None, :] < rank_rows[:, :, None]
    factor = 0.25 * rank_width / rank_rows.astype(jnp.float32)
    lowrank = jnp.where(keep, hidden * factor[:, :, None], jnp.float32(0.0)).astype(jnp.bfloat16)
    matrices = adapter_up_weight[adapter_index_table]
    update = jnp.einsum("jma,jmap->jmp", lowrank, matrices, preferred_element_type=jnp.float32)
    base = jnp.einsum("sbd,dc->sbc", whole, query_weight, preferred_element_type=jnp.float32)
    out = (base + update).astype(jnp.bfloat16)
    return lax.all_to_all(out, "feat", split_axis=1, concat_axis=2, tiled=True)


def on_device(tokens, query_weight, *rest):
    ranks = rest[2].shape[1]
    fits = ranks == 16 and query_weight.shape[1] % 256 == 0
    return (fast if fits else plain)(tokens, query_weight, *rest)


def solution(mesh):
    in_specs = (
        P(None, ("rep", "feat"), None),
        P(None, "feat"),
        P(None, "feat", None),
        P(None, None, "feat"),
        P(None, "rep"),
        P(),
    )
    out_specs = P(None, ("rep", "feat"), None)
    return jax.shard_map(
        on_device, mesh=mesh, in_specs=in_specs, out_specs=out_specs, check_vma=False
    )
```

time: 62.1 us -> 60.2 us (0.969)
  starting transfers between devices: 13.1 us -> 17.2 us
  waiting for transfers between devices: 4.64 us -> 1.86 us
  blocking collectives: 11.8 us -> 10.5 us
  local copies, waits for them, and re-layouts: 2.79 us -> 1.73 us
  other arithmetic: 0.88 us -> 0.02 us
    ppermute x11 -> x14, starting transfers between devices: 13.1 us -> 17.2 us  [exchange(): lax.ppermute(value, 'feat', [(i, i ^ distance) for i in range(ranks)])]
    ppermute x11 -> x14, waiting for transfers between devices: 4.64 us -> 1.86 us  [exchange(): lax.ppermute(value, 'feat', [(i, i ^ distance) for i in range(ranks)])]
    all_to_all x1, blocking collectives: 11.8 us -> 10.5 us  [fast(): lax.all_to_all(out, 'feat', split_axis=0, concat_axis=0, tiled=True)]
    reduce_sum x1 -> x0, other arithmetic: 0.83 us -> none  [fast(): jnp.sum(jnp.where(matches, adapter_rank_sizes[None, :], 0), axis=1, keepd...]
    pallas_call x3, Pallas kernels: 15.7 us -> 16.5 us  [the longest x1 7.7 us: fast(): pl.pallas_call(functools.partial(fetch_both_kernel, at[1]), out_shape=(pi...]
    transpose x1 -> x0, local copies, waits for them, and re-layouts: 0.76 us -> none  [fast(): adapter_index_table.T.reshape(rows, 1)]
  transfers between devices with their start and end apart: 11 -> 14, of which waited for: 5 -> 3; matrix products, arithmetic and copies ran while one was open for 3% -> 0% of each run, Pallas kernels for 35% -> 36%
where the time goes in v3:
time: 60.2 us; the launch traced here: 59.8 us
  Pallas kernels  28.3 us (47%)
  starting transfers between devices  17.2 us (29%)
  blocking collectives  10.5 us (17%)
  waiting for transfers between devices  1.86 us (3%)
  local copies, waits for them, and re-layouts  1.73 us (3%)
    ppermute x14, starting transfers between devices, exchange(): lax.ppermute(value, 'feat', [(i, i ^ distance) for i in range(ranks)])  17.2 us
    all_to_all x1, blocking collectives, fast(): lax.all_to_all(out, 'feat', split_axis=0, concat_axis=0, tiled=True)  10.5 us
    pallas_call x1, Pallas kernels, fast(): pl.pallas_call(functools.partial(fetch_both_kernel, at[1]), out_shape=(pi...  7.7 us
    pallas_call x1, Pallas kernels, fast(): pl.pallas_call(functools.partial(fetch_and_list_kernel, at[0]), out_shape...  5.28 us
    pallas_call x1, Pallas kernels, fast(): pl.pallas_call(functools.partial(first_base_kernel, order), out_shape=(sh...  4.56 us
    pallas_call x1, Pallas kernels, fast(): pl.pallas_call(rest_base_kernel, out_shape=shape((rows, columns), f32), i...  4.15 us
    pallas_call x1, Pallas kernels, fast(): pl.pallas_call(functools.partial(down_kernel, at[2]), out_shape=(shape((r...  3.56 us
    pallas_call x1, Pallas kernels, fast(): pl.pallas_call(up_kernel, out_shape=shape((ranks, steps, columns), bf16),...  3.04 us
  transfers between devices with their start and end apart: 14, of which 3 were waited for; matrix products, arithmetic and copies ran while one was open for 0% of the time, Pallas kernels for 36%

profile of v3, /device:TPU:0, one launch (start us, length us, event | category | flops | bytes accessed | tf_op | source)
XLA Modules:
  0.0 59.8 jit_solution(4540394503350430569)
XLA Ops:
  0.0 1.0 %reshape.9.refs_0_ = bf16[48,1024]{1,0:T(8,128)(2,1)S(1)} reshape(bf16[3,1,16384]{2,0,1:T(4,128)(2,1)} %param.6) | data formatting | bytes 196608 | tf_op jit(solution)/shard_map/reshape | solution.py:237
  1.0 4.1 %collective-permute-start.3 = (bf16[48,1024]{1,0:T(8,128)(2,1)S(1)}, bf16[48,1024]{1,0:T(8,128)(2,1)S(1)}, u32[]{:S(2)}, u32[]{:S(2)}) collective-permute-start(bf16[48,1024]{1,0:T(8,128)(2,1)S(1)} %reshape.9.refs_0_), channel_id=1, source_target_pairs={{0,8},{1,9},{2,10},{3,11},{4,12},{5,13},{6,14},{7,15},{8,0},{9,1},... | collective-permute-start | bytes 294920 | tf_op jit(solution)/shard_map/ppermute | solution.py:190
  5.1 1.3 %collective-permute-start.2 = (bf16[48,1024]{1,0:T(8,128)(2,1)S(1)}, bf16[48,1024]{1,0:T(8,128)(2,1)S(1)}, u32[]{:S(2)}, u32[]{:S(2)}) collective-permute-start(bf16[48,1024]{1,0:T(8,128)(2,1)S(1)} %reshape.9.refs_0_), channel_id=1, source_target_pairs={{0,12},{1,13},{2,14},{3,15},{4,8},{5,9},{6,10},{7,11},{8,4},{9,5},... | collective-permute-start | bytes 294920 | tf_op jit(solution)/shard_map/ppermute | solution.py:190
  6.5 0.2 collective-permute-start.1
  6.7 1.5 %collective-permute-start = (bf16[48,1024]{1,0:T(8,128)(2,1)S(1)}, bf16[48,1024]{1,0:T(8,128)(2,1)S(1)}, u32[]{:S(2)}, u32[]{:S(2)}) collective-permute-start(bf16[48,1024]{1,0:T(8,128)(2,1)S(1)} %reshape.9.refs_0_), channel_id=1, source_target_pairs={{0,2},{1,3},{2,0},{3,1},{4,6},{5,7},{6,4},{7,5},{8,10},{9,11},{10,... | collective-permute-start | bytes 294920 | tf_op jit(solution)/shard_map/ppermute | solution.py:190
  8.2 5.3 %shard_map.64 = (bf16[5120,1024]{1,0:T(8,128)(2,1)S(1)}, s32[50]{0:T(128)S(1)}, s32[48,128]{1,0:T(8,128)S(1)}, s32[48,128]{1,0:T(8,128)S(1)}, s32[48,128]{1,0:T(8,128)S(1)}) custom-call(s32[1]{0:T(128)} %bitcast.me_ref, s32[3,16]{1,0:T(4,128)} %table_ref.1, s32[64]{0:T(128)} %sizes_ref.1, bf16[16384,1024]{1,0:T(8,128)(2,1)} %refs_2_.1), custom_call_target="tpu_custom_call" | custom-call | bytes 10485760 | tf_op jit(solution)/shard_map/pallas_call | solution.py:228
  13.5 0.0 collective-permute-done.3
  13.5 0.0 collective-permute-done.2
  13.6 0.0 collective-permute-done.1
  13.6 0.0 collective-permute-done.refs_2_
  13.6 1.6 %collective-permute-start.4 = (bf16[144,1024]{1,0:T(8,128)(2,1)S(1)}, bf16[144,1024]{1,0:T(8,128)(2,1)S(1)}, u32[]{:S(2)}, u32[]{:S(2)}) collective-permute-start(bf16[144,1024]{1,0:T(8,128)(2,1)S(1)} %constant_dynamic-update-slice_fusion.refs_1_), channel_id=1, source_target_pairs={{0,2},{1,3},{2,0},{3,1},{4,6},{5,7},{6,4},{7,5},{8,10},{9,11},{10,... | collective-permute-start | bytes 884744 | tf_op jit(solution)/shard_map/ppermute | solution.py:190
  15.2 0.0 collective-permute-start.6
  15.2 7.7 %shard_map.65 = (bf16[5120,1024]{1,0:T(8,128)(2,1)S(1)}, bf16[48,1024,128]{2,1,0:T(8,128)(2,1)S(1)}) custom-call(s32[50]{0:T(128)S(1)} %get-tuple-element.36.listed, bf16[16384,1024]{1,0:T(8,128)(2,1)} %refs_2_.1, bf16[64,1024,128]{2,1,0:T(8,128)(2,1)} %slices_ref.1), custom_call_target="tpu_custom_call" | custom-call | bytes 23068672 | tf_op jit(solution)/shard_map/pallas_call | solution.py:242
  22.9 0.0 collective-permute-done.4.refs_3_
  23.0 0.6 collective-permute-start.8
  23.5 0.1 collective-permute-start.5
  23.6 0.4 collective-permute-start.7
  24.0 0.8 %collective-permute-done.5.refs_4_ = bf16[48,1024]{1,0:T(8,128)(2,1)S(1)} collective-permute-done((bf16[48,1024]{1,0:T(8,128)(2,1)S(1)}, bf16[48,1024]{1,0:T(8,128)(2,1)S(1)}, u32[]{:S(2)}, u32[]{:S(2)}) %collective-permute-start.5) | collective-permute-done | bytes 98336 | tf_op jit(solution)/shard_map/ppermute | solution.py:190
  24.9 0.1 collective-permute-done.7.refs_6_
  25.0 0.0 collective-permute-done.6.refs_5_
  25.0 0.0 collective-permute-done.8.refs_7_
  25.0 3.6 %shard_map.66 = (f32[48,128]{1,0:T(8,128)S(1)}, bf16[3072,1024]{1,0:T(8,128)(2,1)S(1)}) custom-call(s32[50]{0:T(128)S(1)} %get-tuple-element.36.listed, s32[48,128]{1,0:T(8,128)S(1)} %get-tuple-element.39.place_ref, s32[48,128]{1,0:T(8,128)S(1)} %get-tuple-element.37.adapter_rows_ref, bf16[48,1024]{1,0:T(8,128)(2,1)S(1)} %reshape.9.refs_0_, ...), custom_call_target="tpu_custom_call" | custom-call | flops 603979776 | bytes 1048576 | tf_op jit(solution)/shard_map/pallas_call | solution.py:258
  28.6 0.4 collective-permute-start.9
  29.0 0.8 %collective-permute-done.9 = f32[48,128]{1,0:T(8,128)S(1)} collective-permute-done((f32[48,128]{1,0:T(8,128)S(1)}, f32[48,128]{1,0:T(8,128)S(1)}, u32[]{:S(2)}, u32[]{:S(2)}) %collective-permute-start.9) | collective-permute-done | bytes 24608 | tf_op jit(solution)/shard_map/ppermute | solution.py:190
  29.9 1.9 %collective-permute-start.12 = (f32[48,128]{1,0:T(8,128)S(1)}, f32[48,128]{1,0:T(8,128)S(1)}, u32[]{:S(2)}, u32[]{:S(2)}) collective-permute-start(f32[48,128]{1,0:T(8,128)S(1)} %add.15), channel_id=1, source_target_pairs={{0,6},{1,7},{2,4},{3,5},{4,2},{5,3},{6,0},{7,1},{8,14},{9,15},{10,... | collective-permute-start | bytes 73736 | tf_op jit(solution)/shard_map/ppermute | solution.py:190
  31.7 0.1 collective-permute-start.11
  31.8 1.5 %collective-permute-start.10 = (f32[48,128]{1,0:T(8,128)S(1)}, f32[48,128]{1,0:T(8,128)S(1)}, u32[]{:S(2)}, u32[]{:S(2)}) collective-permute-start(f32[48,128]{1,0:T(8,128)S(1)} %add.15), channel_id=1, source_target_pairs={{0,2},{1,3},{2,0},{3,1},{4,6},{5,7},{6,4},{7,5},{8,10},{9,11},{10,... | collective-permute-start | bytes 73736 | tf_op jit(solution)/shard_map/ppermute | solution.py:190
  33.4 4.6 %shard_map.67 = (bf16[11,48,1024]{2,1,0:T(8,128)(2,1)S(1)}, f32[48,1024]{1,0:T(8,128)S(1)}, bf16[48,128,1024]{2,1,0:T(8,128)(2,1)S(1)}) custom-call(s32[1]{0:T(128)} %bitcast.me_ref, s32[50]{0:T(128)S(1)} %get-tuple-element.36.listed, bf16[48,1024]{1,0:T(8,128)(2,1)S(1)} %reshape.9.refs_0_, bf16[144,1024]{1,0:T(8,128)(2,1)S(1)} %constant_dynamic-update-slice_fusion.refs_1_, ...), custom_call_target="tpu_custom_call" | custom-call | flops 805306368 | bytes 16777216 | tf_op jit(solution)/shard_map/pallas_call | solution.py:268
  37.9 0.0 collective-permute-done.12
  38.0 0.0 collective-permute-done.11
  38.0 0.0 collective-permute-done.10
  38.0 3.4 %collective-permute-start.13 = (f32[48,128]{1,0:T(8,128)S(1)}, f32[48,128]{1,0:T(8,128)S(1)}, u32[]{:S(2)}, u32[]{:S(2)}) collective-permute-start(f32[48,128]{1,0:T(8,128)S(1)} %add_add_fusion), channel_id=1, source_target_pairs={{0,8},{1,9},{2,10},{3,11},{4,12},{5,13},{6,14},{7,15},{8,0},{9,1},... | collective-permute-start | bytes 73736 | tf_op jit(solution)/shard_map/ppermute | solution.py:190
  41.4 4.2 %shard_map.68.base_ref = f32[48,1024]{1,0:T(8,128)S(1)} custom-call(bf16[11,48,1024]{2,1,0:T(8,128)(2,1)S(1)} %get-tuple-element.56.lhs_ref, f32[48,1024]{1,0:T(8,128)S(1)} %get-tuple-element.57.base_ref, bf16[5120,1024]{1,0:T(8,128)(2,1)S(1)} %get-tuple-element.58.refs_0_, bf16[3072,1024]{1,0:T(8,128)(2,1)S(1)} %get-tuple-element.59.refs_1_, ...), custom_call_target="tpu_custom_call" | custom-call | flops 805306368 | bytes 10485760 | tf_op jit(solution)/shard_map/pallas_call | solution.py:290
  45.6 0.0 collective-permute-done.13
  45.6 3.0 %shard_map.69 = bf16[16,3,1024]{2,1,0:T(4,128)(2,1)S(1)} custom-call(s32[50]{0:T(128)S(1)} %get-tuple-element.36.listed, s32[48,128]{1,0:T(8,128)S(1)} %get-tuple-element.37.adapter_rows_ref, s32[48,128]{1,0:T(8,128)S(1)} %get-tuple-element.38.rank_rows_ref, f32[48,128]{1,0:T(8,128)S(1)} %add.19.hidden_ref, f32[48,1024]{1,0:T(8,128)S(1)} %shard_map.68.base_ref, ...), custom_call_target="tpu_custom_call" | custom-call | flops 603979776 | bytes 1048576 | tf_op jit(solution)/shard_map/pallas_call | solution.py:305
  48.6 10.5 %all_to_all.5 = bf16[16,3,1024]{2,1,0:T(4,128)(2,1)S(1)} all-to-all(bf16[16,3,1024]{2,1,0:T(4,128)(2,1)S(1)} %shard_map.69), channel_id=1, replica_groups=mesh['rep'=2,'feat'=16] {'feat'}, dimensions={0} | all-to-all | bytes 196608 | tf_op jit(solution)/shard_map/all_to_all | solution.py:314
  59.2 0.7 %copy.10 = bf16[3,1,16384]{2,0,1:T(4,128)(2,1)} copy(bf16[3,1,16384]{2,0,1:T(4,128)(2,1)S(1)} %bitcast.6) | data formatting | bytes 196608
  (6 shorter events, 0.0 us)
Async XLA Ops:
  1.0 12.5 %collective-permute-start.3 = (bf16[48,1024]{1,0:T(8,128)(2,1)S(1)}, bf16[48,1024]{1,0:T(8,128)(2,1)S(1)}, u32[]{:S(2)}, u32[]{:S(2)}) collective-permute-start(bf16[48,1024]{1,0:T(8,128)(2,1)S(1)} %reshape.9.refs_0_), channel_id=1, source_target_pairs={{0,8},{1,9},{2,10},{3,11},{4,12},{5,13},{6,14},{7,15},{8,0},{9,1},... | collective-permute-start | bytes 294920 | tf_op jit(solution)/shard_map/ppermute | solution.py:190
  5.1 8.4 %collective-permute-start.2 = (bf16[48,1024]{1,0:T(8,128)(2,1)S(1)}, bf16[48,1024]{1,0:T(8,128)(2,1)S(1)}, u32[]{:S(2)}, u32[]{:S(2)}) collective-permute-start(bf16[48,1024]{1,0:T(8,128)(2,1)S(1)} %reshape.9.refs_0_), channel_id=1, source_target_pairs={{0,12},{1,13},{2,14},{3,15},{4,8},{5,9},{6,10},{7,11},{8,4},{9,5},... | collective-permute-start | bytes 294920 | tf_op jit(solution)/shard_map/ppermute | solution.py:190
  6.5 7.1 %collective-permute-start.1 = (bf16[48,1024]{1,0:T(8,128)(2,1)S(1)}, bf16[48,1024]{1,0:T(8,128)(2,1)S(1)}, u32[]{:S(2)}, u32[]{:S(2)}) collective-permute-start(bf16[48,1024]{1,0:T(8,128)(2,1)S(1)} %reshape.9.refs_0_), channel_id=1, source_target_pairs={{0,4},{1,5},{2,6},{3,7},{4,0},{5,1},{6,2},{7,3},{8,12},{9,13},{10,... | collective-permute-start | bytes 294920 | tf_op jit(solution)/shard_map/ppermute | solution.py:190
  6.7 6.8 %collective-permute-start = (bf16[48,1024]{1,0:T(8,128)(2,1)S(1)}, bf16[48,1024]{1,0:T(8,128)(2,1)S(1)}, u32[]{:S(2)}, u32[]{:S(2)}) collective-permute-start(bf16[48,1024]{1,0:T(8,128)(2,1)S(1)} %reshape.9.refs_0_), channel_id=1, source_target_pairs={{0,2},{1,3},{2,0},{3,1},{4,6},{5,7},{6,4},{7,5},{8,10},{9,11},{10,... | collective-permute-start | bytes 294920 | tf_op jit(solution)/shard_map/ppermute | solution.py:190
  13.6 9.3 %collective-permute-start.4 = (bf16[144,1024]{1,0:T(8,128)(2,1)S(1)}, bf16[144,1024]{1,0:T(8,128)(2,1)S(1)}, u32[]{:S(2)}, u32[]{:S(2)}) collective-permute-start(bf16[144,1024]{1,0:T(8,128)(2,1)S(1)} %constant_dynamic-update-slice_fusion.refs_1_), channel_id=1, source_target_pairs={{0,2},{1,3},{2,0},{3,1},{4,6},{5,7},{6,4},{7,5},{8,10},{9,11},{10,... | collective-permute-start | bytes 884744 | tf_op jit(solution)/shard_map/ppermute | solution.py:190
  15.2 9.8 %collective-permute-start.6 = (bf16[144,1024]{1,0:T(8,128)(2,1)S(1)}, bf16[144,1024]{1,0:T(8,128)(2,1)S(1)}, u32[]{:S(2)}, u32[]{:S(2)}) collective-permute-start(bf16[144,1024]{1,0:T(8,128)(2,1)S(1)} %constant_dynamic-update-slice_fusion.refs_1_), channel_id=1, source_target_pairs={{0,1},{1,0},{2,3},{3,2},{4,5},{5,4},{6,7},{7,6},{8,9},{9,8},{10,11... | collective-permute-start | bytes 884744 | tf_op jit(solution)/shard_map/ppermute | solution.py:190
  23.0 2.1 %collective-permute-start.8 = (bf16[144,1024]{1,0:T(8,128)(2,1)S(1)}, bf16[144,1024]{1,0:T(8,128)(2,1)S(1)}, u32[]{:S(2)}, u32[]{:S(2)}) collective-permute-start(bf16[144,1024]{1,0:T(8,128)(2,1)S(1)} %collective-permute-done.4.refs_3_), channel_id=1, source_target_pairs={{0,1},{1,0},{2,3},{3,2},{4,5},{5,4},{6,7},{7,6},{8,9},{9,8},{10,11... | collective-permute-start | bytes 884744 | tf_op jit(solution)/shard_map/ppermute | solution.py:190
  23.5 1.3 %collective-permute-start.5 = (bf16[48,1024]{1,0:T(8,128)(2,1)S(1)}, bf16[48,1024]{1,0:T(8,128)(2,1)S(1)}, u32[]{:S(2)}, u32[]{:S(2)}) collective-permute-start(bf16[48,1024]{1,0:T(8,128)(2,1)S(1)} %reshape.9.refs_0_), channel_id=1, source_target_pairs={{0,1},{1,0},{2,3},{3,2},{4,5},{5,4},{6,7},{7,6},{8,9},{9,8},{10,11... | collective-permute-start | bytes 294920 | tf_op jit(solution)/shard_map/ppermute | solution.py:190
  23.6 1.4 %collective-permute-start.7 = (bf16[48,1024]{1,0:T(8,128)(2,1)S(1)}, bf16[48,1024]{1,0:T(8,128)(2,1)S(1)}, u32[]{:S(2)}, u32[]{:S(2)}) collective-permute-start(bf16[48,1024]{1,0:T(8,128)(2,1)S(1)} %collective-permute-done.refs_2_), channel_id=1, source_target_pairs={{0,1},{1,0},{2,3},{3,2},{4,5},{5,4},{6,7},{7,6},{8,9},{9,8},{10,11... | collective-permute-start | bytes 294920 | tf_op jit(solution)/shard_map/ppermute | solution.py:190
  28.6 1.3 %collective-permute-start.9 = (f32[48,128]{1,0:T(8,128)S(1)}, f32[48,128]{1,0:T(8,128)S(1)}, u32[]{:S(2)}, u32[]{:S(2)}) collective-permute-start(f32[48,128]{1,0:T(8,128)S(1)} %get-tuple-element.48), channel_id=1, source_target_pairs={{0,1},{1,0},{2,3},{3,2},{4,5},{5,4},{6,7},{7,6},{8,9},{9,8},{10,11... | collective-permute-start | bytes 73736 | tf_op jit(solution)/shard_map/ppermute | solution.py:190
  29.9 8.1 %collective-permute-start.12 = (f32[48,128]{1,0:T(8,128)S(1)}, f32[48,128]{1,0:T(8,128)S(1)}, u32[]{:S(2)}, u32[]{:S(2)}) collective-permute-start(f32[48,128]{1,0:T(8,128)S(1)} %add.15), channel_id=1, source_target_pairs={{0,6},{1,7},{2,4},{3,5},{4,2},{5,3},{6,0},{7,1},{8,14},{9,15},{10,... | collective-permute-start | bytes 73736 | tf_op jit(solution)/shard_map/ppermute | solution.py:190
  31.7 6.2 %collective-permute-start.11 = (f32[48,128]{1,0:T(8,128)S(1)}, f32[48,128]{1,0:T(8,128)S(1)}, u32[]{:S(2)}, u32[]{:S(2)}) collective-permute-start(f32[48,128]{1,0:T(8,128)S(1)} %add.15), channel_id=1, source_target_pairs={{0,4},{1,5},{2,6},{3,7},{4,0},{5,1},{6,2},{7,3},{8,12},{9,13},{10,... | collective-permute-start | bytes 73736 | tf_op jit(solution)/shard_map/ppermute | solution.py:190
  31.8 6.1 %collective-permute-start.10 = (f32[48,128]{1,0:T(8,128)S(1)}, f32[48,128]{1,0:T(8,128)S(1)}, u32[]{:S(2)}, u32[]{:S(2)}) collective-permute-start(f32[48,128]{1,0:T(8,128)S(1)} %add.15), channel_id=1, source_target_pairs={{0,2},{1,3},{2,0},{3,1},{4,6},{5,7},{6,4},{7,5},{8,10},{9,11},{10,... | collective-permute-start | bytes 73736 | tf_op jit(solution)/shard_map/ppermute | solution.py:190
  38.0 7.6 %collective-permute-start.13 = (f32[48,128]{1,0:T(8,128)S(1)}, f32[48,128]{1,0:T(8,128)S(1)}, u32[]{:S(2)}, u32[]{:S(2)}) collective-permute-start(f32[48,128]{1,0:T(8,128)S(1)} %add_add_fusion), channel_id=1, source_target_pairs={{0,8},{1,9},{2,10},{3,11},{4,12},{5,13},{6,14},{7,15},{8,0},{9,1},... | collective-permute-start | bytes 73736 | tf_op jit(solution)/shard_map/ppermute | solution.py:190

commit v4 on v3

--- a/solution.py
+++ b/solution.py
@@ -9,7 +9,7 @@
 
 VMEM, SMEM, ANY = pltpu.VMEM, pltpu.SMEM, pl.ANY
 GROUP = 8
-FETCHED = (0, 5, 10, 13)
+FETCHED = (0, 7, 10, 13)
 LANES = 128
 
 

time: 60.2 us -> 59.7 us (level)
  starting transfers between devices: 17.2 us -> 15.2 us
  waiting for transfers between devices: 1.86 us -> 3.07 us
  blocking collectives: 10.5 us -> 11.2 us
    ppermute x14, starting transfers between devices: 17.2 us -> 15.2 us  [exchange(): lax.ppermute(value, 'feat', [(i, i ^ distance) for i in range(ranks)])]
    ppermute x14, waiting for transfers between devices: 1.86 us -> 3.07 us  [exchange(): lax.ppermute(value, 'feat', [(i, i ^ distance) for i in range(ranks)])]
    pallas_call x1, Pallas kernels: 5.28 us -> 6.47 us  [fast(): pl.pallas_call(functools.partial(fetch_and_list_kernel, at[0]), out_shape...]
    pallas_call x1, Pallas kernels: 7.7 us -> 6.76 us  [fast(): pl.pallas_call(functools.partial(fetch_both_kernel, at[1]), out_shape=(pi...]
    all_to_all x1, blocking collectives: 10.5 us -> 11.2 us  [fast(): lax.all_to_all(out, 'feat', split_axis=0, concat_axis=0, tiled=True)]
  transfers between devices with their start and end apart: 14 -> 14, of which waited for: 3 -> 4; matrix products, arithmetic and copies ran while one was open for 0% -> 0% of each run, Pallas kernels for 36% -> 36%
where the time goes in v4:
time: 59.7 us; the launch traced here: 59.5 us
  Pallas kernels  28.1 us (47%)
  starting transfers between devices  15.2 us (25%)
  blocking collectives  11.2 us (19%)
  waiting for transfers between devices  3.07 us (5%)
  local copies, waits for them, and re-layouts  1.73 us (3%)
    ppermute x14, starting transfers between devices, exchange(): lax.ppermute(value, 'feat', [(i, i ^ distance) for i in range(ranks)])  15.2 us
    all_to_all x1, blocking collectives, fast(): lax.all_to_all(out, 'feat', split_axis=0, concat_axis=0, tiled=True)  11.2 us
    pallas_call x1, Pallas kernels, fast(): pl.pallas_call(functools.partial(fetch_both_kernel, at[1]), out_shape=(pi...  6.76 us
    pallas_call x1, Pallas kernels, fast(): pl.pallas_call(functools.partial(fetch_and_list_kernel, at[0]), out_shape...  6.47 us
    pallas_call x1, Pallas kernels, fast(): pl.pallas_call(functools.partial(first_base_kernel, order), out_shape=(sh...  4.63 us
    pallas_call x1, Pallas kernels, fast(): pl.pallas_call(rest_base_kernel, out_shape=shape((rows, columns), f32), i...  3.6 us
    pallas_call x1, Pallas kernels, fast(): pl.pallas_call(functools.partial(down_kernel, at[2]), out_shape=(shape((r...  3.57 us
    pallas_call x1, Pallas kernels, fast(): pl.pallas_call(up_kernel, out_shape=shape((ranks, steps, columns), bf16),...  3.07 us
  transfers between devices with their start and end apart: 14, of which 4 were waited for; matrix products, arithmetic and copies ran while one was open for 0% of the time, Pallas kernels for 36%

profile of v4, /device:TPU:0, one launch (start us, length us, event | category | flops | bytes accessed | tf_op | source)
XLA Modules:
  0.0 59.5 jit_solution(13634640004346255329)
XLA Ops:
  0.0 1.0 %reshape.9.refs_0_ = bf16[48,1024]{1,0:T(8,128)(2,1)S(1)} reshape(bf16[3,1,16384]{2,0,1:T(4,128)(2,1)} %param.6) | data formatting | bytes 196608 | tf_op jit(solution)/shard_map/reshape | solution.py:237
  1.0 4.1 %collective-permute-start.3 = (bf16[48,1024]{1,0:T(8,128)(2,1)S(1)}, bf16[48,1024]{1,0:T(8,128)(2,1)S(1)}, u32[]{:S(2)}, u32[]{:S(2)}) collective-permute-start(bf16[48,1024]{1,0:T(8,128)(2,1)S(1)} %reshape.9.refs_0_), channel_id=1, source_target_pairs={{0,8},{1,9},{2,10},{3,11},{4,12},{5,13},{6,14},{7,15},{8,0},{9,1},... | collective-permute-start | bytes 294920 | tf_op jit(solution)/shard_map/ppermute | solution.py:190
  5.1 1.3 %collective-permute-start.2 = (bf16[48,1024]{1,0:T(8,128)(2,1)S(1)}, bf16[48,1024]{1,0:T(8,128)(2,1)S(1)}, u32[]{:S(2)}, u32[]{:S(2)}) collective-permute-start(bf16[48,1024]{1,0:T(8,128)(2,1)S(1)} %reshape.9.refs_0_), channel_id=1, source_target_pairs={{0,12},{1,13},{2,14},{3,15},{4,8},{5,9},{6,10},{7,11},{8,4},{9,5},... | collective-permute-start | bytes 294920 | tf_op jit(solution)/shard_map/ppermute | solution.py:190
  6.5 0.2 collective-permute-start.1
  6.7 1.5 %collective-permute-start = (bf16[48,1024]{1,0:T(8,128)(2,1)S(1)}, bf16[48,1024]{1,0:T(8,128)(2,1)S(1)}, u32[]{:S(2)}, u32[]{:S(2)}) collective-permute-start(bf16[48,1024]{1,0:T(8,128)(2,1)S(1)} %reshape.9.refs_0_), channel_id=1, source_target_pairs={{0,2},{1,3},{2,0},{3,1},{4,6},{5,7},{6,4},{7,5},{8,10},{9,11},{10,... | collective-permute-start | bytes 294920 | tf_op jit(solution)/shard_map/ppermute | solution.py:190
  8.2 6.5 %shard_map.64 = (bf16[7168,1024]{1,0:T(8,128)(2,1)S(1)}, s32[50]{0:T(128)S(1)}, s32[48,128]{1,0:T(8,128)S(1)}, s32[48,128]{1,0:T(8,128)S(1)}, s32[48,128]{1,0:T(8,128)S(1)}) custom-call(s32[1]{0:T(128)} %bitcast.me_ref, s32[3,16]{1,0:T(4,128)} %table_ref.1, s32[64]{0:T(128)} %sizes_ref.1, bf16[16384,1024]{1,0:T(8,128)(2,1)} %refs_2_.1), custom_call_target="tpu_custom_call" | custom-call | bytes 14680064 | tf_op jit(solution)/shard_map/pallas_call | solution.py:228
  14.7 0.0 collective-permute-done.3
  14.7 0.0 collective-permute-done.2
  14.7 0.0 collective-permute-done.1
  14.8 0.0 collective-permute-done.refs_2_
  14.8 0.6 collective-permute-start.4
  15.4 0.0 collective-permute-start.6
  15.4 6.8 %shard_map.65 = (bf16[3072,1024]{1,0:T(8,128)(2,1)S(1)}, bf16[48,1024,128]{2,1,0:T(8,128)(2,1)S(1)}) custom-call(s32[50]{0:T(128)S(1)} %get-tuple-element.36.listed, bf16[16384,1024]{1,0:T(8,128)(2,1)} %refs_2_.1, bf16[64,1024,128]{2,1,0:T(8,128)(2,1)} %slices_ref.1), custom_call_target="tpu_custom_call" | custom-call | bytes 18874368 | tf_op jit(solution)/shard_map/pallas_call | solution.py:242
  22.2 0.6 %collective-permute-done.4.refs_3_ = bf16[144,1024]{1,0:T(8,128)(2,1)S(1)} collective-permute-done((bf16[144,1024]{1,0:T(8,128)(2,1)S(1)}, bf16[144,1024]{1,0:T(8,128)(2,1)S(1)}, u32[]{:S(2)}, u32[]{:S(2)}) %collective-permute-start.4) | collective-permute-done | bytes 294944 | tf_op jit(solution)/shard_map/ppermute | solution.py:190
  22.8 0.0 collective-permute-start.8
  22.8 0.5 collective-permute-start.5
  23.3 0.0 collective-permute-start.7
  23.3 1.2 %collective-permute-done.5.refs_4_ = bf16[48,1024]{1,0:T(8,128)(2,1)S(1)} collective-permute-done((bf16[48,1024]{1,0:T(8,128)(2,1)S(1)}, bf16[48,1024]{1,0:T(8,128)(2,1)S(1)}, u32[]{:S(2)}, u32[]{:S(2)}) %collective-permute-start.5) | collective-permute-done | bytes 98336 | tf_op jit(solution)/shard_map/ppermute | solution.py:190
  24.5 0.1 collective-permute-done.7.refs_6_
  24.7 0.0 collective-permute-done.6.refs_5_
  24.7 0.0 collective-permute-done.8.refs_7_
  24.7 3.6 %shard_map.66 = (f32[48,128]{1,0:T(8,128)S(1)}, bf16[3072,1024]{1,0:T(8,128)(2,1)S(1)}) custom-call(s32[50]{0:T(128)S(1)} %get-tuple-element.36.listed, s32[48,128]{1,0:T(8,128)S(1)} %get-tuple-element.39.place_ref, s32[48,128]{1,0:T(8,128)S(1)} %get-tuple-element.37.adapter_rows_ref, bf16[48,1024]{1,0:T(8,128)(2,1)S(1)} %reshape.9.refs_0_, ...), custom_call_target="tpu_custom_call" | custom-call | flops 603979776 | bytes 1048576 | tf_op jit(solution)/shard_map/pallas_call | solution.py:258
  28.2 0.2 collective-permute-start.9
  28.4 1.1 %collective-permute-done.9 = f32[48,128]{1,0:T(8,128)S(1)} collective-permute-done((f32[48,128]{1,0:T(8,128)S(1)}, f32[48,128]{1,0:T(8,128)S(1)}, u32[]{:S(2)}, u32[]{:S(2)}) %collective-permute-start.9) | collective-permute-done | bytes 24608 | tf_op jit(solution)/shard_map/ppermute | solution.py:190
  29.5 2.4 %collective-permute-start.12 = (f32[48,128]{1,0:T(8,128)S(1)}, f32[48,128]{1,0:T(8,128)S(1)}, u32[]{:S(2)}, u32[]{:S(2)}) collective-permute-start(f32[48,128]{1,0:T(8,128)S(1)} %add.15), channel_id=1, source_target_pairs={{0,6},{1,7},{2,4},{3,5},{4,2},{5,3},{6,0},{7,1},{8,14},{9,15},{10,... | collective-permute-start | bytes 73736 | tf_op jit(solution)/shard_map/ppermute | solution.py:190
  31.9 0.2 collective-permute-start.11
  32.1 0.9 %collective-permute-start.10 = (f32[48,128]{1,0:T(8,128)S(1)}, f32[48,128]{1,0:T(8,128)S(1)}, u32[]{:S(2)}, u32[]{:S(2)}) collective-permute-start(f32[48,128]{1,0:T(8,128)S(1)} %add.15), channel_id=1, source_target_pairs={{0,2},{1,3},{2,0},{3,1},{4,6},{5,7},{6,4},{7,5},{8,10},{9,11},{10,... | collective-permute-start | bytes 73736 | tf_op jit(solution)/shard_map/ppermute | solution.py:190
  33.0 4.6 %shard_map.67 = (bf16[9,48,1024]{2,1,0:T(8,128)(2,1)S(1)}, f32[48,1024]{1,0:T(8,128)S(1)}, bf16[48,128,1024]{2,1,0:T(8,128)(2,1)S(1)}) custom-call(s32[1]{0:T(128)} %bitcast.me_ref, s32[50]{0:T(128)S(1)} %get-tuple-element.36.listed, bf16[48,1024]{1,0:T(8,128)(2,1)S(1)} %reshape.9.refs_0_, bf16[144,1024]{1,0:T(8,128)(2,1)S(1)} %constant_dynamic-update-slice_fusion.refs_1_, ...), custom_call_target="tpu_custom_call" | custom-call | flops 805306368 | bytes 16777216 | tf_op jit(solution)/shard_map/pallas_call | solution.py:268
  37.6 0.0 collective-permute-done.12
  37.6 0.0 collective-permute-done.11
  37.6 0.0 collective-permute-done.10
  37.7 3.3 %collective-permute-start.13 = (f32[48,128]{1,0:T(8,128)S(1)}, f32[48,128]{1,0:T(8,128)S(1)}, u32[]{:S(2)}, u32[]{:S(2)}) collective-permute-start(f32[48,128]{1,0:T(8,128)S(1)} %add_add_fusion), channel_id=1, source_target_pairs={{0,8},{1,9},{2,10},{3,11},{4,12},{5,13},{6,14},{7,15},{8,0},{9,1},... | collective-permute-start | bytes 73736 | tf_op jit(solution)/shard_map/ppermute | solution.py:190
  40.9 3.6 %shard_map.68.base_ref = f32[48,1024]{1,0:T(8,128)S(1)} custom-call(bf16[9,48,1024]{2,1,0:T(8,128)(2,1)S(1)} %get-tuple-element.56.lhs_ref, f32[48,1024]{1,0:T(8,128)S(1)} %get-tuple-element.57.base_ref, bf16[3072,1024]{1,0:T(8,128)(2,1)S(1)} %get-tuple-element.58.refs_0_, bf16[3072,1024]{1,0:T(8,128)(2,1)S(1)} %get-tuple-element.59.refs_1_, ...), custom_call_target="tpu_custom_call" | custom-call | flops 805306368 | bytes 10485760 | tf_op jit(solution)/shard_map/pallas_call | solution.py:290
  44.5 0.0 collective-permute-done.13
  44.6 3.1 %shard_map.69 = bf16[16,3,1024]{2,1,0:T(4,128)(2,1)S(1)} custom-call(s32[50]{0:T(128)S(1)} %get-tuple-element.36.listed, s32[48,128]{1,0:T(8,128)S(1)} %get-tuple-element.37.adapter_rows_ref, s32[48,128]{1,0:T(8,128)S(1)} %get-tuple-element.38.rank_rows_ref, f32[48,128]{1,0:T(8,128)S(1)} %add.19.hidden_ref, f32[48,1024]{1,0:T(8,128)S(1)} %shard_map.68.base_ref, ...), custom_call_target="tpu_custom_call" | custom-call | flops 603979776 | bytes 1048576 | tf_op jit(solution)/shard_map/pallas_call | solution.py:305
  47.6 11.2 %all_to_all.5 = bf16[16,3,1024]{2,1,0:T(4,128)(2,1)S(1)} all-to-all(bf16[16,3,1024]{2,1,0:T(4,128)(2,1)S(1)} %shard_map.69), channel_id=1, replica_groups=mesh['rep'=2,'feat'=16] {'feat'}, dimensions={0} | all-to-all | bytes 196608 | tf_op jit(solution)/shard_map/all_to_all | solution.py:314
  58.8 0.7 %copy.10 = bf16[3,1,16384]{2,0,1:T(4,128)(2,1)} copy(bf16[3,1,16384]{2,0,1:T(4,128)(2,1)S(1)} %bitcast.6) | data formatting | bytes 196608
  (6 shorter events, 0.0 us)
Async XLA Ops:
  1.0 13.7 %collective-permute-start.3 = (bf16[48,1024]{1,0:T(8,128)(2,1)S(1)}, bf16[48,1024]{1,0:T(8,128)(2,1)S(1)}, u32[]{:S(2)}, u32[]{:S(2)}) collective-permute-start(bf16[48,1024]{1,0:T(8,128)(2,1)S(1)} %reshape.9.refs_0_), channel_id=1, source_target_pairs={{0,8},{1,9},{2,10},{3,11},{4,12},{5,13},{6,14},{7,15},{8,0},{9,1},... | collective-permute-start | bytes 294920 | tf_op jit(solution)/shard_map/ppermute | solution.py:190
  5.1 9.6 %collective-permute-start.2 = (bf16[48,1024]{1,0:T(8,128)(2,1)S(1)}, bf16[48,1024]{1,0:T(8,128)(2,1)S(1)}, u32[]{:S(2)}, u32[]{:S(2)}) collective-permute-start(bf16[48,1024]{1,0:T(8,128)(2,1)S(1)} %reshape.9.refs_0_), channel_id=1, source_target_pairs={{0,12},{1,13},{2,14},{3,15},{4,8},{5,9},{6,10},{7,11},{8,4},{9,5},... | collective-permute-start | bytes 294920 | tf_op jit(solution)/shard_map/ppermute | solution.py:190
  6.5 8.3 %collective-permute-start.1 = (bf16[48,1024]{1,0:T(8,128)(2,1)S(1)}, bf16[48,1024]{1,0:T(8,128)(2,1)S(1)}, u32[]{:S(2)}, u32[]{:S(2)}) collective-permute-start(bf16[48,1024]{1,0:T(8,128)(2,1)S(1)} %reshape.9.refs_0_), channel_id=1, source_target_pairs={{0,4},{1,5},{2,6},{3,7},{4,0},{5,1},{6,2},{7,3},{8,12},{9,13},{10,... | collective-permute-start | bytes 294920 | tf_op jit(solution)/shard_map/ppermute | solution.py:190
  6.7 8.0 %collective-permute-start = (bf16[48,1024]{1,0:T(8,128)(2,1)S(1)}, bf16[48,1024]{1,0:T(8,128)(2,1)S(1)}, u32[]{:S(2)}, u32[]{:S(2)}) collective-permute-start(bf16[48,1024]{1,0:T(8,128)(2,1)S(1)} %reshape.9.refs_0_), channel_id=1, source_target_pairs={{0,2},{1,3},{2,0},{3,1},{4,6},{5,7},{6,4},{7,5},{8,10},{9,11},{10,... | collective-permute-start | bytes 294920 | tf_op jit(solution)/shard_map/ppermute | solution.py:190
  14.8 8.0 %collective-permute-start.4 = (bf16[144,1024]{1,0:T(8,128)(2,1)S(1)}, bf16[144,1024]{1,0:T(8,128)(2,1)S(1)}, u32[]{:S(2)}, u32[]{:S(2)}) collective-permute-start(bf16[144,1024]{1,0:T(8,128)(2,1)S(1)} %constant_dynamic-update-slice_fusion.refs_1_), channel_id=1, source_target_pairs={{0,2},{1,3},{2,0},{3,1},{4,6},{5,7},{6,4},{7,5},{8,10},{9,11},{10,... | collective-permute-start | bytes 884744 | tf_op jit(solution)/shard_map/ppermute | solution.py:190
  15.4 9.3 %collective-permute-start.6 = (bf16[144,1024]{1,0:T(8,128)(2,1)S(1)}, bf16[144,1024]{1,0:T(8,128)(2,1)S(1)}, u32[]{:S(2)}, u32[]{:S(2)}) collective-permute-start(bf16[144,1024]{1,0:T(8,128)(2,1)S(1)} %constant_dynamic-update-slice_fusion.refs_1_), channel_id=1, source_target_pairs={{0,1},{1,0},{2,3},{3,2},{4,5},{5,4},{6,7},{7,6},{8,9},{9,8},{10,11... | collective-permute-start | bytes 884744 | tf_op jit(solution)/shard_map/ppermute | solution.py:190
  22.8 1.9 %collective-permute-start.8 = (bf16[144,1024]{1,0:T(8,128)(2,1)S(1)}, bf16[144,1024]{1,0:T(8,128)(2,1)S(1)}, u32[]{:S(2)}, u32[]{:S(2)}) collective-permute-start(bf16[144,1024]{1,0:T(8,128)(2,1)S(1)} %collective-permute-done.4.refs_3_), channel_id=1, source_target_pairs={{0,1},{1,0},{2,3},{3,2},{4,5},{5,4},{6,7},{7,6},{8,9},{9,8},{10,11... | collective-permute-start | bytes 884744 | tf_op jit(solution)/shard_map/ppermute | solution.py:190
  22.8 1.7 %collective-permute-start.5 = (bf16[48,1024]{1,0:T(8,128)(2,1)S(1)}, bf16[48,1024]{1,0:T(8,128)(2,1)S(1)}, u32[]{:S(2)}, u32[]{:S(2)}) collective-permute-start(bf16[48,1024]{1,0:T(8,128)(2,1)S(1)} %reshape.9.refs_0_), channel_id=1, source_target_pairs={{0,1},{1,0},{2,3},{3,2},{4,5},{5,4},{6,7},{7,6},{8,9},{9,8},{10,11... | collective-permute-start | bytes 294920 | tf_op jit(solution)/shard_map/ppermute | solution.py:190
  23.3 1.4 %collective-permute-start.7 = (bf16[48,1024]{1,0:T(8,128)(2,1)S(1)}, bf16[48,1024]{1,0:T(8,128)(2,1)S(1)}, u32[]{:S(2)}, u32[]{:S(2)}) collective-permute-start(bf16[48,1024]{1,0:T(8,128)(2,1)S(1)} %collective-permute-done.refs_2_), channel_id=1, source_target_pairs={{0,1},{1,0},{2,3},{3,2},{4,5},{5,4},{6,7},{7,6},{8,9},{9,8},{10,11... | collective-permute-start | bytes 294920 | tf_op jit(solution)/shard_map/ppermute | solution.py:190
  28.2 1.3 %collective-permute-start.9 = (f32[48,128]{1,0:T(8,128)S(1)}, f32[48,128]{1,0:T(8,128)S(1)}, u32[]{:S(2)}, u32[]{:S(2)}) collective-permute-start(f32[48,128]{1,0:T(8,128)S(1)} %get-tuple-element.48), channel_id=1, source_target_pairs={{0,1},{1,0},{2,3},{3,2},{4,5},{5,4},{6,7},{7,6},{8,9},{9,8},{10,11... | collective-permute-start | bytes 73736 | tf_op jit(solution)/shard_map/ppermute | solution.py:190
  29.5 8.1 %collective-permute-start.12 = (f32[48,128]{1,0:T(8,128)S(1)}, f32[48,128]{1,0:T(8,128)S(1)}, u32[]{:S(2)}, u32[]{:S(2)}) collective-permute-start(f32[48,128]{1,0:T(8,128)S(1)} %add.15), channel_id=1, source_target_pairs={{0,6},{1,7},{2,4},{3,5},{4,2},{5,3},{6,0},{7,1},{8,14},{9,15},{10,... | collective-permute-start | bytes 73736 | tf_op jit(solution)/shard_map/ppermute | solution.py:190
  31.9 5.8 %collective-permute-start.11 = (f32[48,128]{1,0:T(8,128)S(1)}, f32[48,128]{1,0:T(8,128)S(1)}, u32[]{:S(2)}, u32[]{:S(2)}) collective-permute-start(f32[48,128]{1,0:T(8,128)S(1)} %add.15), channel_id=1, source_target_pairs={{0,4},{1,5},{2,6},{3,7},{4,0},{5,1},{6,2},{7,3},{8,12},{9,13},{10,... | collective-permute-start | bytes 73736 | tf_op jit(solution)/shard_map/ppermute | solution.py:190
  32.1 5.6 %collective-permute-start.10 = (f32[48,128]{1,0:T(8,128)S(1)}, f32[48,128]{1,0:T(8,128)S(1)}, u32[]{:S(2)}, u32[]{:S(2)}) collective-permute-start(f32[48,128]{1,0:T(8,128)S(1)} %add.15), channel_id=1, source_target_pairs={{0,2},{1,3},{2,0},{3,1},{4,6},{5,7},{6,4},{7,5},{8,10},{9,11},{10,... | collective-permute-start | bytes 73736 | tf_op jit(solution)/shard_map/ppermute | solution.py:190
  37.7 6.9 %collective-permute-start.13 = (f32[48,128]{1,0:T(8,128)S(1)}, f32[48,128]{1,0:T(8,128)S(1)}, u32[]{:S(2)}, u32[]{:S(2)}) collective-permute-start(f32[48,128]{1,0:T(8,128)S(1)} %add_add_fusion), channel_id=1, source_target_pairs={{0,8},{1,9},{2,10},{3,11},{4,12},{5,13},{6,14},{7,15},{8,0},{9,1},... | collective-permute-start | bytes 73736 | tf_op jit(solution)/shard_map/ppermute | solution.py:190

commit v5 on v4

--- a/solution.py
+++ b/solution.py
@@ -29,8 +29,7 @@
         count = count + new
         distance = jnp.bitwise_xor(me, jnp.int32(b // steps))
         part = (distance & 1) * 2 + ((distance >> 1) & 1)
-        across = (distance >> 2) + jnp.where(distance < 4, 0, jnp.where(distance < 8, 2, -1))
-        spot = (part * (owners // 4) + across) * rows + (b % steps) * owners + me
+        spot = (part * (owners // 4) + (distance >> 2)) * rows + (b % steps) * owners + me
         adapter_rows[b : b + 1, :] = jnp.full((1, lanes), adapter, jnp.int32)
         rank_rows[b : b + 1, :] = jnp.full((1, lanes), sizes_ref[adapter], jnp.int32)
         place[b : b + 1, :] = jnp.full((1, lanes), spot, jnp.int32)
@@ -225,6 +224,8 @@
     def piece(i):
         return VMEM((at[i + 1] - at[i], columns), bf16)
 
+    order = ((0, 4, 8, 12, 2), (6, 10, 14))
+    order = order + tuple(tuple(i ^ 1 for i in owners) for owners in order)
     held_0, listed, adapter_rows, rank_rows, place = pl.pallas_call(
         functools.partial(fetch_and_list_kernel, at[0]),
         out_shape=(piece(0), shape((rows + 2,), jnp.int32)) + (shape((rows, width), jnp.int32),) * 3,
@@ -238,7 +239,7 @@
     across = (swap(own, 2), swap(own, 4), swap(own, 12), swap(own, 8))
     across, held_0, listed = lax.optimization_barrier((across, held_0, listed))
     own_y = across[0]
-    near = jnp.concatenate(across[:0:-1], axis=0)
+    near = jnp.concatenate([across[1], across[3], across[2]], axis=0)
     held_1, down_slices = pl.pallas_call(
         functools.partial(fetch_both_kernel, at[1]),
         out_shape=(piece(1), VMEM((rows, depth, width), bf16)),
@@ -250,10 +251,8 @@
     )(listed, left_there(query_weight), left_there(adapter_down_weight))
     far = swap(near, 2)
     far, held_1, down_slices = lax.optimization_barrier((far, held_1, down_slices))
-    parts = (own, near, own_y, far)
-    parts = parts + tuple(swap(part, 1) for part in parts)
-    order = ((0,), (8, 12, 4), (2,), (10, 14, 6))
-    order = order + tuple(tuple(i ^ 1 for i in owners) for owners in order)
+    mine = jnp.concatenate([own, near, own_y], axis=0)
+    parts = (mine, far, swap(mine, 1), swap(far, 1))
 
     hidden, held_2 = pl.pallas_call(
         functools.partial(down_kernel, at[2]),

time: 59.7 us -> 58.9 us (0.987)
  Pallas kernels: 28.1 us -> 26.3 us
  waiting for transfers between devices: 3.07 us -> 4.03 us
    ppermute x14 -> x12, waiting for transfers between devices: 3.07 us -> 4.03 us  [exchange(): lax.ppermute(value, 'feat', [(i, i ^ distance) for i in range(ranks)])]
    pallas_call x1, Pallas kernels: 6.76 us -> 5.94 us  [fast(): pl.pallas_call(functools.partial(fetch_both_kernel, at[1]), out_shape=(pi...]
    ppermute x14 -> x12, starting transfers between devices: 15.2 us -> 14.8 us  [exchange(): lax.ppermute(value, 'feat', [(i, i ^ distance) for i in range(ranks)])]
  transfers between devices with their start and end apart: 14 -> 12, of which waited for: 4 -> 3; matrix products, arithmetic and copies ran while one was open for 0% -> 0% of each run, Pallas kernels for 36% -> 35%
where the time goes in v5:
time: 58.9 us; the launch traced here: 58.3 us
  Pallas kernels  26.3 us (45%)
  starting transfers between devices  14.8 us (25%)
  blocking collectives  11.2 us (19%)
  waiting for transfers between devices  4.03 us (7%)
  local copies, waits for them, and re-layouts  1.74 us (3%)
    ppermute x12, starting transfers between devices, exchange(): lax.ppermute(value, 'feat', [(i, i ^ distance) for i in range(ranks)])  14.8 us
    all_to_all x1, blocking collectives, fast(): lax.all_to_all(out, 'feat', split_axis=0, concat_axis=0, tiled=True)  11.2 us
    pallas_call x1, Pallas kernels, fast(): pl.pallas_call(functools.partial(fetch_and_list_kernel, at[0]), out_shape...  6.47 us
    pallas_call x1, Pallas kernels, fast(): pl.pallas_call(functools.partial(fetch_both_kernel, at[1]), out_shape=(pi...  5.94 us
    pallas_call x1, Pallas kernels, fast(): pl.pallas_call(functools.partial(first_base_kernel, order), out_shape=(sh...  4.42 us
    ppermute x12, waiting for transfers between devices, exchange(): lax.ppermute(value, 'feat', [(i, i ^ distance) for i in range(ranks)])  4.03 us
    pallas_call x1, Pallas kernels, fast(): pl.pallas_call(rest_base_kernel, out_shape=shape((rows, columns), f32), i...  3.6 us
    pallas_call x1, Pallas kernels, fast(): pl.pallas_call(functools.partial(down_kernel, at[2]), out_shape=(shape((r...  3.33 us
  transfers between devices with their start and end apart: 12, of which 3 were waited for; matrix products, arithmetic and copies ran while one was open for 0% of the time, Pallas kernels for 35%

profile of v5, /device:TPU:0, one launch (start us, length us, event | category | flops | bytes accessed | tf_op | source)
XLA Modules:
  0.0 58.3 jit_solution(12206452402524915658)
XLA Ops:
  0.0 1.0 %reshape.9 = bf16[48,1024]{1,0:T(8,128)(2,1)S(1)} reshape(bf16[3,1,16384]{2,0,1:T(4,128)(2,1)} %param.6) | data formatting | bytes 196608 | tf_op jit(solution)/shard_map/reshape | solution.py:238
  1.0 4.1 %collective-permute-start.3 = (bf16[48,1024]{1,0:T(8,128)(2,1)S(1)}, bf16[48,1024]{1,0:T(8,128)(2,1)S(1)}, u32[]{:S(2)}, u32[]{:S(2)}) collective-permute-start(bf16[48,1024]{1,0:T(8,128)(2,1)S(1)} %reshape.9), channel_id=1, source_target_pairs={{0,8},{1,9},{2,10},{3,11},{4,12},{5,13},{6,14},{7,15},{8,0},{9,1},... | collective-permute-start | bytes 294920 | tf_op jit(solution)/shard_map/ppermute | solution.py:189
  5.1 1.3 %collective-permute-start.2 = (bf16[48,1024]{1,0:T(8,128)(2,1)S(1)}, bf16[48,1024]{1,0:T(8,128)(2,1)S(1)}, u32[]{:S(2)}, u32[]{:S(2)}) collective-permute-start(bf16[48,1024]{1,0:T(8,128)(2,1)S(1)} %reshape.9), channel_id=1, source_target_pairs={{0,12},{1,13},{2,14},{3,15},{4,8},{5,9},{6,10},{7,11},{8,4},{9,5},... | collective-permute-start | bytes 294920 | tf_op jit(solution)/shard_map/ppermute | solution.py:189
  6.5 0.2 collective-permute-start.1
  6.7 1.5 %collective-permute-start = (bf16[48,1024]{1,0:T(8,128)(2,1)S(1)}, bf16[48,1024]{1,0:T(8,128)(2,1)S(1)}, u32[]{:S(2)}, u32[]{:S(2)}) collective-permute-start(bf16[48,1024]{1,0:T(8,128)(2,1)S(1)} %reshape.9), channel_id=1, source_target_pairs={{0,2},{1,3},{2,0},{3,1},{4,6},{5,7},{6,4},{7,5},{8,10},{9,11},{10,... | collective-permute-start | bytes 294920 | tf_op jit(solution)/shard_map/ppermute | solution.py:189
  8.2 6.5 %shard_map.64 = (bf16[7168,1024]{1,0:T(8,128)(2,1)S(1)}, s32[50]{0:T(128)S(1)}, s32[48,128]{1,0:T(8,128)S(1)}, s32[48,128]{1,0:T(8,128)S(1)}, s32[48,128]{1,0:T(8,128)S(1)}) custom-call(s32[1]{0:T(128)} %bitcast.me_ref, s32[3,16]{1,0:T(4,128)} %table_ref.1, s32[64]{0:T(128)} %sizes_ref.1, bf16[16384,1024]{1,0:T(8,128)(2,1)} %refs_2_.1), custom_call_target="tpu_custom_call" | custom-call | bytes 14680064 | tf_op jit(solution)/shard_map/pallas_call | solution.py:229
  14.7 0.0 collective-permute-done.3
  14.8 0.0 collective-permute-done.2
  14.8 0.0 collective-permute-done.1
  14.8 0.0 collective-permute-done
  14.9 0.6 collective-permute-start.4
  15.4 0.1 collective-permute-start.5
  15.5 5.9 %shard_map.65 = (bf16[3072,1024]{1,0:T(8,128)(2,1)S(1)}, bf16[48,1024,128]{2,1,0:T(8,128)(2,1)S(1)}) custom-call(s32[50]{0:T(128)S(1)} %get-tuple-element.36.listed, bf16[16384,1024]{1,0:T(8,128)(2,1)} %refs_2_.1, bf16[64,1024,128]{2,1,0:T(8,128)(2,1)} %slices_ref.1), custom_call_target="tpu_custom_call" | custom-call | bytes 18874368 | tf_op jit(solution)/shard_map/pallas_call | solution.py:243
  21.5 1.4 %collective-permute-done.4.refs_1_ = bf16[144,1024]{1,0:T(8,128)(2,1)S(1)} collective-permute-done((bf16[144,1024]{1,0:T(8,128)(2,1)S(1)}, bf16[144,1024]{1,0:T(8,128)(2,1)S(1)}, u32[]{:S(2)}, u32[]{:S(2)}) %collective-permute-start.4) | collective-permute-done | bytes 294944 | tf_op jit(solution)/shard_map/ppermute | solution.py:189
  22.8 0.0 collective-permute-start.6
  22.8 0.0 collective-permute-done.5.refs_2_
  22.8 1.6 %collective-permute-done.6.refs_3_ = bf16[144,1024]{1,0:T(8,128)(2,1)S(1)} collective-permute-done((bf16[144,1024]{1,0:T(8,128)(2,1)S(1)}, bf16[144,1024]{1,0:T(8,128)(2,1)S(1)}, u32[]{:S(2)}, u32[]{:S(2)}) %collective-permute-start.6) | collective-permute-done | bytes 294944 | tf_op jit(solution)/shard_map/ppermute | solution.py:189
  24.4 3.3 %shard_map.66 = (f32[48,128]{1,0:T(8,128)S(1)}, bf16[3072,1024]{1,0:T(8,128)(2,1)S(1)}) custom-call(s32[50]{0:T(128)S(1)} %get-tuple-element.36.listed, s32[48,128]{1,0:T(8,128)S(1)} %get-tuple-element.39.place_ref, s32[48,128]{1,0:T(8,128)S(1)} %get-tuple-element.37.adapter_rows_ref, bf16[240,1024]{1,0:T(8,128)(2,1)S(1)} %constant_dynamic-update-slice_fusion.refs_0_, ...), custom_call_target="tpu_custom_call" | custom-call | flops 603979776 | bytes 1048576 | tf_op jit(solution)/shard_map/pallas_call | solution.py:257
  27.8 0.2 collective-permute-start.7
  28.0 1.1 %collective-permute-done.7 = f32[48,128]{1,0:T(8,128)S(1)} collective-permute-done((f32[48,128]{1,0:T(8,128)S(1)}, f32[48,128]{1,0:T(8,128)S(1)}, u32[]{:S(2)}, u32[]{:S(2)}) %collective-permute-start.7) | collective-permute-done | bytes 24608 | tf_op jit(solution)/shard_map/ppermute | solution.py:189
  29.0 2.2 %collective-permute-start.10 = (f32[48,128]{1,0:T(8,128)S(1)}, f32[48,128]{1,0:T(8,128)S(1)}, u32[]{:S(2)}, u32[]{:S(2)}) collective-permute-start(f32[48,128]{1,0:T(8,128)S(1)} %add.15), channel_id=1, source_target_pairs={{0,6},{1,7},{2,4},{3,5},{4,2},{5,3},{6,0},{7,1},{8,14},{9,15},{10,... | collective-permute-start | bytes 73736 | tf_op jit(solution)/shard_map/ppermute | solution.py:189
  31.3 0.0 collective-permute-start.9
  31.3 1.3 %collective-permute-start.8 = (f32[48,128]{1,0:T(8,128)S(1)}, f32[48,128]{1,0:T(8,128)S(1)}, u32[]{:S(2)}, u32[]{:S(2)}) collective-permute-start(f32[48,128]{1,0:T(8,128)S(1)} %add.15), channel_id=1, source_target_pairs={{0,2},{1,3},{2,0},{3,1},{4,6},{5,7},{6,4},{7,5},{8,10},{9,11},{10,... | collective-permute-start | bytes 73736 | tf_op jit(solution)/shard_map/ppermute | solution.py:189
  32.5 4.4 %shard_map.67 = (bf16[9,48,1024]{2,1,0:T(8,128)(2,1)S(1)}, f32[48,1024]{1,0:T(8,128)S(1)}, bf16[48,128,1024]{2,1,0:T(8,128)(2,1)S(1)}) custom-call(s32[1]{0:T(128)} %bitcast.me_ref, s32[50]{0:T(128)S(1)} %get-tuple-element.36.listed, bf16[240,1024]{1,0:T(8,128)(2,1)S(1)} %constant_dynamic-update-slice_fusion.refs_0_, ...), custom_call_target="tpu_custom_call" | custom-call | flops 805306368 | bytes 16777216 | tf_op jit(solution)/shard_map/pallas_call | solution.py:267
  36.9 0.0 collective-permute-done.10
  37.0 0.0 collective-permute-done.9
  37.0 0.0 collective-permute-done.8
  37.0 3.2 %collective-permute-start.11 = (f32[48,128]{1,0:T(8,128)S(1)}, f32[48,128]{1,0:T(8,128)S(1)}, u32[]{:S(2)}, u32[]{:S(2)}) collective-permute-start(f32[48,128]{1,0:T(8,128)S(1)} %add_add_fusion), channel_id=1, source_target_pairs={{0,8},{1,9},{2,10},{3,11},{4,12},{5,13},{6,14},{7,15},{8,0},{9,1},... | collective-permute-start | bytes 73736 | tf_op jit(solution)/shard_map/ppermute | solution.py:189
  40.2 3.6 %shard_map.68.base_ref = f32[48,1024]{1,0:T(8,128)S(1)} custom-call(bf16[9,48,1024]{2,1,0:T(8,128)(2,1)S(1)} %get-tuple-element.56.lhs_ref, f32[48,1024]{1,0:T(8,128)S(1)} %get-tuple-element.57.base_ref, bf16[3072,1024]{1,0:T(8,128)(2,1)S(1)} %get-tuple-element.58.refs_0_, bf16[3072,1024]{1,0:T(8,128)(2,1)S(1)} %get-tuple-element.59.refs_1_, ...), custom_call_target="tpu_custom_call" | custom-call | flops 805306368 | bytes 10485760 | tf_op jit(solution)/shard_map/pallas_call | solution.py:289
  43.8 0.0 collective-permute-done.11
  43.9 2.6 %shard_map.69 = bf16[16,3,1024]{2,1,0:T(4,128)(2,1)S(1)} custom-call(s32[50]{0:T(128)S(1)} %get-tuple-element.36.listed, s32[48,128]{1,0:T(8,128)S(1)} %get-tuple-element.37.adapter_rows_ref, s32[48,128]{1,0:T(8,128)S(1)} %get-tuple-element.38.rank_rows_ref, f32[48,128]{1,0:T(8,128)S(1)} %add.19.hidden_ref, f32[48,1024]{1,0:T(8,128)S(1)} %shard_map.68.base_ref, ...), custom_call_target="tpu_custom_call" | custom-call | flops 603979776 | bytes 1048576 | tf_op jit(solution)/shard_map/pallas_call | solution.py:304
  46.5 11.2 %all_to_all.5 = bf16[16,3,1024]{2,1,0:T(4,128)(2,1)S(1)} all-to-all(bf16[16,3,1024]{2,1,0:T(4,128)(2,1)S(1)} %shard_map.69), channel_id=1, replica_groups=mesh['rep'=2,'feat'=16] {'feat'}, dimensions={0} | all-to-all | bytes 196608 | tf_op jit(solution)/shard_map/all_to_all | solution.py:313
  57.6 0.7 %copy.12 = bf16[3,1,16384]{2,0,1:T(4,128)(2,1)} copy(bf16[3,1,16384]{2,0,1:T(4,128)(2,1)S(1)} %bitcast.6) | data formatting | bytes 196608
  (9 shorter events, 0.1 us)
Async XLA Ops:
  1.0 13.7 %collective-permute-start.3 = (bf16[48,1024]{1,0:T(8,128)(2,1)S(1)}, bf16[48,1024]{1,0:T(8,128)(2,1)S(1)}, u32[]{:S(2)}, u32[]{:S(2)}) collective-permute-start(bf16[48,1024]{1,0:T(8,128)(2,1)S(1)} %reshape.9), channel_id=1, source_target_pairs={{0,8},{1,9},{2,10},{3,11},{4,12},{5,13},{6,14},{7,15},{8,0},{9,1},... | collective-permute-start | bytes 294920 | tf_op jit(solution)/shard_map/ppermute | solution.py:189
  5.1 9.6 %collective-permute-start.2 = (bf16[48,1024]{1,0:T(8,128)(2,1)S(1)}, bf16[48,1024]{1,0:T(8,128)(2,1)S(1)}, u32[]{:S(2)}, u32[]{:S(2)}) collective-permute-start(bf16[48,1024]{1,0:T(8,128)(2,1)S(1)} %reshape.9), channel_id=1, source_target_pairs={{0,12},{1,13},{2,14},{3,15},{4,8},{5,9},{6,10},{7,11},{8,4},{9,5},... | collective-permute-start | bytes 294920 | tf_op jit(solution)/shard_map/ppermute | solution.py:189
  6.5 8.3 %collective-permute-start.1 = (bf16[48,1024]{1,0:T(8,128)(2,1)S(1)}, bf16[48,1024]{1,0:T(8,128)(2,1)S(1)}, u32[]{:S(2)}, u32[]{:S(2)}) collective-permute-start(bf16[48,1024]{1,0:T(8,128)(2,1)S(1)} %reshape.9), channel_id=1, source_target_pairs={{0,4},{1,5},{2,6},{3,7},{4,0},{5,1},{6,2},{7,3},{8,12},{9,13},{10,... | collective-permute-start | bytes 294920 | tf_op jit(solution)/shard_map/ppermute | solution.py:189
  6.7 8.0 %collective-permute-start = (bf16[48,1024]{1,0:T(8,128)(2,1)S(1)}, bf16[48,1024]{1,0:T(8,128)(2,1)S(1)}, u32[]{:S(2)}, u32[]{:S(2)}) collective-permute-start(bf16[48,1024]{1,0:T(8,128)(2,1)S(1)} %reshape.9), channel_id=1, source_target_pairs={{0,2},{1,3},{2,0},{3,1},{4,6},{5,7},{6,4},{7,5},{8,10},{9,11},{10,... | collective-permute-start | bytes 294920 | tf_op jit(solution)/shard_map/ppermute | solution.py:189
  14.9 8.0 %collective-permute-start.4 = (bf16[144,1024]{1,0:T(8,128)(2,1)S(1)}, bf16[144,1024]{1,0:T(8,128)(2,1)S(1)}, u32[]{:S(2)}, u32[]{:S(2)}) collective-permute-start(bf16[144,1024]{1,0:T(8,128)(2,1)S(1)} %pad_maximum_fusion), channel_id=1, source_target_pairs={{0,2},{1,3},{2,0},{3,1},{4,6},{5,7},{6,4},{7,5},{8,10},{9,11},{10,... | collective-permute-start | bytes 884744 | tf_op jit(solution)/shard_map/ppermute | solution.py:189
  15.4 7.4 %collective-permute-start.5 = (bf16[240,1024]{1,0:T(8,128)(2,1)S(1)}, bf16[240,1024]{1,0:T(8,128)(2,1)S(1)}, u32[]{:S(2)}, u32[]{:S(2)}) collective-permute-start(bf16[240,1024]{1,0:T(8,128)(2,1)S(1)} %constant_dynamic-update-slice_fusion.refs_0_), channel_id=1, source_target_pairs={{0,1},{1,0},{2,3},{3,2},{4,5},{5,4},{6,7},{7,6},{8,9},{9,8},{10,11... | collective-permute-start | bytes 1474568 | tf_op jit(solution)/shard_map/ppermute | solution.py:189
  22.8 1.6 %collective-permute-start.6 = (bf16[144,1024]{1,0:T(8,128)(2,1)S(1)}, bf16[144,1024]{1,0:T(8,128)(2,1)S(1)}, u32[]{:S(2)}, u32[]{:S(2)}) collective-permute-start(bf16[144,1024]{1,0:T(8,128)(2,1)S(1)} %collective-permute-done.4.refs_1_), channel_id=1, source_target_pairs={{0,1},{1,0},{2,3},{3,2},{4,5},{5,4},{6,7},{7,6},{8,9},{9,8},{10,11... | collective-permute-start | bytes 884744 | tf_op jit(solution)/shard_map/ppermute | solution.py:189
  27.8 1.3 %collective-permute-start.7 = (f32[48,128]{1,0:T(8,128)S(1)}, f32[48,128]{1,0:T(8,128)S(1)}, u32[]{:S(2)}, u32[]{:S(2)}) collective-permute-start(f32[48,128]{1,0:T(8,128)S(1)} %get-tuple-element.48), channel_id=1, source_target_pairs={{0,1},{1,0},{2,3},{3,2},{4,5},{5,4},{6,7},{7,6},{8,9},{9,8},{10,11... | collective-permute-start | bytes 73736 | tf_op jit(solution)/shard_map/ppermute | solution.py:189
  29.0 7.9 %collective-permute-start.10 = (f32[48,128]{1,0:T(8,128)S(1)}, f32[48,128]{1,0:T(8,128)S(1)}, u32[]{:S(2)}, u32[]{:S(2)}) collective-permute-start(f32[48,128]{1,0:T(8,128)S(1)} %add.15), channel_id=1, source_target_pairs={{0,6},{1,7},{2,4},{3,5},{4,2},{5,3},{6,0},{7,1},{8,14},{9,15},{10,... | collective-permute-start | bytes 73736 | tf_op jit(solution)/shard_map/ppermute | solution.py:189
  31.3 5.7 %collective-permute-start.9 = (f32[48,128]{1,0:T(8,128)S(1)}, f32[48,128]{1,0:T(8,128)S(1)}, u32[]{:S(2)}, u32[]{:S(2)}) collective-permute-start(f32[48,128]{1,0:T(8,128)S(1)} %add.15), channel_id=1, source_target_pairs={{0,4},{1,5},{2,6},{3,7},{4,0},{5,1},{6,2},{7,3},{8,12},{9,13},{10,... | collective-permute-start | bytes 73736 | tf_op jit(solution)/shard_map/ppermute | solution.py:189
  31.3 5.7 %collective-permute-start.8 = (f32[48,128]{1,0:T(8,128)S(1)}, f32[48,128]{1,0:T(8,128)S(1)}, u32[]{:S(2)}, u32[]{:S(2)}) collective-permute-start(f32[48,128]{1,0:T(8,128)S(1)} %add.15), channel_id=1, source_target_pairs={{0,2},{1,3},{2,0},{3,1},{4,6},{5,7},{6,4},{7,5},{8,10},{9,11},{10,... | collective-permute-start | bytes 73736 | tf_op jit(solution)/shard_map/ppermute | solution.py:189
  37.0 6.9 %collective-permute-start.11 = (f32[48,128]{1,0:T(8,128)S(1)}, f32[48,128]{1,0:T(8,128)S(1)}, u32[]{:S(2)}, u32[]{:S(2)}) collective-permute-start(f32[48,128]{1,0:T(8,128)S(1)} %add_add_fusion), channel_id=1, source_target_pairs={{0,8},{1,9},{2,10},{3,11},{4,12},{5,13},{6,14},{7,15},{8,0},{9,1},... | collective-permute-start | bytes 73736 | tf_op jit(solution)/shard_map/ppermute | solution.py:189

commit v6 on v5

--- a/solution.py
+++ b/solution.py
@@ -282,9 +282,9 @@
     )(me, listed, *parts, held_here(held_0), left_there(adapter_up_weight))
 
     hidden = hidden + swap(hidden, 1)
-    three = (swap(hidden, 2), swap(hidden, 4), swap(hidden, 6))
-    three, lhs, base, up_slices = lax.optimization_barrier((three, lhs, base, up_slices))
-    hidden = hidden + three[0] + three[1] + three[2]
+    across = swap(hidden, 8)
+    across, lhs, base, up_slices = lax.optimization_barrier((across, lhs, base, up_slices))
+    hidden = hidden + across
 
     base = pl.pallas_call(
         rest_base_kernel,
@@ -298,8 +298,9 @@
         compiler_params=pltpu.CompilerParams(vmem_limit_bytes=(2 * (ranks - FETCHED[-1]) + 3) << 20),
         cost_estimate=cost(flops // 2, 10 << 20),
     )(lhs, base, held_here(held_1), held_here(held_2), left_there(query_weight))
-    last, base = lax.optimization_barrier((swap(hidden, 8), base))
-    hidden = hidden + last
+    near = (swap(hidden, 2), swap(hidden, 4), swap(hidden, 6))
+    near, base = lax.optimization_barrier((near, base))
+    hidden = hidden + near[0] + near[1] + near[2]
 
     out = pl.pallas_call(
         up_kernel,

time: 58.9 us -> 58.7 us (level)
  Pallas kernels: 26.3 us -> 27.7 us
  waiting for transfers between devices: 4.03 us -> 3.39 us
  blocking collectives: 11.2 us -> 10.6 us
    ppermute x12, waiting for transfers between devices: 4.03 us -> 3.39 us  [exchange(): lax.ppermute(value, 'feat', [(i, i ^ distance) for i in range(ranks)])]
    pallas_call x1, Pallas kernels: 5.94 us -> 6.58 us  [fast(): pl.pallas_call(functools.partial(fetch_both_kernel, at[1]), out_shape=(pi...]
  transfers between devices with their start and end apart: 12 -> 12, of which waited for: 3 -> 3; matrix products, arithmetic and copies ran while one was open for 0% -> 0% of each run, Pallas kernels for 35% -> 36%
where the time goes in v6:
time: 58.7 us; the launch traced here: 58.4 us
  Pallas kernels  27.7 us (47%)
  starting transfers between devices  14.8 us (25%)
  blocking collectives  10.6 us (18%)
  waiting for transfers between devices  3.39 us (6%)
  local copies, waits for them, and re-layouts  1.74 us (3%)
    ppermute x12, starting transfers between devices, exchange(): lax.ppermute(value, 'feat', [(i, i ^ distance) for i in range(ranks)])  14.8 us
    all_to_all x1, blocking collectives, fast(): lax.all_to_all(out, 'feat', split_axis=0, concat_axis=0, tiled=True)  10.6 us
    pallas_call x1, Pallas kernels, fast(): pl.pallas_call(functools.partial(fetch_both_kernel, at[1]), out_shape=(pi...  6.58 us
    pallas_call x1, Pallas kernels, fast(): pl.pallas_call(functools.partial(fetch_and_list_kernel, at[0]), out_shape...  6.47 us
    pallas_call x1, Pallas kernels, fast(): pl.pallas_call(functools.partial(first_base_kernel, order), out_shape=(sh...  4.56 us
    pallas_call x1, Pallas kernels, fast(): pl.pallas_call(rest_base_kernel, out_shape=shape((rows, columns), f32), i...  3.6 us
    ppermute x12, waiting for transfers between devices, exchange(): lax.ppermute(value, 'feat', [(i, i ^ distance) for i in range(ranks)])  3.39 us
    pallas_call x1, Pallas kernels, fast(): pl.pallas_call(functools.partial(down_kernel, at[2]), out_shape=(shape((r...  3.39 us
  transfers between devices with their start and end apart: 12, of which 3 were waited for; matrix products, arithmetic and copies ran while one was open for 0% of the time, Pallas kernels for 36%

profile of v6, /device:TPU:0, one launch (start us, length us, event | category | flops | bytes accessed | tf_op | source)
XLA Modules:
  0.0 58.4 jit_solution(13270819018398575612)
XLA Ops:
  0.0 1.0 %reshape.9 = bf16[48,1024]{1,0:T(8,128)(2,1)S(1)} reshape(bf16[3,1,16384]{2,0,1:T(4,128)(2,1)} %param.6) | data formatting | bytes 196608 | tf_op jit(solution)/shard_map/reshape | solution.py:238
  1.0 4.1 %collective-permute-start.3 = (bf16[48,1024]{1,0:T(8,128)(2,1)S(1)}, bf16[48,1024]{1,0:T(8,128)(2,1)S(1)}, u32[]{:S(2)}, u32[]{:S(2)}) collective-permute-start(bf16[48,1024]{1,0:T(8,128)(2,1)S(1)} %reshape.9), channel_id=1, source_target_pairs={{0,8},{1,9},{2,10},{3,11},{4,12},{5,13},{6,14},{7,15},{8,0},{9,1},... | collective-permute-start | bytes 294920 | tf_op jit(solution)/shard_map/ppermute | solution.py:189
  5.1 1.3 %collective-permute-start.2 = (bf16[48,1024]{1,0:T(8,128)(2,1)S(1)}, bf16[48,1024]{1,0:T(8,128)(2,1)S(1)}, u32[]{:S(2)}, u32[]{:S(2)}) collective-permute-start(bf16[48,1024]{1,0:T(8,128)(2,1)S(1)} %reshape.9), channel_id=1, source_target_pairs={{0,12},{1,13},{2,14},{3,15},{4,8},{5,9},{6,10},{7,11},{8,4},{9,5},... | collective-permute-start | bytes 294920 | tf_op jit(solution)/shard_map/ppermute | solution.py:189
  6.5 0.2 collective-permute-start.1
  6.7 1.5 %collective-permute-start = (bf16[48,1024]{1,0:T(8,128)(2,1)S(1)}, bf16[48,1024]{1,0:T(8,128)(2,1)S(1)}, u32[]{:S(2)}, u32[]{:S(2)}) collective-permute-start(bf16[48,1024]{1,0:T(8,128)(2,1)S(1)} %reshape.9), channel_id=1, source_target_pairs={{0,2},{1,3},{2,0},{3,1},{4,6},{5,7},{6,4},{7,5},{8,10},{9,11},{10,... | collective-permute-start | bytes 294920 | tf_op jit(solution)/shard_map/ppermute | solution.py:189
  8.2 6.5 %shard_map.64 = (bf16[7168,1024]{1,0:T(8,128)(2,1)S(1)}, s32[50]{0:T(128)S(1)}, s32[48,128]{1,0:T(8,128)S(1)}, s32[48,128]{1,0:T(8,128)S(1)}, s32[48,128]{1,0:T(8,128)S(1)}) custom-call(s32[1]{0:T(128)} %bitcast.me_ref, s32[3,16]{1,0:T(4,128)} %table_ref.1, s32[64]{0:T(128)} %sizes_ref.1, bf16[16384,1024]{1,0:T(8,128)(2,1)} %refs_2_.1), custom_call_target="tpu_custom_call" | custom-call | bytes 14680064 | tf_op jit(solution)/shard_map/pallas_call | solution.py:229
  14.7 0.0 collective-permute-done.3
  14.8 0.0 collective-permute-done.2
  14.8 0.0 collective-permute-done.1
  14.8 0.0 collective-permute-done
  14.9 0.6 collective-permute-start.4
  15.4 0.1 collective-permute-start.5
  15.5 6.6 %shard_map.65 = (bf16[3072,1024]{1,0:T(8,128)(2,1)S(1)}, bf16[48,1024,128]{2,1,0:T(8,128)(2,1)S(1)}) custom-call(s32[50]{0:T(128)S(1)} %get-tuple-element.36.listed, bf16[16384,1024]{1,0:T(8,128)(2,1)} %refs_2_.1, bf16[64,1024,128]{2,1,0:T(8,128)(2,1)} %slices_ref.1), custom_call_target="tpu_custom_call" | custom-call | bytes 18874368 | tf_op jit(solution)/shard_map/pallas_call | solution.py:243
  22.1 0.7 %collective-permute-done.4.refs_1_ = bf16[144,1024]{1,0:T(8,128)(2,1)S(1)} collective-permute-done((bf16[144,1024]{1,0:T(8,128)(2,1)S(1)}, bf16[144,1024]{1,0:T(8,128)(2,1)S(1)}, u32[]{:S(2)}, u32[]{:S(2)}) %collective-permute-start.4) | collective-permute-done | bytes 294944 | tf_op jit(solution)/shard_map/ppermute | solution.py:189
  22.8 0.0 collective-permute-start.6
  22.8 0.0 collective-permute-done.5.refs_2_
  22.8 1.6 %collective-permute-done.6.refs_3_ = bf16[144,1024]{1,0:T(8,128)(2,1)S(1)} collective-permute-done((bf16[144,1024]{1,0:T(8,128)(2,1)S(1)}, bf16[144,1024]{1,0:T(8,128)(2,1)S(1)}, u32[]{:S(2)}, u32[]{:S(2)}) %collective-permute-start.6) | collective-permute-done | bytes 294944 | tf_op jit(solution)/shard_map/ppermute | solution.py:189
  24.4 3.4 %shard_map.66 = (f32[48,128]{1,0:T(8,128)S(1)}, bf16[3072,1024]{1,0:T(8,128)(2,1)S(1)}) custom-call(s32[50]{0:T(128)S(1)} %get-tuple-element.36.listed, s32[48,128]{1,0:T(8,128)S(1)} %get-tuple-element.39.place_ref, s32[48,128]{1,0:T(8,128)S(1)} %get-tuple-element.37.adapter_rows_ref, bf16[240,1024]{1,0:T(8,128)(2,1)S(1)} %constant_dynamic-update-slice_fusion.refs_0_, ...), custom_call_target="tpu_custom_call" | custom-call | flops 603979776 | bytes 1048576 | tf_op jit(solution)/shard_map/pallas_call | solution.py:257
  27.8 0.2 collective-permute-start.7
  28.0 1.1 %collective-permute-done.7 = f32[48,128]{1,0:T(8,128)S(1)} collective-permute-done((f32[48,128]{1,0:T(8,128)S(1)}, f32[48,128]{1,0:T(8,128)S(1)}, u32[]{:S(2)}, u32[]{:S(2)}) %collective-permute-start.7) | collective-permute-done | bytes 24608 | tf_op jit(solution)/shard_map/ppermute | solution.py:189
  29.1 3.2 %collective-permute-start.8 = (f32[48,128]{1,0:T(8,128)S(1)}, f32[48,128]{1,0:T(8,128)S(1)}, u32[]{:S(2)}, u32[]{:S(2)}) collective-permute-start(f32[48,128]{1,0:T(8,128)S(1)} %add.15), channel_id=1, source_target_pairs={{0,8},{1,9},{2,10},{3,11},{4,12},{5,13},{6,14},{7,15},{8,0},{9,1},... | collective-permute-start | bytes 73736 | tf_op jit(solution)/shard_map/ppermute | solution.py:189
  32.3 4.6 %shard_map.67 = (bf16[9,48,1024]{2,1,0:T(8,128)(2,1)S(1)}, f32[48,1024]{1,0:T(8,128)S(1)}, bf16[48,128,1024]{2,1,0:T(8,128)(2,1)S(1)}) custom-call(s32[1]{0:T(128)} %bitcast.me_ref, s32[50]{0:T(128)S(1)} %get-tuple-element.36.listed, bf16[240,1024]{1,0:T(8,128)(2,1)S(1)} %constant_dynamic-update-slice_fusion.refs_0_, ...), custom_call_target="tpu_custom_call" | custom-call | flops 805306368 | bytes 16777216 | tf_op jit(solution)/shard_map/pallas_call | solution.py:267
  36.8 0.0 collective-permute-done.8
  36.9 0.8 %collective-permute-start.11 = (f32[48,128]{1,0:T(8,128)S(1)}, f32[48,128]{1,0:T(8,128)S(1)}, u32[]{:S(2)}, u32[]{:S(2)}) collective-permute-start(f32[48,128]{1,0:T(8,128)S(1)} %add.16), channel_id=1, source_target_pairs={{0,6},{1,7},{2,4},{3,5},{4,2},{5,3},{6,0},{7,1},{8,14},{9,15},{10,... | collective-permute-start | bytes 73736 | tf_op jit(solution)/shard_map/ppermute | solution.py:189
  37.7 2.2 %collective-permute-start.10 = (f32[48,128]{1,0:T(8,128)S(1)}, f32[48,128]{1,0:T(8,128)S(1)}, u32[]{:S(2)}, u32[]{:S(2)}) collective-permute-start(f32[48,128]{1,0:T(8,128)S(1)} %add.16), channel_id=1, source_target_pairs={{0,4},{1,5},{2,6},{3,7},{4,0},{5,1},{6,2},{7,3},{8,12},{9,13},{10,... | collective-permute-start | bytes 73736 | tf_op jit(solution)/shard_map/ppermute | solution.py:189
  39.9 0.5 collective-permute-start.9
  40.4 3.6 %shard_map.68.base_ref = f32[48,1024]{1,0:T(8,128)S(1)} custom-call(bf16[9,48,1024]{2,1,0:T(8,128)(2,1)S(1)} %get-tuple-element.54.lhs_ref, f32[48,1024]{1,0:T(8,128)S(1)} %get-tuple-element.55.base_ref, bf16[3072,1024]{1,0:T(8,128)(2,1)S(1)} %get-tuple-element.56.refs_0_, bf16[3072,1024]{1,0:T(8,128)(2,1)S(1)} %get-tuple-element.57.refs_1_, ...), custom_call_target="tpu_custom_call" | custom-call | flops 805306368 | bytes 10485760 | tf_op jit(solution)/shard_map/pallas_call | solution.py:289
  44.0 0.0 collective-permute-done.11
  44.0 0.0 collective-permute-done.10
  44.0 0.0 collective-permute-done.9
  44.1 3.1 %shard_map.69 = bf16[16,3,1024]{2,1,0:T(4,128)(2,1)S(1)} custom-call(s32[50]{0:T(128)S(1)} %get-tuple-element.36.listed, s32[48,128]{1,0:T(8,128)S(1)} %get-tuple-element.37.adapter_rows_ref, s32[48,128]{1,0:T(8,128)S(1)} %get-tuple-element.38.rank_rows_ref, f32[48,128]{1,0:T(8,128)S(1)} %add_add_fusion.hidden_ref, f32[48,1024]{1,0:T(8,128)S(1)} %shard_map.68.base_ref, ...), custom_call_target="tpu_custom_call" | custom-call | flops 603979776 | bytes 1048576 | tf_op jit(solution)/shard_map/pallas_call | solution.py:305
  47.2 10.6 %all_to_all.5 = bf16[16,3,1024]{2,1,0:T(4,128)(2,1)S(1)} all-to-all(bf16[16,3,1024]{2,1,0:T(4,128)(2,1)S(1)} %shard_map.69), channel_id=1, replica_groups=mesh['rep'=2,'feat'=16] {'feat'}, dimensions={0} | all-to-all | bytes 196608 | tf_op jit(solution)/shard_map/all_to_all | solution.py:314
  57.8 0.7 %copy.12 = bf16[3,1,16384]{2,0,1:T(4,128)(2,1)} copy(bf16[3,1,16384]{2,0,1:T(4,128)(2,1)S(1)} %bitcast.6) | data formatting | bytes 196608
  (9 shorter events, 0.1 us)
Async XLA Ops:
  1.0 13.7 %collective-permute-start.3 = (bf16[48,1024]{1,0:T(8,128)(2,1)S(1)}, bf16[48,1024]{1,0:T(8,128)(2,1)S(1)}, u32[]{:S(2)}, u32[]{:S(2)}) collective-permute-start(bf16[48,1024]{1,0:T(8,128)(2,1)S(1)} %reshape.9), channel_id=1, source_target_pairs={{0,8},{1,9},{2,10},{3,11},{4,12},{5,13},{6,14},{7,15},{8,0},{9,1},... | collective-permute-start | bytes 294920 | tf_op jit(solution)/shard_map/ppermute | solution.py:189
  5.1 9.6 %collective-permute-start.2 = (bf16[48,1024]{1,0:T(8,128)(2,1)S(1)}, bf16[48,1024]{1,0:T(8,128)(2,1)S(1)}, u32[]{:S(2)}, u32[]{:S(2)}) collective-permute-start(bf16[48,1024]{1,0:T(8,128)(2,1)S(1)} %reshape.9), channel_id=1, source_target_pairs={{0,12},{1,13},{2,14},{3,15},{4,8},{5,9},{6,10},{7,11},{8,4},{9,5},... | collective-permute-start | bytes 294920 | tf_op jit(solution)/shard_map/ppermute | solution.py:189
  6.5 8.3 %collective-permute-start.1 = (bf16[48,1024]{1,0:T(8,128)(2,1)S(1)}, bf16[48,1024]{1,0:T(8,128)(2,1)S(1)}, u32[]{:S(2)}, u32[]{:S(2)}) collective-permute-start(bf16[48,1024]{1,0:T(8,128)(2,1)S(1)} %reshape.9), channel_id=1, source_target_pairs={{0,4},{1,5},{2,6},{3,7},{4,0},{5,1},{6,2},{7,3},{8,12},{9,13},{10,... | collective-permute-start | bytes 294920 | tf_op jit(solution)/shard_map/ppermute | solution.py:189
  6.7 8.0 %collective-permute-start = (bf16[48,1024]{1,0:T(8,128)(2,1)S(1)}, bf16[48,1024]{1,0:T(8,128)(2,1)S(1)}, u32[]{:S(2)}, u32[]{:S(2)}) collective-permute-start(bf16[48,1024]{1,0:T(8,128)(2,1)S(1)} %reshape.9), channel_id=1, source_target_pairs={{0,2},{1,3},{2,0},{3,1},{4,6},{5,7},{6,4},{7,5},{8,10},{9,11},{10,... | collective-permute-start | bytes 294920 | tf_op jit(solution)/shard_map/ppermute | solution.py:189
  14.9 8.0 %collective-permute-start.4 = (bf16[144,1024]{1,0:T(8,128)(2,1)S(1)}, bf16[144,1024]{1,0:T(8,128)(2,1)S(1)}, u32[]{:S(2)}, u32[]{:S(2)}) collective-permute-start(bf16[144,1024]{1,0:T(8,128)(2,1)S(1)} %pad_maximum_fusion), channel_id=1, source_target_pairs={{0,2},{1,3},{2,0},{3,1},{4,6},{5,7},{6,4},{7,5},{8,10},{9,11},{10,... | collective-permute-start | bytes 884744 | tf_op jit(solution)/shard_map/ppermute | solution.py:189
  15.4 7.4 %collective-permute-start.5 = (bf16[240,1024]{1,0:T(8,128)(2,1)S(1)}, bf16[240,1024]{1,0:T(8,128)(2,1)S(1)}, u32[]{:S(2)}, u32[]{:S(2)}) collective-permute-start(bf16[240,1024]{1,0:T(8,128)(2,1)S(1)} %constant_dynamic-update-slice_fusion.refs_0_), channel_id=1, source_target_pairs={{0,1},{1,0},{2,3},{3,2},{4,5},{5,4},{6,7},{7,6},{8,9},{9,8},{10,11... | collective-permute-start | bytes 1474568 | tf_op jit(solution)/shard_map/ppermute | solution.py:189
  22.8 1.6 %collective-permute-start.6 = (bf16[144,1024]{1,0:T(8,128)(2,1)S(1)}, bf16[144,1024]{1,0:T(8,128)(2,1)S(1)}, u32[]{:S(2)}, u32[]{:S(2)}) collective-permute-start(bf16[144,1024]{1,0:T(8,128)(2,1)S(1)} %collective-permute-done.4.refs_1_), channel_id=1, source_target_pairs={{0,1},{1,0},{2,3},{3,2},{4,5},{5,4},{6,7},{7,6},{8,9},{9,8},{10,11... | collective-permute-start | bytes 884744 | tf_op jit(solution)/shard_map/ppermute | solution.py:189
  27.8 1.3 %collective-permute-start.7 = (f32[48,128]{1,0:T(8,128)S(1)}, f32[48,128]{1,0:T(8,128)S(1)}, u32[]{:S(2)}, u32[]{:S(2)}) collective-permute-start(f32[48,128]{1,0:T(8,128)S(1)} %get-tuple-element.48), channel_id=1, source_target_pairs={{0,1},{1,0},{2,3},{3,2},{4,5},{5,4},{6,7},{7,6},{8,9},{9,8},{10,11... | collective-permute-start | bytes 73736 | tf_op jit(solution)/shard_map/ppermute | solution.py:189
  29.1 7.8 %collective-permute-start.8 = (f32[48,128]{1,0:T(8,128)S(1)}, f32[48,128]{1,0:T(8,128)S(1)}, u32[]{:S(2)}, u32[]{:S(2)}) collective-permute-start(f32[48,128]{1,0:T(8,128)S(1)} %add.15), channel_id=1, source_target_pairs={{0,8},{1,9},{2,10},{3,11},{4,12},{5,13},{6,14},{7,15},{8,0},{9,1},... | collective-permute-start | bytes 73736 | tf_op jit(solution)/shard_map/ppermute | solution.py:189
  36.9 7.2 %collective-permute-start.11 = (f32[48,128]{1,0:T(8,128)S(1)}, f32[48,128]{1,0:T(8,128)S(1)}, u32[]{:S(2)}, u32[]{:S(2)}) collective-permute-start(f32[48,128]{1,0:T(8,128)S(1)} %add.16), channel_id=1, source_target_pairs={{0,6},{1,7},{2,4},{3,5},{4,2},{5,3},{6,0},{7,1},{8,14},{9,15},{10,... | collective-permute-start | bytes 73736 | tf_op jit(solution)/shard_map/ppermute | solution.py:189
  37.7 6.4 %collective-permute-start.10 = (f32[48,128]{1,0:T(8,128)S(1)}, f32[48,128]{1,0:T(8,128)S(1)}, u32[]{:S(2)}, u32[]{:S(2)}) collective-permute-start(f32[48,128]{1,0:T(8,128)S(1)} %add.16), channel_id=1, source_target_pairs={{0,4},{1,5},{2,6},{3,7},{4,0},{5,1},{6,2},{7,3},{8,12},{9,13},{10,... | collective-permute-start | bytes 73736 | tf_op jit(solution)/shard_map/ppermute | solution.py:189
  39.9 4.1 %collective-permute-start.9 = (f32[48,128]{1,0:T(8,128)S(1)}, f32[48,128]{1,0:T(8,128)S(1)}, u32[]{:S(2)}, u32[]{:S(2)}) collective-permute-start(f32[48,128]{1,0:T(8,128)S(1)} %add.16), channel_id=1, source_target_pairs={{0,2},{1,3},{2,0},{3,1},{4,6},{5,7},{6,4},{7,5},{8,10},{9,11},{10,... | collective-permute-start | bytes 73736 | tf_op jit(solution)/shard_map/ppermute | solution.py:189

commit v7 on v6

--- a/solution.py
+++ b/solution.py
@@ -236,10 +236,10 @@
         cost_estimate=cost(0, (at[1] - at[0]) * columns * 2),
     )(me, left_there(adapter_index_table), left_there(adapter_rank_sizes), left_there(query_weight))
     own = tokens.reshape(steps * ranks, chunk)
-    across = (swap(own, 2), swap(own, 4), swap(own, 12), swap(own, 8))
+    across = (swap(own, 4), swap(own, 2), swap(own, 12), swap(own, 8))
     across, held_0, listed = lax.optimization_barrier((across, held_0, listed))
-    own_y = across[0]
-    near = jnp.concatenate([across[1], across[3], across[2]], axis=0)
+    own_y = across[1]
+    near = jnp.concatenate([across[0], across[3], across[2]], axis=0)
     held_1, down_slices = pl.pallas_call(
         functools.partial(fetch_both_kernel, at[1]),
         out_shape=(piece(1), VMEM((rows, depth, width), bf16)),

time: 58.7 us -> 58 us (0.988)
  Pallas kernels: 27.7 us -> 26.3 us
  waiting for transfers between devices: 3.39 us -> 4.28 us
    ppermute x12, waiting for transfers between devices: 3.39 us -> 4.28 us  [exchange(): lax.ppermute(value, 'feat', [(i, i ^ distance) for i in range(ranks)])]
    pallas_call x1, Pallas kernels: 6.58 us -> 5.91 us  [fast(): pl.pallas_call(functools.partial(fetch_both_kernel, at[1]), out_shape=(pi...]
  transfers between devices with their start and end apart: 12 -> 12, of which waited for: 3 -> 3; matrix products, arithmetic and copies ran while one was open for 0% -> 0% of each run, Pallas kernels for 36% -> 35%
where the time goes in v7:
time: 58 us; the launch traced here: 57.7 us
  Pallas kernels  26.3 us (45%)
  starting transfers between devices  14.6 us (25%)
  blocking collectives  10.6 us (18%)
  waiting for transfers between devices  4.28 us (7%)
  local copies, waits for them, and re-layouts  1.74 us (3%)
    ppermute x12, starting transfers between devices, exchange(): lax.ppermute(value, 'feat', [(i, i ^ distance) for i in range(ranks)])  14.6 us
    all_to_all x1, blocking collectives, fast(): lax.all_to_all(out, 'feat', split_axis=0, concat_axis=0, tiled=True)  10.6 us
    pallas_call x1, Pallas kernels, fast(): pl.pallas_call(functools.partial(fetch_and_list_kernel, at[0]), out_shape...  6.47 us
    pallas_call x1, Pallas kernels, fast(): pl.pallas_call(functools.partial(fetch_both_kernel, at[1]), out_shape=(pi...  5.91 us
    pallas_call x1, Pallas kernels, fast(): pl.pallas_call(functools.partial(first_base_kernel, order), out_shape=(sh...  4.41 us
    ppermute x12, waiting for transfers between devices, exchange(): lax.ppermute(value, 'feat', [(i, i ^ distance) for i in range(ranks)])  4.28 us
    pallas_call x1, Pallas kernels, fast(): pl.pallas_call(rest_base_kernel, out_shape=shape((rows, columns), f32), i...  3.6 us
    pallas_call x1, Pallas kernels, fast(): pl.pallas_call(functools.partial(down_kernel, at[2]), out_shape=(shape((r...  3.33 us
  transfers between devices with their start and end apart: 12, of which 3 were waited for; matrix products, arithmetic and copies ran while one was open for 0% of the time, Pallas kernels for 35%

profile of v7, /device:TPU:0, one launch (start us, length us, event | category | flops | bytes accessed | tf_op | source)
XLA Modules:
  0.0 57.7 jit_solution(12534754795568328736)
XLA Ops:
  0.0 1.0 %reshape.9 = bf16[48,1024]{1,0:T(8,128)(2,1)S(1)} reshape(bf16[3,1,16384]{2,0,1:T(4,128)(2,1)} %param.6) | data formatting | bytes 196608 | tf_op jit(solution)/shard_map/reshape | solution.py:238
  1.0 4.1 %collective-permute-start.3 = (bf16[48,1024]{1,0:T(8,128)(2,1)S(1)}, bf16[48,1024]{1,0:T(8,128)(2,1)S(1)}, u32[]{:S(2)}, u32[]{:S(2)}) collective-permute-start(bf16[48,1024]{1,0:T(8,128)(2,1)S(1)} %reshape.9), channel_id=1, source_target_pairs={{0,8},{1,9},{2,10},{3,11},{4,12},{5,13},{6,14},{7,15},{8,0},{9,1},... | collective-permute-start | bytes 294920 | tf_op jit(solution)/shard_map/ppermute | solution.py:189
  5.1 1.3 %collective-permute-start.2 = (bf16[48,1024]{1,0:T(8,128)(2,1)S(1)}, bf16[48,1024]{1,0:T(8,128)(2,1)S(1)}, u32[]{:S(2)}, u32[]{:S(2)}) collective-permute-start(bf16[48,1024]{1,0:T(8,128)(2,1)S(1)} %reshape.9), channel_id=1, source_target_pairs={{0,12},{1,13},{2,14},{3,15},{4,8},{5,9},{6,10},{7,11},{8,4},{9,5},... | collective-permute-start | bytes 294920 | tf_op jit(solution)/shard_map/ppermute | solution.py:189
  6.5 1.5 %collective-permute-start.1 = (bf16[48,1024]{1,0:T(8,128)(2,1)S(1)}, bf16[48,1024]{1,0:T(8,128)(2,1)S(1)}, u32[]{:S(2)}, u32[]{:S(2)}) collective-permute-start(bf16[48,1024]{1,0:T(8,128)(2,1)S(1)} %reshape.9), channel_id=1, source_target_pairs={{0,2},{1,3},{2,0},{3,1},{4,6},{5,7},{6,4},{7,5},{8,10},{9,11},{10,... | collective-permute-start | bytes 294920 | tf_op jit(solution)/shard_map/ppermute | solution.py:189
  8.0 0.2 collective-permute-start
  8.2 6.5 %shard_map.64 = (bf16[7168,1024]{1,0:T(8,128)(2,1)S(1)}, s32[50]{0:T(128)S(1)}, s32[48,128]{1,0:T(8,128)S(1)}, s32[48,128]{1,0:T(8,128)S(1)}, s32[48,128]{1,0:T(8,128)S(1)}) custom-call(s32[1]{0:T(128)} %bitcast.me_ref, s32[3,16]{1,0:T(4,128)} %table_ref.1, s32[64]{0:T(128)} %sizes_ref.1, bf16[16384,1024]{1,0:T(8,128)(2,1)} %refs_2_.1), custom_call_target="tpu_custom_call" | custom-call | bytes 14680064 | tf_op jit(solution)/shard_map/pallas_call | solution.py:229
  14.7 0.0 collective-permute-done.3
  14.8 0.0 collective-permute-done.2
  14.8 0.0 collective-permute-done.1
  14.8 0.0 collective-permute-done
  14.9 0.6 %collective-permute-start.4 = (bf16[144,1024]{1,0:T(8,128)(2,1)S(1)}, bf16[144,1024]{1,0:T(8,128)(2,1)S(1)}, u32[]{:S(2)}, u32[]{:S(2)}) collective-permute-start(bf16[144,1024]{1,0:T(8,128)(2,1)S(1)} %pad_maximum_fusion), channel_id=1, source_target_pairs={{0,2},{1,3},{2,0},{3,1},{4,6},{5,7},{6,4},{7,5},{8,10},{9,11},{10,... | collective-permute-start | bytes 884744 | tf_op jit(solution)/shard_map/ppermute | solution.py:189
  15.5 0.1 collective-permute-start.5
  15.6 5.9 %shard_map.65 = (bf16[3072,1024]{1,0:T(8,128)(2,1)S(1)}, bf16[48,1024,128]{2,1,0:T(8,128)(2,1)S(1)}) custom-call(s32[50]{0:T(128)S(1)} %get-tuple-element.36.listed, bf16[16384,1024]{1,0:T(8,128)(2,1)} %refs_2_.1, bf16[64,1024,128]{2,1,0:T(8,128)(2,1)} %slices_ref.1), custom_call_target="tpu_custom_call" | custom-call | bytes 18874368 | tf_op jit(solution)/shard_map/pallas_call | solution.py:243
  21.5 1.6 %collective-permute-done.4.refs_1_ = bf16[144,1024]{1,0:T(8,128)(2,1)S(1)} collective-permute-done((bf16[144,1024]{1,0:T(8,128)(2,1)S(1)}, bf16[144,1024]{1,0:T(8,128)(2,1)S(1)}, u32[]{:S(2)}, u32[]{:S(2)}) %collective-permute-start.4) | collective-permute-done | bytes 294944 | tf_op jit(solution)/shard_map/ppermute | solution.py:189
  23.1 0.0 collective-permute-start.6
  23.1 0.0 collective-permute-done.5.refs_2_
  23.1 1.6 %collective-permute-done.6.refs_3_ = bf16[144,1024]{1,0:T(8,128)(2,1)S(1)} collective-permute-done((bf16[144,1024]{1,0:T(8,128)(2,1)S(1)}, bf16[144,1024]{1,0:T(8,128)(2,1)S(1)}, u32[]{:S(2)}, u32[]{:S(2)}) %collective-permute-start.6) | collective-permute-done | bytes 294944 | tf_op jit(solution)/shard_map/ppermute | solution.py:189
  24.7 3.3 %shard_map.66 = (f32[48,128]{1,0:T(8,128)S(1)}, bf16[3072,1024]{1,0:T(8,128)(2,1)S(1)}) custom-call(s32[50]{0:T(128)S(1)} %get-tuple-element.36.listed, s32[48,128]{1,0:T(8,128)S(1)} %get-tuple-element.39.place_ref, s32[48,128]{1,0:T(8,128)S(1)} %get-tuple-element.37.adapter_rows_ref, bf16[240,1024]{1,0:T(8,128)(2,1)S(1)} %constant_dynamic-update-slice_fusion.refs_0_, ...), custom_call_target="tpu_custom_call" | custom-call | flops 603979776 | bytes 1048576 | tf_op jit(solution)/shard_map/pallas_call | solution.py:257
  28.0 0.2 collective-permute-start.7
  28.2 1.1 %collective-permute-done.7 = f32[48,128]{1,0:T(8,128)S(1)} collective-permute-done((f32[48,128]{1,0:T(8,128)S(1)}, f32[48,128]{1,0:T(8,128)S(1)}, u32[]{:S(2)}, u32[]{:S(2)}) %collective-permute-start.7) | collective-permute-done | bytes 24608 | tf_op jit(solution)/shard_map/ppermute | solution.py:189
  29.3 2.9 %collective-permute-start.8 = (f32[48,128]{1,0:T(8,128)S(1)}, f32[48,128]{1,0:T(8,128)S(1)}, u32[]{:S(2)}, u32[]{:S(2)}) collective-permute-start(f32[48,128]{1,0:T(8,128)S(1)} %add.15), channel_id=1, source_target_pairs={{0,8},{1,9},{2,10},{3,11},{4,12},{5,13},{6,14},{7,15},{8,0},{9,1},... | collective-permute-start | bytes 73736 | tf_op jit(solution)/shard_map/ppermute | solution.py:189
  32.2 4.4 %shard_map.67 = (bf16[9,48,1024]{2,1,0:T(8,128)(2,1)S(1)}, f32[48,1024]{1,0:T(8,128)S(1)}, bf16[48,128,1024]{2,1,0:T(8,128)(2,1)S(1)}) custom-call(s32[1]{0:T(128)} %bitcast.me_ref, s32[50]{0:T(128)S(1)} %get-tuple-element.36.listed, bf16[240,1024]{1,0:T(8,128)(2,1)S(1)} %constant_dynamic-update-slice_fusion.refs_0_, ...), custom_call_target="tpu_custom_call" | custom-call | flops 805306368 | bytes 16777216 | tf_op jit(solution)/shard_map/pallas_call | solution.py:267
  36.6 0.0 collective-permute-done.8
  36.7 0.8 %collective-permute-start.11 = (f32[48,128]{1,0:T(8,128)S(1)}, f32[48,128]{1,0:T(8,128)S(1)}, u32[]{:S(2)}, u32[]{:S(2)}) collective-permute-start(f32[48,128]{1,0:T(8,128)S(1)} %add.16), channel_id=1, source_target_pairs={{0,6},{1,7},{2,4},{3,5},{4,2},{5,3},{6,0},{7,1},{8,14},{9,15},{10,... | collective-permute-start | bytes 73736 | tf_op jit(solution)/shard_map/ppermute | solution.py:189
  37.4 2.3 %collective-permute-start.10 = (f32[48,128]{1,0:T(8,128)S(1)}, f32[48,128]{1,0:T(8,128)S(1)}, u32[]{:S(2)}, u32[]{:S(2)}) collective-permute-start(f32[48,128]{1,0:T(8,128)S(1)} %add.16), channel_id=1, source_target_pairs={{0,4},{1,5},{2,6},{3,7},{4,0},{5,1},{6,2},{7,3},{8,12},{9,13},{10,... | collective-permute-start | bytes 73736 | tf_op jit(solution)/shard_map/ppermute | solution.py:189
  39.7 0.5 collective-permute-start.9
  40.2 3.6 %shard_map.68.base_ref = f32[48,1024]{1,0:T(8,128)S(1)} custom-call(bf16[9,48,1024]{2,1,0:T(8,128)(2,1)S(1)} %get-tuple-element.54.lhs_ref, f32[48,1024]{1,0:T(8,128)S(1)} %get-tuple-element.55.base_ref, bf16[3072,1024]{1,0:T(8,128)(2,1)S(1)} %get-tuple-element.56.refs_0_, bf16[3072,1024]{1,0:T(8,128)(2,1)S(1)} %get-tuple-element.57.refs_1_, ...), custom_call_target="tpu_custom_call" | custom-call | flops 805306368 | bytes 10485760 | tf_op jit(solution)/shard_map/pallas_call | solution.py:289
  43.8 0.0 collective-permute-done.11
  43.8 0.0 collective-permute-done.10
  43.8 0.0 collective-permute-done.9
  43.9 2.6 %shard_map.69 = bf16[16,3,1024]{2,1,0:T(4,128)(2,1)S(1)} custom-call(s32[50]{0:T(128)S(1)} %get-tuple-element.36.listed, s32[48,128]{1,0:T(8,128)S(1)} %get-tuple-element.37.adapter_rows_ref, s32[48,128]{1,0:T(8,128)S(1)} %get-tuple-element.38.rank_rows_ref, f32[48,128]{1,0:T(8,128)S(1)} %add_add_fusion.hidden_ref, f32[48,1024]{1,0:T(8,128)S(1)} %shard_map.68.base_ref, ...), custom_call_target="tpu_custom_call" | custom-call | flops 603979776 | bytes 1048576 | tf_op jit(solution)/shard_map/pallas_call | solution.py:305
  46.5 10.6 %all_to_all.5 = bf16[16,3,1024]{2,1,0:T(4,128)(2,1)S(1)} all-to-all(bf16[16,3,1024]{2,1,0:T(4,128)(2,1)S(1)} %shard_map.69), channel_id=1, replica_groups=mesh['rep'=2,'feat'=16] {'feat'}, dimensions={0} | all-to-all | bytes 196608 | tf_op jit(solution)/shard_map/all_to_all | solution.py:314
  57.1 0.7 %copy.12 = bf16[3,1,16384]{2,0,1:T(4,128)(2,1)} copy(bf16[3,1,16384]{2,0,1:T(4,128)(2,1)S(1)} %bitcast.6) | data formatting | bytes 196608
  (9 shorter events, 0.1 us)
Async XLA Ops:
  1.0 13.7 %collective-permute-start.3 = (bf16[48,1024]{1,0:T(8,128)(2,1)S(1)}, bf16[48,1024]{1,0:T(8,128)(2,1)S(1)}, u32[]{:S(2)}, u32[]{:S(2)}) collective-permute-start(bf16[48,1024]{1,0:T(8,128)(2,1)S(1)} %reshape.9), channel_id=1, source_target_pairs={{0,8},{1,9},{2,10},{3,11},{4,12},{5,13},{6,14},{7,15},{8,0},{9,1},... | collective-permute-start | bytes 294920 | tf_op jit(solution)/shard_map/ppermute | solution.py:189
  5.1 9.6 %collective-permute-start.2 = (bf16[48,1024]{1,0:T(8,128)(2,1)S(1)}, bf16[48,1024]{1,0:T(8,128)(2,1)S(1)}, u32[]{:S(2)}, u32[]{:S(2)}) collective-permute-start(bf16[48,1024]{1,0:T(8,128)(2,1)S(1)} %reshape.9), channel_id=1, source_target_pairs={{0,12},{1,13},{2,14},{3,15},{4,8},{5,9},{6,10},{7,11},{8,4},{9,5},... | collective-permute-start | bytes 294920 | tf_op jit(solution)/shard_map/ppermute | solution.py:189
  6.5 8.3 %collective-permute-start.1 = (bf16[48,1024]{1,0:T(8,128)(2,1)S(1)}, bf16[48,1024]{1,0:T(8,128)(2,1)S(1)}, u32[]{:S(2)}, u32[]{:S(2)}) collective-permute-start(bf16[48,1024]{1,0:T(8,128)(2,1)S(1)} %reshape.9), channel_id=1, source_target_pairs={{0,2},{1,3},{2,0},{3,1},{4,6},{5,7},{6,4},{7,5},{8,10},{9,11},{10,... | collective-permute-start | bytes 294920 | tf_op jit(solution)/shard_map/ppermute | solution.py:189
  8.0 6.8 %collective-permute-start = (bf16[48,1024]{1,0:T(8,128)(2,1)S(1)}, bf16[48,1024]{1,0:T(8,128)(2,1)S(1)}, u32[]{:S(2)}, u32[]{:S(2)}) collective-permute-start(bf16[48,1024]{1,0:T(8,128)(2,1)S(1)} %reshape.9), channel_id=1, source_target_pairs={{0,4},{1,5},{2,6},{3,7},{4,0},{5,1},{6,2},{7,3},{8,12},{9,13},{10,... | collective-permute-start | bytes 294920 | tf_op jit(solution)/shard_map/ppermute | solution.py:189
  14.9 8.2 %collective-permute-start.4 = (bf16[144,1024]{1,0:T(8,128)(2,1)S(1)}, bf16[144,1024]{1,0:T(8,128)(2,1)S(1)}, u32[]{:S(2)}, u32[]{:S(2)}) collective-permute-start(bf16[144,1024]{1,0:T(8,128)(2,1)S(1)} %pad_maximum_fusion), channel_id=1, source_target_pairs={{0,2},{1,3},{2,0},{3,1},{4,6},{5,7},{6,4},{7,5},{8,10},{9,11},{10,... | collective-permute-start | bytes 884744 | tf_op jit(solution)/shard_map/ppermute | solution.py:189
  15.5 7.6 %collective-permute-start.5 = (bf16[240,1024]{1,0:T(8,128)(2,1)S(1)}, bf16[240,1024]{1,0:T(8,128)(2,1)S(1)}, u32[]{:S(2)}, u32[]{:S(2)}) collective-permute-start(bf16[240,1024]{1,0:T(8,128)(2,1)S(1)} %constant_dynamic-update-slice_fusion.refs_0_), channel_id=1, source_target_pairs={{0,1},{1,0},{2,3},{3,2},{4,5},{5,4},{6,7},{7,6},{8,9},{9,8},{10,11... | collective-permute-start | bytes 1474568 | tf_op jit(solution)/shard_map/ppermute | solution.py:189
  23.1 1.6 %collective-permute-start.6 = (bf16[144,1024]{1,0:T(8,128)(2,1)S(1)}, bf16[144,1024]{1,0:T(8,128)(2,1)S(1)}, u32[]{:S(2)}, u32[]{:S(2)}) collective-permute-start(bf16[144,1024]{1,0:T(8,128)(2,1)S(1)} %collective-permute-done.4.refs_1_), channel_id=1, source_target_pairs={{0,1},{1,0},{2,3},{3,2},{4,5},{5,4},{6,7},{7,6},{8,9},{9,8},{10,11... | collective-permute-start | bytes 884744 | tf_op jit(solution)/shard_map/ppermute | solution.py:189
  28.0 1.3 %collective-permute-start.7 = (f32[48,128]{1,0:T(8,128)S(1)}, f32[48,128]{1,0:T(8,128)S(1)}, u32[]{:S(2)}, u32[]{:S(2)}) collective-permute-start(f32[48,128]{1,0:T(8,128)S(1)} %get-tuple-element.48), channel_id=1, source_target_pairs={{0,1},{1,0},{2,3},{3,2},{4,5},{5,4},{6,7},{7,6},{8,9},{9,8},{10,11... | collective-permute-start | bytes 73736 | tf_op jit(solution)/shard_map/ppermute | solution.py:189
  29.3 7.3 %collective-permute-start.8 = (f32[48,128]{1,0:T(8,128)S(1)}, f32[48,128]{1,0:T(8,128)S(1)}, u32[]{:S(2)}, u32[]{:S(2)}) collective-permute-start(f32[48,128]{1,0:T(8,128)S(1)} %add.15), channel_id=1, source_target_pairs={{0,8},{1,9},{2,10},{3,11},{4,12},{5,13},{6,14},{7,15},{8,0},{9,1},... | collective-permute-start | bytes 73736 | tf_op jit(solution)/shard_map/ppermute | solution.py:189
  36.7 7.2 %collective-permute-start.11 = (f32[48,128]{1,0:T(8,128)S(1)}, f32[48,128]{1,0:T(8,128)S(1)}, u32[]{:S(2)}, u32[]{:S(2)}) collective-permute-start(f32[48,128]{1,0:T(8,128)S(1)} %add.16), channel_id=1, source_target_pairs={{0,6},{1,7},{2,4},{3,5},{4,2},{5,3},{6,0},{7,1},{8,14},{9,15},{10,... | collective-permute-start | bytes 73736 | tf_op jit(solution)/shard_map/ppermute | solution.py:189
  37.4 6.4 %collective-permute-start.10 = (f32[48,128]{1,0:T(8,128)S(1)}, f32[48,128]{1,0:T(8,128)S(1)}, u32[]{:S(2)}, u32[]{:S(2)}) collective-permute-start(f32[48,128]{1,0:T(8,128)S(1)} %add.16), channel_id=1, source_target_pairs={{0,4},{1,5},{2,6},{3,7},{4,0},{5,1},{6,2},{7,3},{8,12},{9,13},{10,... | collective-permute-start | bytes 73736 | tf_op jit(solution)/shard_map/ppermute | solution.py:189
  39.7 4.1 %collective-permute-start.9 = (f32[48,128]{1,0:T(8,128)S(1)}, f32[48,128]{1,0:T(8,128)S(1)}, u32[]{:S(2)}, u32[]{:S(2)}) collective-permute-start(f32[48,128]{1,0:T(8,128)S(1)} %add.16), channel_id=1, source_target_pairs={{0,2},{1,3},{2,0},{3,1},{4,6},{5,7},{6,4},{7,5},{8,10},{9,11},{10,... | collective-permute-start | bytes 73736 | tf_op jit(solution)/shard_map/ppermute | solution.py:189
